TPU v7x, 256 devices: a whole 4x4x8 slice. The times are simulated.
256 devices in a mesh: view: 64 (over y, x, z_hi, core), bin: 4 (over z_lo).
Axes of the slice: x: 4, y: 4, z: 8 (z_hi: 2, z_lo: 4; z = z_hi * 4 + z_lo), core: 2. Of those that a mesh axis runs over, the one named last changes fastest.
Arguments:
- volume: bfloat16 [64, 3, 16, 256], P('view'), may hold values from -6 to 6
- basis: bfloat16 [16, 256, 128], replicated, may hold values from -0.046875 to 0.046875
- tile_index: int32 [256, 12, 56], P('view'), may hold values from 0 to 63, as said below
- tile_offset: int32 [256, 12, 56], P('view'), may hold values from 0 to 15
- attenuation: float32 [8, 3], P('bin'), may hold values from 0.1 to 0.6
- flux: float32 [8], P('bin'), may hold values from 4 to 40
- counts: int32 [256, 8, 16, 1536], P('view', 'bin'), may hold values from 0 to 63
Outputs:
- gradient: float32 [64, 3, 16, 256], P('view')
Inputs may be any that keep to these rules, and one draw needn't show every extreme that they name: `tile_index`: each view's detector tile lists 56 different volume tiles.
All inputs are finite; a program needn't handle non-finite values.
Results may differ from a plain program's by a relative error of at most 0.00058.
Values may be sent and summed in bfloat16 or wider, within the bound.
No kernel may reach another device: no remote copies, remote signals or barrier semaphores. Data moves between devices by JAX's collectives and lax.ppermute only.
A program may use at most 64 MiB of HBM per device.

v0:
```python
import math

import jax
import jax.numpy as jnp
from jax import lax
from jax.sharding import PartitionSpec as P


def selector(indices, count):
    labels = lax.broadcasted_iota(jnp.int32, (indices.shape[0], count), 1)
    return indices[:, None] == labels


def on_device(volume, basis, tile_index, tile_offset, attenuation, flux, counts):
    whole = lax.all_gather(volume, "view", axis=0, tiled=True)
    tiles_all, materials, slices, width = whole.shape
    channels = materials * slices
    flat_rows = whole.reshape(tiles_all, channels * width)
    views, det_tiles, band = tile_index.shape
    bank = basis.shape[0]
    depth = basis.shape[2]
    bank_rows = basis.reshape(bank, width * depth)
    bins_axis = lax.axis_size("bin")
    position = lax.axis_index("bin")
    own_tiles = det_tiles // bins_axis
    own_cols = own_tiles * depth
    scale = 1.0 / (8.0 * math.sqrt(views * lax.axis_size("view")))

    def select_blocks(offsets):
        pick_bank = selector(offsets, bank).astype(jnp.bfloat16)
        blocks = jnp.dot(pick_bank, bank_rows, preferred_element_type=jnp.float32)
        return blocks.astype(jnp.bfloat16).reshape(band, width, depth)

    def forward(inputs):
        indices, offsets = inputs
        pick_tiles = selector(indices, tiles_all).astype(jnp.bfloat16)
        tiles = jnp.dot(pick_tiles, flat_rows, preferred_element_type=jnp.float32)
        tiles = tiles.astype(jnp.bfloat16).reshape(band, channels, width)
        blocks = select_blocks(offsets)
        return jnp.einsum("kcs,kst->ct", tiles, blocks, preferred_element_type=jnp.float32)

    mine_index = lax.dynamic_slice_in_dim(tile_index, position * own_tiles, own_tiles, 1)
    mine_offset = lax.dynamic_slice_in_dim(tile_offset, position * own_tiles, own_tiles, 1)
    pair_index = mine_index.reshape(views * own_tiles, band)
    pair_offset = mine_offset.reshape(views * own_tiles, band)
    projected = lax.map(forward, (pair_index, pair_offset))
    lines_own = projected.reshape(views, own_tiles, channels, depth).transpose(0, 2, 1, 3)
    lines_own = lines_own.reshape(views, channels, own_cols)
    lines = lax.all_gather(lines_own, "bin", axis=2, tiled=True)
    lines = lines.reshape(views, materials, slices, -1)
    exponent = attenuation[None, :, 0, None, None] * lines[:, None, 0]
    for material in range(1, materials):
        exponent = exponent + attenuation[None, :, material, None, None] * lines[:, None, material]
    predicted = flux[None, :, None, None] * jnp.exp(-exponent)
    misfit = counts.astype(jnp.float32) - predicted
    partial_value = jnp.sum(attenuation.T[None, :, :, None, None] * misfit[:, None], axis=2)
    summed = lax.psum_scatter(partial_value, "bin", scatter_dimension=3, tiled=True)
    rounded = summed.astype(jnp.bfloat16).reshape(views, channels, own_tiles, depth)
    rounded = rounded.transpose(0, 2, 1, 3).reshape(views * own_tiles, channels, depth)

    def backward(total, inputs):
        grads, indices, offsets = inputs
        blocks = select_blocks(offsets)
        products = jnp.einsum("ct,kst->kcs", grads, blocks, preferred_element_type=jnp.float32)
        place = selector(indices, tiles_all).astype(jnp.float32)
        total = total + jnp.dot(
            place.T,
            products.reshape(band, channels * width),
            precision=lax.Precision.HIGHEST,
            preferred_element_type=jnp.float32,
        )
        return (total, None)

    start = jnp.zeros((tiles_all, channels * width), jnp.float32)
    term, unused = lax.scan(backward, start, (rounded, pair_index, pair_offset))
    term = term.reshape(tiles_all, channels, width)
    local_tiles = volume.shape[0]
    shard = lax.psum_scatter(term, "view", scatter_dimension=0, tiled=True)
    shard = lax.psum(shard, "bin")
    return (shard * scale).reshape(local_tiles, materials, slices, width)


def solution(mesh):
    placed = (
        P("view", None, None, None),
        P(),
        P("view", None, None),
        P("view", None, None),
        P("bin", None),
        P("bin"),
        P("view", "bin", None, None),
    )
    return jax.shard_map(
        on_device,
        mesh=mesh,
        in_specs=placed,
        out_specs=P("view", None, None, None),
        check_vma=False,
    )
```

profile of v0, /device:TPU:2, one launch (start us, length us, event | category | flops | bytes accessed | tf_op | source)
XLA Modules:
  0.0 556.4 jit_solution(9157774512296886976)
XLA Ops:
  8.1 2.9 copy.39
  10.9 81.7 %all-gather.3.cloned.1.call-done = bf16[64,3,16,256]{3,2,1,0:T(8,128)(2,1)} async-done(((bf16[1,3,16,256]{3,2,1,0:T(8,128)(2,1)}), bf16[64,3,16,256]{3,2,1,0:T(8,128)(2,1)}) %all-gather.3.cloned.1.call-update) | async-done | bytes 1572880 | tf_op jit(solution)/shard_map/all_gather | solution.py:15
  94.7 60.5 %while.21 = (s32[]{:T(128)}, f32[12,48,128]{2,1,0:T(8,128)S(1)}, s32[12,56]{1,0:T(8,128)S(1)}, bf16[64,12288]{1,0:T(8,128)(2,1)S(1)}, s32[12,56]{1,0:T(8,128)S(1)}, /*index=5*/bf16[16,32768]{1,0:T(8,128)(2,1)}, s32[]{:T(128)}) while((s32[]{:T(128)}, f32[12,48,128]{2,1,0:T(8,128)S(1)}, s32[12,56]{1,0:T(8,128)S(1)}, ...), condition=%wide.region_1.2_spmd, body=%wide.region_0.1_spmd.sunk | while | flops 325489024 | bytes 22832532 | solution.py:46
  109.8 2.4 fusion.41
  124.9 2.4 fusion.41
  156.6 30.4 %all-gather.5.cloned.1.call-done = f32[4,48,1536]{2,1,0:T(8,128)} async-done(((f32[4,48,384]{2,1,0:T(8,128)}), f32[4,48,1536]{2,1,0:T(8,128)}) %all-gather.5.cloned.1.call-update) | async-done | bytes 1179664 | tf_op jit(solution)/shard_map/all_gather | solution.py:49
  190.2 33.5 %reduce-scatter.3.cloned.1.call-done = f32[4,3,16,384]{3,2,1,0:T(8,128)} async-done(((f32[4,3,16,1536]{3,2,1,0:T(8,128)}), f32[4,3,16,384]{3,2,1,0:T(8,128)}) %reduce-scatter.3.cloned.1.call-update) | async-done | bytes 294928 | tf_op jit(solution)/shard_map/reduce_scatter | solution.py:57
  224.8 137.9 %while.22 = (s32[]{:T(128)}, f32[64,12288]{1,0:T(8,128)}, s32[12,56]{1,0:T(8,128)S(1)}, s32[12,56]{1,0:T(8,128)S(1)}, bf16[16,32768]{1,0:T(8,128)(2,1)}, /*index...) while((s32[]{:T(128)}, f32[64,12288]{1,0:T(8,128)}, s32[12,56]{1,0:T(8,128)S(1)}, ...), condition=%wide.region_5.6_spmd.clone, body=%wide.region_4.5_spmd.clone.sunk | while | flops 766775680 | bytes 33043876 | solution.py:75
  231.1 3.4 convolution_add_fusion.2
  234.6 2.4 fusion.48
  240.9 5.3 convolution_add_fusion.2
  252.6 5.3 convolution_add_fusion.2
  264.2 5.3 convolution_add_fusion.2
  275.9 5.3 convolution_add_fusion.2
  287.5 5.3 convolution_add_fusion.2
  299.1 5.3 convolution_add_fusion.2
  310.8 5.3 convolution_add_fusion.2
  322.4 5.3 convolution_add_fusion.2
  334.1 5.3 convolution_add_fusion.2
  345.7 5.3 convolution_add_fusion.2
  357.4 5.3 convolution_add_fusion.2
  362.7 4.5 copy.36
  367.2 164.6 %reduce-scatter.5.cloned.1.call-done = f32[1,48,256]{2,1,0:T(8,128)} async-done(((f32[64,48,256]{2,1,0:T(8,128)}), f32[1,48,256]{2,1,0:T(8,128)}) %reduce-scatter.5.cloned.1.call-update) | async-done | bytes 49168 | tf_op jit(solution)/shard_map/reduce_scatter | solution.py:78
  531.9 17.4 %psum.7 = f32[1,48,256]{2,1,0:T(8,128)S(1)} all-reduce(f32[1,48,256]{2,1,0:T(8,128)} %reduce-scatter.5.cloned.1.call-done), channel_id=1, replica_groups=mesh['view'=64,'bin'=4] {'bin'}, use_global_device_ids=true, to_apply=%region_7.8 | all-reduce | flops 12288 | bytes 98304 | tf_op jit(solution)/shard_map/psum | solution.py:79
  (162 shorter events, 138.0 us)
Async XLA Ops:
  6.5 86.1 %all-gather.3.cloned.1.call-start = ((), (), s32[]{:S(2)}) async-start(), calls=%async_computation.2 | async-start | bytes 1597440 | tf_op jit(solution)/shard_map/all_gather | solution.py:15
  7.3 179.7 %all-gather.5.cloned.1.call-start = ((), (), s32[]{:S(2)}) async-start(), calls=%async_computation.3 | async-start | bytes 1474560 | tf_op jit(solution)/shard_map/all_gather | solution.py:49
  94.7 61.6 %copy-start.1 = (f32[2,3]{1,0:T(2,128)S(1)}, f32[2,3]{1,0:T(2,128)}, u32[]{:S(2)}) copy-start(f32[2,3]{1,0:T(2,128)} %param.15) | copy-start | bytes 76
  155.1 33.2 %copy-start = (s32[4,2,16,1536]{3,2,1,0:T(8,128)S(1)}, s32[4,2,16,1536]{3,2,1,0:T(8,128)}, u32[]{:S(2)}) copy-start(s32[4,2,16,1536]{3,2,1,0:T(8,128)} %param.17) | copy-start | bytes 2359300
  155.2 33.2 %copy-start.2 = (f32[2]{0:T(128)S(1)}, f32[2]{0:T(128)}, u32[]{:S(2)}) copy-start(f32[2]{0:T(128)} %param.16) | copy-start | bytes 28
  156.2 67.5 %reduce-scatter.3.cloned.1.call-start = ((), (), s32[]{:S(2)}) async-start(), calls=%async_computation.4 | async-start | bytes 1474560 | tf_op jit(solution)/shard_map/reduce_scatter | solution.py:57
  190.0 341.9 %reduce-scatter.5.cloned.1.call-start = ((), (), s32[]{:S(2)}) async-start(), calls=%async_computation.5 | async-start | bytes 3194880 | tf_op jit(solution)/shard_map/reduce_scatter | solution.py:78
Sparse Core Ops, SparseCore 0:
  10.8 81.7 all-gather.2
  156.4 30.5 all-gather.4
  190.1 33.5 reduce-scatter.2
  367.4 164.4 reduce-scatter.4
where the time goes:
time: 558 us; the launch traced here: 556 us
  waiting for transfers between devices  311 us (56%)
  matrix products  152 us (27%)
  local copies, waits for them, and re-layouts  58.6 us (11%)
  blocking collectives  17.4 us (3%)
  between operations  13.3 us (2%)
    reduce_scatter x1, waiting for transfers between devices, on_device(): shard = lax.psum_scatter(term, 'view', scatter_dimension=0, tiled=True)  165 us
    all_gather x1, waiting for transfers between devices, on_device(): whole = lax.all_gather(volume, 'view', axis=0, tiled=True)  81.7 us
    dot_general x12, matrix products, backward(): jnp.dot(place.T, products.reshape(band, channels * width), precision=lax....  62 us
    dot_general x24, matrix products, select_blocks(): blocks = jnp.dot(pick_bank, bank_rows, preferred_element_type=jnp.float32)  56.8 us
    while x48, local copies, waits for them, and re-layouts  45.6 us
    reduce_scatter x1, waiting for transfers between devices, on_device(): lax.psum_scatter(partial_value, 'bin', scatter_dimension=3, tiled=True)  33.5 us
    all_gather x1, waiting for transfers between devices, on_device(): lines = lax.all_gather(lines_own, 'bin', axis=2, tiled=True)  30.4 us
    psum x1, blocking collectives, on_device(): shard = lax.psum(shard, 'bin')  17.4 us
  transfers between devices with their start and end apart: 4, of which 4 were waited for; matrix products, arithmetic and copies ran while one was open for 1% of the time, Pallas kernels for 0%

commit v1 on v0

v1 whole, which is shorter than its diff:
```python
import math

import jax
import jax.numpy as jnp
from jax import lax
from jax.experimental import pallas as pl
from jax.experimental.pallas import tpu as pltpu
from jax.sharding import PartitionSpec as P

BOTH = ("view", "bin")
BF16 = jnp.bfloat16
F32 = jnp.float32

CORE = 4
FAR = 8 + 2
PLANE = 15
LINE = 11

HALF = 32
SPOTS = 16
QUARTERS = 4
CHANNELS = 12
PAIRS = 48
BANK = 16
WIDTH = 256
DEPTH = 128
SPAN = QUARTERS * DEPTH
BLOCK = 2 * CHANNELS


def partners(mask):
    return [(place, place ^ mask) for place in range(256)]


def groups_of(same):
    return [[place for place in range(256) if place & same == rest] for rest in range(256) if rest & same == rest]


def split(value):
    high = value.astype(BF16)
    low = (value - high.astype(F32)).astype(BF16)
    return high, low


def select_kernel(index_ref, offset_ref, picks_ref, places_ref):
    labels = lax.broadcasted_iota(jnp.int32, (2 * HALF, 128), 0)
    chosen = jnp.full((2 * HALF, 128), -1, jnp.int32)
    for step in range(index_ref.shape[0]):
        chosen = jnp.where(labels == index_ref[step : step + 1, :], offset_ref[step : step + 1, :], chosen)
    chosen = chosen.astype(F32)
    part = (lax.broadcasted_iota(jnp.int32, (PAIRS, 128), 1) // HALF).astype(F32)
    for core in range(2):
        mine = chosen[core * HALF : (core + 1) * HALF]
        turned = jnp.concatenate([mine] * 4, axis=0).T[:PAIRS] - part
        for j in range(BANK // 4):
            picks_ref[core, :, j * 128 : (j + 1) * 128] = (turned == 4 * j).astype(F32).astype(BF16)
        for p in range(BANK):
            places_ref[core, p * HALF : (p + 1) * HALF, :] = (mine == p).astype(F32).astype(BF16)


def select(index, offset):
    vmem = pl.BlockSpec(memory_space=pltpu.VMEM)
    return pl.pallas_call(
        select_kernel,
        out_shape=[
            jax.ShapeDtypeStruct((2, PAIRS, BANK * HALF), BF16),
            jax.ShapeDtypeStruct((2, BANK * HALF, 128), BF16),
        ],
        in_specs=[vmem] * 2,
        out_specs=[vmem] * 2,
    )(index, offset)


def project(core, volume_ref, basis_ref, picks_ref, rows_ref, high_ref, low_ref):
    rows_ref[...] = volume_ref[...].astype(F32)
    volume = [rows_ref[:, far * CHANNELS + c, :].astype(BF16) for c in range(CHANNELS) for far in range(2)]
    volume = jnp.concatenate(volume, axis=0)
    for j in range(BANK // 2):
        both = jnp.concatenate([basis_ref[2 * j], basis_ref[2 * j + 1]], axis=1)
        table = jnp.dot(volume, both, preferred_element_type=F32)
        high, low = split(table)
        for p in range(2):
            row = (2 * j + p) * HALF
            for c in range(CHANNELS):
                piece = (slice(c * HALF, (c + 1) * HALF), slice(p * DEPTH, (p + 1) * DEPTH))
                high_ref[row : row + HALF, c * DEPTH : (c + 1) * DEPTH] = high[piece]
                low_ref[row : row + HALF, c * DEPTH : (c + 1) * DEPTH] = low[piece]
    picks = picks_ref[core]
    return jnp.dot(picks, high_ref[...], preferred_element_type=F32) + jnp.dot(
        picks, low_ref[...], preferred_element_type=F32
    )


def back_project(core, rounded, basis_ref, places_ref, grad_ref, high_ref, low_ref):
    for j in range(BANK // 4):
        places = places_ref[core, j * 128 : (j + 1) * 128, :][:, :PAIRS]
        summed = jnp.dot(places, rounded, preferred_element_type=F32)
        high, low = split(summed)
        for p in range(4):
            col = (4 * j + p) * DEPTH
            for c in range(CHANNELS):
                piece = (slice(p * HALF, (p + 1) * HALF), slice(c * DEPTH, (c + 1) * DEPTH))
                high_ref[c * HALF : (c + 1) * HALF, col : col + DEPTH] = high[piece]
                low_ref[c * HALF : (c + 1) * HALF, col : col + DEPTH] = low[piece]
    bank = jnp.concatenate([basis_ref[p] for p in range(BANK)], axis=1)
    turned = (((1,), (1,)), ((), ()))
    total = lax.dot_general(high_ref[...], bank, turned, preferred_element_type=F32) + lax.dot_general(
        low_ref[...], bank, turned, preferred_element_type=F32
    )
    for c in range(CHANNELS):
        for far in range(2):
            row = c * HALF + far * SPOTS
            grad_ref[:, far * CHANNELS + c, :] = total[row : row + SPOTS]


def first_kernel(volume_ref, basis_ref, picks_ref, lines_ref, rows_ref, high_ref, low_ref):
    lines_ref[...] = project(0, volume_ref, basis_ref, picks_ref, rows_ref, high_ref, low_ref)


def second_kernel(
    volume_ref,
    basis_ref,
    picks_ref,
    places_ref,
    lines_ref,
    message0_ref,
    message1_ref,
    message2_ref,
    message3_ref,
    rounded_ref,
    grad_ref,
    rows_ref,
    high_ref,
    low_ref,
    zhigh_ref,
    zlow_ref,
):
    lines = lines_ref[...] + project(1, volume_ref, basis_ref, picks_ref, rows_ref, high_ref, low_ref)
    line = [lines[:, m * SPAN : (m + 1) * SPAN] for m in range(3)]
    grads = [jnp.zeros((PAIRS, SPAN), F32) for m in range(3)]
    for message_ref in (message0_ref, message1_ref, message2_ref, message3_ref):
        figures = message_ref[2 * PAIRS : 2 * PAIRS + 16, :].astype(F32)
        figures = (figures[:, :128] + figures[:, 128:256]) + figures[:, 256:384]
        figures = jnp.concatenate([figures] * QUARTERS, axis=1)
        for b in range(2):
            weight = [figures[4 * b + m : 4 * b + m + 1, :] for m in range(4)]
            exponent = weight[0] * line[0] + weight[1] * line[1] + weight[2] * line[2]
            photons = message_ref[b * PAIRS : (b + 1) * PAIRS, :].astype(F32)
            misfit = photons - weight[3] * jnp.exp(-exponent)
            grads = [grads[m] + weight[m] * misfit for m in range(3)]
    rounded = jnp.concatenate([g.astype(BF16) for g in grads], axis=1)
    rounded_ref[...] = rounded
    back_project(1, rounded, basis_ref, places_ref, grad_ref, zhigh_ref, zlow_ref)


def third_kernel(rounded_ref, basis_ref, places_ref, grad_ref, zhigh_ref, zlow_ref):
    back_project(0, rounded_ref[...], basis_ref, places_ref, grad_ref, zhigh_ref, zlow_ref)


def call(kernel, out_shape, forward, backward, *operands):
    vmem = pl.BlockSpec(memory_space=pltpu.VMEM)
    scratch = []
    if forward:
        scratch += [pltpu.VMEM((SPOTS, BLOCK, WIDTH), F32)]
        scratch += [pltpu.VMEM((BANK * HALF, CHANNELS * DEPTH), BF16)] * 2
    if backward:
        scratch += [pltpu.VMEM((CHANNELS * HALF, BANK * DEPTH), BF16)] * 2
    return pl.pallas_call(
        kernel,
        out_shape=out_shape,
        in_specs=[vmem] * len(operands),
        out_specs=[vmem] * len(out_shape),
        scratch_shapes=scratch,
        compiler_params=pltpu.CompilerParams(vmem_limit_bytes=40 * 2**20),
    )(*operands)


def on_device(volume, basis, tile_index, tile_offset, attenuation, flux, counts):
    view = lax.axis_index("view")
    far = (view >> 1) & 1
    quarter = lax.axis_index("bin") ^ (2 * far)
    views, det_tiles, band = tile_index.shape
    slices = volume.shape[2]
    own_slices = slices // QUARTERS
    plane_groups = groups_of(PLANE)
    line_groups = groups_of(255 ^ LINE)

    mine = lax.dynamic_slice_in_dim(volume[0], quarter * own_slices, own_slices, 1).reshape(CHANNELS, WIDTH)
    theirs = lax.ppermute(mine, BOTH, partners(FAR))
    stack = jnp.concatenate([mine, theirs], axis=0)

    figures = jnp.concatenate([attenuation, flux[:, None]], axis=1).reshape(8)
    first = lax.reduce_precision(figures, 8, 7)
    rest = figures - first
    second = lax.reduce_precision(rest, 8, 7)
    third = rest - second
    figures = jnp.stack([first, second, third, jnp.zeros_like(third)], axis=1).astype(BF16)
    figures = jnp.broadcast_to(figures[:, :, None], (8, QUARTERS, DEPTH)).reshape(8, SPAN)
    figures = jnp.pad(figures, ((0, 8), (0, 0)))
    photons = counts.astype(BF16).reshape(views, 2, QUARTERS, own_slices, det_tiles, DEPTH)
    photons = photons.transpose(2, 1, 0, 4, 3, 5).reshape(QUARTERS, 2 * PAIRS, SPAN)
    messages = jnp.concatenate([photons, jnp.broadcast_to(figures[None], (QUARTERS, 16, SPAN))], axis=1)
    payloads = [lax.dynamic_index_in_dim(messages, quarter ^ shift, 0, keepdims=False) for shift in range(QUARTERS)]
    stack, payloads = lax.optimization_barrier((stack, payloads))

    stack = jnp.broadcast_to(stack[None], (SPOTS, BLOCK, WIDTH))
    own = lax.all_to_all(stack, BOTH, 0, 0, tiled=True, axis_index_groups=plane_groups)
    arrived = payloads[:1] + [lax.ppermute(payloads[shift], BOTH, partners(shift)) for shift in range(1, QUARTERS)]

    index = tile_index.reshape(PAIRS, band) ^ (view & 3)
    index = (index & 1) * HALF + ((index >> 1) & 1) * SPOTS + (index >> 2)
    index = jnp.pad(index.T, ((0, 0), (0, 128 - PAIRS)))
    offset = jnp.pad(tile_offset.reshape(PAIRS, band).T, ((0, 0), (0, 128 - PAIRS)))
    picks, places = select(index, offset)

    other = lax.ppermute(own, BOTH, partners(CORE))
    lines_shape = jax.ShapeDtypeStruct((PAIRS, CHANNELS * DEPTH), F32)
    rounded_shape = jax.ShapeDtypeStruct((PAIRS, CHANNELS * DEPTH), BF16)
    grad_shape = jax.ShapeDtypeStruct((SPOTS, BLOCK, WIDTH), F32)
    (lines,) = call(first_kernel, [lines_shape], True, False, own, basis, picks)
    rounded, send = call(
        second_kernel, [rounded_shape, grad_shape], True, True, other, basis, picks, places, lines, *arrived
    )
    received = lax.ppermute(send, BOTH, partners(CORE))
    (keep,) = call(third_kernel, [grad_shape], False, True, rounded, basis, places)

    parts = lax.all_to_all(keep + received, BOTH, 0, 0, tiled=True, axis_index_groups=plane_groups)
    total = jnp.sum(parts, axis=0)
    scale = 1.0 / (8.0 * math.sqrt(views * lax.axis_size("view")))
    total = (total * scale).reshape(2, CHANNELS, WIDTH)
    blocks = jnp.where(far == 0, total, total[::-1])
    blocks = jnp.broadcast_to(blocks[:, None], (2, QUARTERS, CHANNELS, WIDTH)).reshape(2 * QUARTERS, CHANNELS, WIDTH)
    blocks = lax.all_to_all(blocks, BOTH, 0, 0, tiled=True, axis_index_groups=line_groups)
    quarters = blocks[:4] + jnp.concatenate([blocks[6:], blocks[4:6]], axis=0)
    quarters = quarters.reshape(QUARTERS, 3, own_slices, WIDTH).transpose(1, 0, 2, 3)
    return quarters.reshape(1, 3, slices, WIDTH)


def solution(mesh):
    placed = (
        P("view", None, None, None),
        P(),
        P("view", None, None),
        P("view", None, None),
        P("bin", None),
        P("bin"),
        P("view", "bin", None, None),
    )
    return jax.shard_map(
        on_device,
        mesh=mesh,
        in_specs=placed,
        out_specs=P("view", None, None, None),
        check_vma=False,
    )
```

time: 558 us -> 68.2 us (0.12)
  waiting for transfers between devices: 311 us -> 12 us
  matrix products: 152 us -> 0 us
  local copies, waits for them, and re-layouts: 58.6 us -> 6.76 us
  starting transfers between devices: 0.31 us -> 24.7 us
  between operations: 13.3 us -> 0.25 us
  Pallas kernels: 0 us -> 8.76 us
    reduce_scatter x2 -> x0, waiting for transfers between devices: 198 us -> none  [the longest x1 165 us: on_device(): shard = lax.psum_scatter(term, 'view', scatter_dimension=0, tiled=True)]
    dot_general x72 -> x0, matrix products: 152 us -> none  [the longest x12 62 us: backward(): jnp.dot(place.T, products.reshape(band, channels * width), precision=lax....]
    all_gather x2 -> x0, waiting for transfers between devices: 112 us -> none  [the longest x1 81.7 us: on_device(): whole = lax.all_gather(volume, 'view', axis=0, tiled=True)]
    while x48 -> x0, local copies, waits for them, and re-layouts: 45.6 us -> none
    psum x1 -> x0, blocking collectives: 17.4 us -> none  [on_device(): shard = lax.psum(shard, 'bin')]
    all_to_all x0 -> x2, starting transfers between devices: none -> 13.3 us  [the longest x1 7.61 us: on_device(): lax.all_to_all(stack, BOTH, 0, 0, tiled=True, axis_index_groups=plane_gro...]
    all_to_all x0 -> x1, blocking collectives: none -> 12.8 us  [on_device(): lax.all_to_all(blocks, BOTH, 0, 0, tiled=True, axis_index_groups=line_gro...]
    all_to_all x0 -> x2, waiting for transfers between devices: none -> 12 us  [the longest x1 9.37 us: on_device(): lax.all_to_all(keep + received, BOTH, 0, 0, tiled=True, axis_index_groups...]
  transfers between devices with their start and end apart: 4 -> 8, of which waited for: 4 -> 2; matrix products, arithmetic and copies ran while one was open for 1% -> 6% of each run, Pallas kernels for 0% -> 7%
where the time goes in v1:
time: 68.2 us; the launch traced here: 67.6 us
  starting transfers between devices  24.7 us (36%)
  blocking collectives  12.8 us (19%)
  waiting for transfers between devices  12 us (18%)
  Pallas kernels  8.76 us (13%)
  local copies, waits for them, and re-layouts  6.76 us (10%)
  other arithmetic  2.27 us (3%)
    all_to_all x1, blocking collectives, on_device(): lax.all_to_all(blocks, BOTH, 0, 0, tiled=True, axis_index_groups=line_gro...  12.8 us
    all_to_all x1, waiting for transfers between devices, on_device(): lax.all_to_all(keep + received, BOTH, 0, 0, tiled=True, axis_index_groups...  9.37 us
    all_to_all x1, starting transfers between devices, on_device(): lax.all_to_all(stack, BOTH, 0, 0, tiled=True, axis_index_groups=plane_gro...  7.61 us
    pallas_call x3, Pallas kernels, call(): pl.pallas_call(kernel, out_shape=out_shape, in_specs=[vmem] * len(operand...  7.03 us
    ppermute x1, starting transfers between devices, on_device(): theirs = lax.ppermute(mine, BOTH, partners(FAR))  6.39 us
    all_to_all x1, starting transfers between devices, on_device(): lax.all_to_all(keep + received, BOTH, 0, 0, tiled=True, axis_index_groups...  5.71 us
    ppermute x3, starting transfers between devices, on_device(): lax.ppermute(payloads[shift], BOTH, partners(shift))  4.39 us
    unnamed x17, local copies, waits for them, and re-layouts  3.01 us
  transfers between devices with their start and end apart: 8, of which 2 were waited for; matrix products, arithmetic and copies ran while one was open for 6% of the time, Pallas kernels for 7%

profile of v1, /device:TPU:2, one launch (start us, length us, event | category | flops | bytes accessed | tf_op | source)
XLA Modules:
  0.0 67.6 jit_solution(1629824905250948341)
XLA Ops:
  0.0 0.7 %copy-done = bf16[1,3,16,256]{3,2,1,0:T(8,128)(2,1)S(1)} copy-done((bf16[1,3,16,256]{3,2,1,0:T(8,128)(2,1)S(1)}, bf16[1,3,16,256]{3,2,1,0:T(8,128)(2,1)}, u32[]{:S(2)}) %copy-start) | copy-done | bytes 24600
  0.8 6.4 %collective-permute-start = (bf16[12,256]{1,0:T(8,128)(2,1)S(1)}, bf16[12,256]{1,0:T(8,128)(2,1)S(1)}, u32[]{:S(2)}, u32[]{:S(2)}) collective-permute-start(bf16[12,256]{1,0:T(8,128)(2,1)S(1)} %reshape.115), channel_id=1, source_target_pairs={{0,10},{1,11},{2,8},{3,9},{4,14},{5,15},{6,12},{7,13},{8,2},{9,3},... | collective-permute-start | bytes 18440 | tf_op jit(solution)/shard_map/ppermute | solution.py:189
  7.2 0.7 copy-done.7
  7.9 0.6 copy-done.6
  8.9 1.2 %convert_element_type.10 = bf16[4,2,16,1536]{3,2,1,0:T(8,128)(2,1)S(1)} convert(s32[4,2,16,1536]{3,2,1,0:T(8,128)} %param.13) | non-fusion elementwise | flops 196608 | bytes 1179648 | tf_op jit(solution)/shard_map/convert_element_type | solution.py:200
  10.8 0.7 %broadcast_in_dim.13 = bf16[16,24,256]{2,1,0:T(8,128)(2,1)} broadcast(bf16[24,256]{1,0:T(8,128)(2,1)S(1)} %pad_maximum_fusion), dimensions={1,2} | broadcast | bytes 208896 | tf_op jit(solution)/shard_map/broadcast_in_dim | solution.py:206
  11.5 7.6 %all-to-all-start = ((bf16[16,24,256]{2,1,0:T(8,128)(2,1)}), bf16[16,24,256]{2,1,0:T(8,128)(2,1)S(1)}, u32[]{:S(2)}, u32[]{:S(2)}) async-start(bf16[16,24,256]{2,1,0:T(8,128)(2,1)} %broadcast_in_dim.13), calls=%async_computation | async-start | bytes 393216 | tf_op jit(solution)/shard_map/all_to_all | solution.py:207
  19.1 1.0 %collective-permute-start.2 = (bf16[112,512]{1,0:T(8,128)(2,1)S(1)}, bf16[112,512]{1,0:T(8,128)(2,1)S(1)}, u32[]{:S(2)}, u32[]{:S(2)}) collective-permute-start(bf16[112,512]{1,0:T(8,128)(2,1)S(1)} %get-tuple-element.18), channel_id=1, source_target_pairs={{0,1},{1,0},{2,3},{3,2},{4,5},{5,4},{6,7},{7,6},{8,9},{9,8},{10,11... | collective-permute-start | bytes 344072 | tf_op jit(solution)/shard_map/ppermute | solution.py:208
  20.1 1.5 %collective-permute-start.3 = (bf16[112,512]{1,0:T(8,128)(2,1)S(1)}, bf16[112,512]{1,0:T(8,128)(2,1)S(1)}, u32[]{:S(2)}, u32[]{:S(2)}) collective-permute-start(bf16[112,512]{1,0:T(8,128)(2,1)S(1)} %get-tuple-element.19), channel_id=1, source_target_pairs={{0,2},{1,3},{2,0},{3,1},{4,6},{5,7},{6,4},{7,5},{8,10},{9,11},{10,... | collective-permute-start | bytes 344072 | tf_op jit(solution)/shard_map/ppermute | solution.py:208
  21.6 1.9 %collective-permute-start.4 = (bf16[112,512]{1,0:T(8,128)(2,1)S(1)}, bf16[112,512]{1,0:T(8,128)(2,1)S(1)}, u32[]{:S(2)}, u32[]{:S(2)}) collective-permute-start(bf16[112,512]{1,0:T(8,128)(2,1)S(1)} %get-tuple-element.20), channel_id=1, source_target_pairs={{0,3},{1,2},{2,1},{3,0},{4,7},{5,6},{6,5},{7,4},{8,11},{9,10},{10,... | collective-permute-start | bytes 344072 | tf_op jit(solution)/shard_map/ppermute | solution.py:208
  23.5 2.6 %all-to-all-done.volume_ref = bf16[16,24,256]{2,1,0:T(8,128)(2,1)S(1)} async-done(((bf16[16,24,256]{2,1,0:T(8,128)(2,1)}), bf16[16,24,256]{2,1,0:T(8,128)(2,1)S(1)}, u32[]{:S(2)}, u32[]{:S(2)}) %all-to-all-start) | async-done | bytes 196640 | tf_op jit(solution)/shard_map/all_to_all | solution.py:207
  26.2 0.6 pad.12.index_ref
  27.1 0.6 pad.13.offset_ref
  27.7 1.7 %shard_map.73 = (bf16[2,48,512]{2,1,0:T(8,128)(2,1)}, bf16[2,512,128]{2,1,0:T(8,128)(2,1)}) custom-call(s32[56,128]{1,0:T(8,128)} %pad.12.index_ref, s32[56,128]{1,0:T(8,128)} %pad.13.offset_ref), custom_call_target="tpu_custom_call" | custom-call | tf_op jit(solution)/shard_map/pallas_call | solution.py:63
  29.4 0.9 %copy-done.3 = bf16[2,48,512]{2,1,0:T(8,128)(2,1)S(1)} copy-done((bf16[2,48,512]{2,1,0:T(8,128)(2,1)S(1)}, bf16[2,48,512]{2,1,0:T(8,128)(2,1)}, u32[]{:S(2)}) %copy-start.3) | copy-done | bytes 98328
  30.3 1.4 %shard_map.74.lines_ref = f32[48,1536]{1,0:T(8,128)S(1)} custom-call(bf16[16,24,256]{2,1,0:T(8,128)(2,1)S(1)} %all-to-all-done.volume_ref, bf16[16,256,128]{2,1,0:T(8,128)(2,1)S(1)} %copy-done.1, bf16[2,48,512]{2,1,0:T(8,128)(2,1)S(1)} %copy-done.3), custom_call_target="tpu_custom_call" | custom-call | tf_op jit(solution)/shard_map/pallas_call | solution.py:168
  31.8 3.9 %shard_map.75 = (bf16[48,1536]{1,0:T(8,128)(2,1)S(1)}, f32[16,24,256]{2,1,0:T(8,128)S(1)}) custom-call(bf16[16,24,256]{2,1,0:T(8,128)(2,1)S(1)} %collective-permute-done.1.volume_ref, bf16[16,256,128]{2,1,0:T(8,128)(2,1)S(1)} %copy-done.1, bf16[2,48,512]{2,1,0:T(8,128)(2,1)S(1)} %copy-done.3, bf16[2,512,128]{2,1,0:T(8,128)(2,1)S(1)} %copy-done.2, ...), custom_call_target="tpu_custom_call" | custom-call | tf_op jit(solution)/shard_map/pallas_call | solution.py:168
  35.7 0.6 collective-permute-start.5
  36.3 1.7 %shard_map.76 = f32[16,24,256]{2,1,0:T(8,128)S(1)} custom-call(bf16[48,1536]{1,0:T(8,128)(2,1)S(1)} %get-tuple-element.21.rounded_ref, bf16[16,256,128]{2,1,0:T(8,128)(2,1)S(1)} %copy-done.1, bf16[2,512,128]{2,1,0:T(8,128)(2,1)S(1)} %copy-done.2), custom_call_target="tpu_custom_call" | custom-call | tf_op jit(solution)/shard_map/pallas_call | solution.py:168
  38.0 0.8 %add.41 = f32[16,24,256]{2,1,0:T(8,128)} add(f32[16,24,256]{2,1,0:T(8,128)S(1)} %shard_map.76, f32[16,24,256]{2,1,0:T(8,128)S(1)} %collective-permute-done.5) | non-fusion elementwise | flops 98304 | bytes 1179648 | tf_op jit(solution)/shard_map/add | solution.py:227
  38.8 5.7 %all-to-all-start.1 = ((f32[16,24,256]{2,1,0:T(8,128)}), f32[16,24,256]{2,1,0:T(8,128)S(1)}, u32[]{:S(2)}, u32[]{:S(2)}) async-start(f32[16,24,256]{2,1,0:T(8,128)} %add.41), calls=%async_computation.1 | async-start | bytes 786432 | tf_op jit(solution)/shard_map/all_to_all | solution.py:227
  44.5 9.4 %all-to-all-done.1 = f32[16,24,256]{2,1,0:T(8,128)S(1)} async-done(((f32[16,24,256]{2,1,0:T(8,128)}), f32[16,24,256]{2,1,0:T(8,128)S(1)}, u32[]{:S(2)}, u32[]{:S(2)}) %all-to-all-start.1) | async-done | bytes 393248 | tf_op jit(solution)/shard_map/all_to_all | solution.py:227
  54.0 12.8 %all_to_all.15 = f32[8,12,256]{2,1,0:T(8,128)S(1)} all-to-all(f32[8,12,256]{2,1,0:T(8,128)S(1)} %bitcast.22), channel_id=1, replica_groups={{0,1,2,3,8,9,10,11},{4,5,6,7,12,13,14,15},{16,17,18,19,24,25,26,27},{20..., dimensions={0} | all-to-all | bytes 196608 | tf_op jit(solution)/shard_map/all_to_all | solution.py:233
  66.9 0.6 reshape.123
  (50 shorter events, 1.6 us)
Async XLA Ops:
  0.0 0.7 %copy-start = (bf16[1,3,16,256]{3,2,1,0:T(8,128)(2,1)S(1)}, bf16[1,3,16,256]{3,2,1,0:T(8,128)(2,1)}, u32[]{:S(2)}) copy-start(bf16[1,3,16,256]{3,2,1,0:T(8,128)(2,1)} %param.7) | copy-start | bytes 73732
  0.8 10.0 %collective-permute-start = (bf16[12,256]{1,0:T(8,128)(2,1)S(1)}, bf16[12,256]{1,0:T(8,128)(2,1)S(1)}, u32[]{:S(2)}, u32[]{:S(2)}) collective-permute-start(bf16[12,256]{1,0:T(8,128)(2,1)S(1)} %reshape.115), channel_id=1, source_target_pairs={{0,10},{1,11},{2,8},{3,9},{4,14},{5,15},{6,12},{7,13},{8,2},{9,3},... | collective-permute-start | bytes 18440 | tf_op jit(solution)/shard_map/ppermute | solution.py:189
  7.2 0.7 copy-start.7
  7.8 0.7 %copy-start.6 = (f32[2,3]{1,0:T(2,128)S(1)}, f32[2,3]{1,0:T(2,128)}, u32[]{:S(2)}) copy-start(f32[2,3]{1,0:T(2,128)} %param.11) | copy-start | bytes 76
  10.7 18.7 %copy-start.1 = (bf16[16,256,128]{2,1,0:T(8,128)(2,1)S(1)}, bf16[16,256,128]{2,1,0:T(8,128)(2,1)}, u32[]{:S(2)}) copy-start(bf16[16,256,128]{2,1,0:T(8,128)(2,1)} %basis_ref.5) | copy-start | bytes 3145732
  11.5 14.6 %copy-start.5 = (s32[4,12,56]{2,0,1:T(4,128)S(1)}, s32[4,12,56]{2,0,1:T(4,128)}, u32[]{:S(2)}) copy-start(s32[4,12,56]{2,0,1:T(4,128)} %param.9) | copy-start | bytes 32260
  11.5 14.6 %all-to-all-start = ((bf16[16,24,256]{2,1,0:T(8,128)(2,1)}), bf16[16,24,256]{2,1,0:T(8,128)(2,1)S(1)}, u32[]{:S(2)}, u32[]{:S(2)}) async-start(bf16[16,24,256]{2,1,0:T(8,128)(2,1)} %broadcast_in_dim.13), calls=%async_computation | async-start | bytes 393216 | tf_op jit(solution)/shard_map/all_to_all | solution.py:207
  19.1 12.6 %collective-permute-start.2 = (bf16[112,512]{1,0:T(8,128)(2,1)S(1)}, bf16[112,512]{1,0:T(8,128)(2,1)S(1)}, u32[]{:S(2)}, u32[]{:S(2)}) collective-permute-start(bf16[112,512]{1,0:T(8,128)(2,1)S(1)} %get-tuple-element.18), channel_id=1, source_target_pairs={{0,1},{1,0},{2,3},{3,2},{4,5},{5,4},{6,7},{7,6},{8,9},{9,8},{10,11... | collective-permute-start | bytes 344072 | tf_op jit(solution)/shard_map/ppermute | solution.py:208
  20.1 11.6 %collective-permute-start.3 = (bf16[112,512]{1,0:T(8,128)(2,1)S(1)}, bf16[112,512]{1,0:T(8,128)(2,1)S(1)}, u32[]{:S(2)}, u32[]{:S(2)}) collective-permute-start(bf16[112,512]{1,0:T(8,128)(2,1)S(1)} %get-tuple-element.19), channel_id=1, source_target_pairs={{0,2},{1,3},{2,0},{3,1},{4,6},{5,7},{6,4},{7,5},{8,10},{9,11},{10,... | collective-permute-start | bytes 344072 | tf_op jit(solution)/shard_map/ppermute | solution.py:208
  21.6 10.2 %collective-permute-start.4 = (bf16[112,512]{1,0:T(8,128)(2,1)S(1)}, bf16[112,512]{1,0:T(8,128)(2,1)S(1)}, u32[]{:S(2)}, u32[]{:S(2)}) collective-permute-start(bf16[112,512]{1,0:T(8,128)(2,1)S(1)} %get-tuple-element.20), channel_id=1, source_target_pairs={{0,3},{1,2},{2,1},{3,0},{4,7},{5,6},{6,5},{7,4},{8,11},{9,10},{10,... | collective-permute-start | bytes 344072 | tf_op jit(solution)/shard_map/ppermute | solution.py:208
  26.1 5.7 %collective-permute-start.1 = (bf16[16,24,256]{2,1,0:T(8,128)(2,1)S(1)}, bf16[16,24,256]{2,1,0:T(8,128)(2,1)S(1)}, u32[]{:S(2)}, u32[]{:S(2)}) collective-permute-start(bf16[16,24,256]{2,1,0:T(8,128)(2,1)S(1)} %all-to-all-done.volume_ref), channel_id=1, source_target_pairs={{0,4},{1,5},{2,6},{3,7},{4,0},{5,1},{6,2},{7,3},{8,12},{9,13},{10,... | collective-permute-start | bytes 589832 | tf_op jit(solution)/shard_map/ppermute | solution.py:216
  26.2 0.7 %copy-start.4 = (s32[4,12,56]{2,0,1:T(4,128)S(1)}, s32[4,12,56]{2,0,1:T(4,128)}, u32[]{:S(2)}) copy-start(s32[4,12,56]{2,0,1:T(4,128)} %param.10) | copy-start | bytes 32260
  29.4 0.9 %copy-start.3 = (bf16[2,48,512]{2,1,0:T(8,128)(2,1)S(1)}, bf16[2,48,512]{2,1,0:T(8,128)(2,1)}, u32[]{:S(2)}) copy-start(bf16[2,48,512]{2,1,0:T(8,128)(2,1)} %get-tuple-element.15.picks_ref) | copy-start | bytes 294916
  30.3 1.5 %copy-start.2 = (bf16[2,512,128]{2,1,0:T(8,128)(2,1)S(1)}, bf16[2,512,128]{2,1,0:T(8,128)(2,1)}, u32[]{:S(2)}) copy-start(bf16[2,512,128]{2,1,0:T(8,128)(2,1)} %get-tuple-element.16.places_ref) | copy-start | bytes 786436
  35.7 2.3 %collective-permute-start.5 = (f32[16,24,256]{2,1,0:T(8,128)S(1)}, f32[16,24,256]{2,1,0:T(8,128)S(1)}, u32[]{:S(2)}, u32[]{:S(2)}) collective-permute-start(f32[16,24,256]{2,1,0:T(8,128)S(1)} %get-tuple-element.22), channel_id=1, source_target_pairs={{0,4},{1,5},{2,6},{3,7},{4,0},{5,1},{6,2},{7,3},{8,12},{9,13},{10,... | collective-permute-start | bytes 1179656 | tf_op jit(solution)/shard_map/ppermute | solution.py:224
  38.8 15.1 %all-to-all-start.1 = ((f32[16,24,256]{2,1,0:T(8,128)}), f32[16,24,256]{2,1,0:T(8,128)S(1)}, u32[]{:S(2)}, u32[]{:S(2)}) async-start(f32[16,24,256]{2,1,0:T(8,128)} %add.41), calls=%async_computation.1 | async-start | bytes 786432 | tf_op jit(solution)/shard_map/all_to_all | solution.py:227

commit v2 on v0

v2 whole, which is shorter than its diff:
```python
import math

import jax
import jax.numpy as jnp
from jax import lax
from jax.experimental import pallas as pl
from jax.experimental.pallas import tpu as pltpu
from jax.sharding import PartitionSpec as P

BOTH = ("view", "bin")
BF16 = jnp.bfloat16
F32 = jnp.float32

CORE = 4
FAR = 8 + 2
PLANE = 15
LINE = 11

SPOTS = 16
HALF = 32
TILES = 64
QUARTERS = 4
CHANNELS = 6
PAIRS = 48
BANK = 16
WIDTH = 256
DEPTH = 128
SPAN = 2 * DEPTH
BLOCK = 2 * CHANNELS


def partners(mask):
    return [(place, place ^ mask) for place in range(256)]


def groups_of(same):
    return [[place for place in range(256) if place & same == rest] for rest in range(256) if rest & same == rest]


def split(value):
    high = value.astype(BF16)
    low = (value - high.astype(F32)).astype(BF16)
    return high, low


def select(code_ref, square_ref):
    square_ref[...] = jnp.zeros((128, 128), F32)
    square_ref[: 2 * PAIRS, : code_ref.shape[1]] = code_ref[...].astype(F32)
    code = square_ref[...].T.astype(jnp.int32)
    labels = lax.broadcasted_iota(jnp.int32, (TILES, 128), 0)
    chosen = jnp.full((TILES, 128), -1, jnp.int32)
    for step in range(code_ref.shape[1]):
        row = code[step : step + 1, :]
        chosen = jnp.where(labels == (row & (TILES - 1)), row >> 6, chosen)
    return chosen.astype(F32)


def message_kernel(counts_ref, attenuation_ref, flux_ref, message0_ref, message1_ref, message2_ref, message3_ref, rows_ref):
    view = lax.axis_index("view")
    quarter = lax.axis_index("bin") ^ (2 * ((view >> 1) & 1))
    for v in range(4):
        for b in range(2):
            for s in range(0, 16, 8):
                piece = counts_ref[v, b, s : s + 8, :].astype(F32)
                piece = jnp.stack([piece[:, d * DEPTH : (d + 1) * DEPTH] for d in range(12)])
                row = b * PAIRS + v * 12
                rows_ref[s : s + 8, row : row + 12, :] = jnp.swapaxes(piece, 0, 1)
    refs = (message0_ref, message1_ref, message2_ref, message3_ref)
    for shift, ref in enumerate(refs):
        for s in range(4):
            piece = rows_ref[(quarter ^ shift) * 4 + s].astype(BF16)
            ref[: 2 * PAIRS, s * DEPTH : (s + 1) * DEPTH] = piece
    labels = lax.broadcasted_iota(jnp.int32, (8, DEPTH), 0)
    value = jnp.zeros((8, DEPTH), F32)
    for b in range(2):
        for m in range(4):
            figure = attenuation_ref[b, m] if m < 3 else flux_ref[b]
            value = jnp.where(labels == 4 * b + m, figure, value)
    first = value.astype(BF16)
    rest = value - first.astype(F32)
    second = rest.astype(BF16)
    third = (rest - second.astype(F32)).astype(BF16)
    upper = jnp.concatenate([first.astype(F32), second.astype(F32)], axis=1)
    lower = jnp.concatenate([third.astype(F32), jnp.zeros((8, DEPTH), F32)], axis=1)
    figures = jnp.concatenate([upper, lower], axis=0).astype(BF16)
    figures = jnp.concatenate([figures, figures], axis=1)
    for ref in refs:
        ref[2 * PAIRS :, :] = figures


def local_kernel(
    code_ref,
    volume_ref,
    basis_ref,
    mine_ref,
    theirs_ref,
    grad_ref,
    square_ref,
    rows_ref,
    high_ref,
    low_ref,
    zhigh_ref,
    zlow_ref,
):
    rows_ref[...] = volume_ref[...].astype(F32)
    volume = [rows_ref[:, near * CHANNELS + c, :].astype(BF16) for c in range(CHANNELS) for near in range(4)]
    volume = jnp.concatenate(volume, axis=0)
    for j in range(BANK // 2):
        both = jnp.concatenate([basis_ref[2 * j], basis_ref[2 * j + 1]], axis=1)
        table = jnp.dot(volume, both, preferred_element_type=F32)
        high, low = split(table)
        for p in range(2):
            row = (2 * j + p) * TILES
            for c in range(CHANNELS):
                piece = (slice(c * TILES, (c + 1) * TILES), slice(p * DEPTH, (p + 1) * DEPTH))
                high_ref[row : row + TILES, c * DEPTH : (c + 1) * DEPTH] = high[piece]
                low_ref[row : row + TILES, c * DEPTH : (c + 1) * DEPTH] = low[piece]
    chosen = select(code_ref, square_ref)
    part = (lax.broadcasted_iota(jnp.int32, (2 * PAIRS, 128), 1) // TILES).astype(F32)
    turned = jnp.concatenate([chosen, chosen], axis=0).T[: 2 * PAIRS] - part
    picks = jnp.concatenate([(turned == 2 * j).astype(F32).astype(BF16) for j in range(BANK // 2)], axis=1)
    lines = jnp.dot(picks, high_ref[...], preferred_element_type=F32) + jnp.dot(
        picks, low_ref[...], preferred_element_type=F32
    )

    line = [lines[:, m * SPAN : (m + 1) * SPAN] for m in range(3)]
    grads = [jnp.zeros((2 * PAIRS, SPAN), F32) for m in range(3)]
    for source in range(QUARTERS):
        figures = mine_ref[source, 2 * PAIRS :, :].astype(F32)
        figures = (figures[:8, :DEPTH] + figures[:8, DEPTH:]) + figures[8:, :DEPTH]
        figures = jnp.concatenate([figures] * 2, axis=1)
        for b in range(2):
            weight = [figures[4 * b + m : 4 * b + m + 1, :] for m in range(4)]
            exponent = weight[0] * line[0] + weight[1] * line[1] + weight[2] * line[2]
            photons = [ref[source, b * PAIRS : (b + 1) * PAIRS, :] for ref in (mine_ref, theirs_ref)]
            photons = jnp.concatenate(photons, axis=0).astype(F32)
            misfit = photons - weight[3] * jnp.exp(-exponent)
            grads = [grads[m] + weight[m] * misfit for m in range(3)]
    rounded = jnp.concatenate([g.astype(BF16) for g in grads], axis=1)

    chosen = chosen[:, : 2 * PAIRS]
    for j in range(BANK // 2):
        places = [(chosen == 2 * j + p).astype(F32).astype(BF16) for p in range(2)]
        summed = jnp.dot(jnp.concatenate(places, axis=0), rounded, preferred_element_type=F32)
        high, low = split(summed)
        for p in range(2):
            col = (2 * j + p) * DEPTH
            for c in range(CHANNELS):
                piece = (slice(p * TILES, (p + 1) * TILES), slice(c * DEPTH, (c + 1) * DEPTH))
                zhigh_ref[c * TILES : (c + 1) * TILES, col : col + DEPTH] = high[piece]
                zlow_ref[c * TILES : (c + 1) * TILES, col : col + DEPTH] = low[piece]
    bank = jnp.concatenate([basis_ref[p] for p in range(BANK)], axis=1)
    turn = (((1,), (1,)), ((), ()))
    total = lax.dot_general(zhigh_ref[...], bank, turn, preferred_element_type=F32) + lax.dot_general(
        zlow_ref[...], bank, turn, preferred_element_type=F32
    )
    for c in range(CHANNELS):
        for near in range(4):
            row = c * TILES + near * SPOTS
            grad_ref[:, near * CHANNELS + c, :] = total[row : row + SPOTS]


def local(*operands):
    vmem = pl.BlockSpec(memory_space=pltpu.VMEM)
    return pl.pallas_call(
        local_kernel,
        out_shape=jax.ShapeDtypeStruct((SPOTS, 2 * BLOCK, WIDTH), F32),
        in_specs=[vmem] * len(operands),
        out_specs=vmem,
        scratch_shapes=[
            pltpu.VMEM((128, 128), F32),
            pltpu.VMEM((SPOTS, 2 * BLOCK, WIDTH), F32),
            pltpu.VMEM((BANK * TILES, CHANNELS * DEPTH), BF16),
            pltpu.VMEM((BANK * TILES, CHANNELS * DEPTH), BF16),
            pltpu.VMEM((CHANNELS * TILES, BANK * DEPTH), BF16),
            pltpu.VMEM((CHANNELS * TILES, BANK * DEPTH), BF16),
        ],
        compiler_params=pltpu.CompilerParams(vmem_limit_bytes=32 * 2**20),
    )(*operands)


def on_device(volume, basis, tile_index, tile_offset, attenuation, flux, counts):
    view = lax.axis_index("view")
    core = view & 1
    far = (view >> 1) & 1
    quarter = lax.axis_index("bin") ^ (2 * far)
    views, det_tiles, band = tile_index.shape
    slices = volume.shape[2]
    plane_groups = groups_of(PLANE)
    line_groups = groups_of(255 ^ LINE)

    def eighth(of_core):
        return lax.dynamic_slice_in_dim(volume[0], quarter * 4 + of_core * 2, 2, 1).reshape(CHANNELS, WIDTH)

    mine = eighth(core)
    theirs = lax.ppermute(eighth(1 - core), BOTH, partners(CORE))
    near = jnp.where(core == 0, jnp.concatenate([mine, theirs]), jnp.concatenate([theirs, mine]))
    stack = jnp.concatenate([near, lax.ppermute(near, BOTH, partners(FAR))], axis=0)

    vmem = pl.BlockSpec(memory_space=pltpu.VMEM)
    smem = pl.BlockSpec(memory_space=pltpu.SMEM)
    messages = pl.pallas_call(
        message_kernel,
        out_shape=[jax.ShapeDtypeStruct((2 * PAIRS + 16, 2 * SPAN), BF16)] * QUARTERS,
        in_specs=[vmem, smem, smem],
        out_specs=[vmem] * QUARTERS,
        scratch_shapes=[pltpu.VMEM((16, 2 * PAIRS, DEPTH), F32)],
    )(counts, attenuation, flux)

    stack, messages = lax.optimization_barrier((stack, messages))
    stack = jnp.broadcast_to(stack[None], (SPOTS, 2 * BLOCK, WIDTH))
    tiles = lax.all_to_all(stack, BOTH, 0, 0, tiled=True, axis_index_groups=plane_groups)

    code = tile_index.reshape(PAIRS, band) + TILES * tile_offset.reshape(PAIRS, band)
    code = jnp.concatenate([code, lax.ppermute(code, BOTH, partners(CORE))], axis=0)
    index = code & (TILES - 1)
    index = (((index >> 1) & 1) ^ far) * 2 * SPOTS + (index & 1) * SPOTS + (index >> 2)
    code = index | (code & -TILES)

    arrived = [lax.ppermute(messages[shift], BOTH, partners(shift)) if shift else messages[0] for shift in range(QUARTERS)]
    arrived = jnp.stack(arrived)
    keep = lax.dynamic_slice_in_dim(arrived, core * SPAN, SPAN, 2)
    other = lax.dynamic_slice_in_dim(arrived[:, : 2 * PAIRS], (1 - core) * SPAN, SPAN, 2)
    other = lax.ppermute(other, BOTH, partners(CORE))

    grads = local(code, tiles, basis, keep, other)

    nearer, first = far == 0, core == 0
    grads, nearer, first = lax.optimization_barrier((grads, nearer, first))
    parts = lax.all_to_all(grads, BOTH, 0, 0, tiled=True, axis_index_groups=plane_groups)
    total = jnp.sum(parts, axis=0)
    scale = 1.0 / (8.0 * math.sqrt(views * lax.axis_size("view")))
    total = (total * scale).reshape(2, 2, CHANNELS, WIDTH)
    mine = jnp.where(first, total[:, 0], total[:, 1])
    theirs = lax.ppermute(jnp.where(first, total[:, 1], total[:, 0]), BOTH, partners(CORE))
    total = jnp.where(first, jnp.stack([mine, theirs], axis=1), jnp.stack([theirs, mine], axis=1))
    total = jnp.where(nearer, total, total[::-1]).reshape(2, 1, BLOCK, WIDTH)
    blocks = jnp.broadcast_to(total, (2, QUARTERS, BLOCK, WIDTH)).reshape(2 * QUARTERS, BLOCK, WIDTH)
    blocks = lax.all_to_all(blocks, BOTH, 0, 0, tiled=True, axis_index_groups=line_groups)
    quarters = blocks[:4] + jnp.concatenate([blocks[6:], blocks[4:6]], axis=0)
    quarters = quarters.reshape(QUARTERS, 2, 3, 2, WIDTH).transpose(2, 0, 1, 3, 4)
    return quarters.reshape(1, 3, slices, WIDTH)


def solution(mesh):
    placed = (
        P("view", None, None, None),
        P(),
        P("view", None, None),
        P("view", None, None),
        P("bin", None),
        P("bin"),
        P("view", "bin", None, None),
    )
    return jax.shard_map(
        on_device,
        mesh=mesh,
        in_specs=placed,
        out_specs=P("view", None, None, None),
        check_vma=False,
    )
```

time: 558 us -> 64.9 us (0.12)
  waiting for transfers between devices: 311 us -> 8.93 us
  matrix products: 152 us -> 0 us
  local copies, waits for them, and re-layouts: 58.6 us -> 2.39 us
  starting transfers between devices: 0.31 us -> 18.8 us
  between operations: 13.3 us -> 0.22 us
  blocking collectives: 17.4 us -> 27.3 us
  Pallas kernels: 0 us -> 6.42 us
    reduce_scatter x2 -> x0, waiting for transfers between devices: 198 us -> none  [the longest x1 165 us: on_device(): shard = lax.psum_scatter(term, 'view', scatter_dimension=0, tiled=True)]
    dot_general x72 -> x0, matrix products: 152 us -> none  [the longest x12 62 us: backward(): jnp.dot(place.T, products.reshape(band, channels * width), precision=lax....]
    all_gather x2 -> x0, waiting for transfers between devices: 112 us -> none  [the longest x1 81.7 us: on_device(): whole = lax.all_gather(volume, 'view', axis=0, tiled=True)]
    while x48 -> x0, local copies, waits for them, and re-layouts: 45.6 us -> none
    all_to_all x0 -> x2, blocking collectives: none -> 27.3 us  [the longest x1 14.9 us: on_device(): lax.all_to_all(blocks, BOTH, 0, 0, tiled=True, axis_index_groups=line_gro...]
    psum x1 -> x0, blocking collectives: 17.4 us -> none  [on_device(): shard = lax.psum(shard, 'bin')]
    ppermute x0 -> x8, starting transfers between devices: none -> 11.2 us  [the longest x1 6.39 us: on_device(): lax.ppermute(near, BOTH, partners(FAR))]
    unnamed x9, local copies, waits for them, and re-layouts: 9.4 us -> 0.02 us
  transfers between devices with their start and end apart: 4 -> 9, of which waited for: 4 -> 4; matrix products, arithmetic and copies ran while one was open for 1% -> 1% of each run, Pallas kernels for 0% -> 3%
where the time goes in v2:
time: 64.9 us; the launch traced here: 64.2 us
  blocking collectives  27.3 us (42%)
  starting transfers between devices  18.8 us (29%)
  waiting for transfers between devices  8.93 us (14%)
  Pallas kernels  6.42 us (10%)
  local copies, waits for them, and re-layouts  2.39 us (4%)
    all_to_all x1, blocking collectives, on_device(): lax.all_to_all(blocks, BOTH, 0, 0, tiled=True, axis_index_groups=line_gro...  14.9 us
    all_to_all x1, blocking collectives, on_device(): lax.all_to_all(grads, BOTH, 0, 0, tiled=True, axis_index_groups=plane_gro...  12.4 us
    all_to_all x1, starting transfers between devices, on_device(): lax.all_to_all(stack, BOTH, 0, 0, tiled=True, axis_index_groups=plane_gro...  7.61 us
    ppermute x1, starting transfers between devices, on_device(): lax.ppermute(near, BOTH, partners(FAR))  6.39 us
    all_to_all x1, waiting for transfers between devices, on_device(): lax.all_to_all(stack, BOTH, 0, 0, tiled=True, axis_index_groups=plane_gro...  6.3 us
    ppermute x3, starting transfers between devices, on_device(): lax.ppermute(messages[shift], BOTH, partners(shift))  4.47 us
    pallas_call x1, Pallas kernels, local(): pl.pallas_call(local_kernel, out_shape=jax.ShapeDtypeStruct((SPOTS, 2 * B...  4.31 us
    pallas_call x1, Pallas kernels, on_device(): pl.pallas_call(message_kernel, out_shape=[jax.ShapeDtypeStruct((2 * PAIRS...  2.11 us
  transfers between devices with their start and end apart: 9, of which 4 were waited for; matrix products, arithmetic and copies ran while one was open for 1% of the time, Pallas kernels for 3%

profile of v2, /device:TPU:2, one launch (start us, length us, event | category | flops | bytes accessed | tf_op | source)
XLA Modules:
  0.0 64.2 jit_solution(6475952881398201740)
XLA Ops:
  0.0 0.8 %constant_dynamic-slice_fusion.3 = (bf16[1,3,2,256]{3,2,1,0:T(2,128)(2,1)S(1)}, bf16[1,3,2,256]{3,2,1,0:T(2,128)(2,1)S(1)}) fusion(bf16[1,3,16,256]{3,2,1,0:T(8,128)(2,1)} %param.7, s32[]{:T(128)S(6)} %select_n.51, s32[]{:T(128)S(6)} %select_n.52), kind=kLoop, calls=%fused_computation.20 | loop fusion | bytes 12296 | tf_op jit(solution)/shard_map/dynamic_slice | solution.py:193
  0.8 0.1 collective-permute-start.1
  0.9 1.1 %collective-permute-done.1 = bf16[6,256]{1,0:T(8,128)(2,1)S(1)} collective-permute-done((bf16[6,256]{1,0:T(8,128)(2,1)S(1)}, bf16[6,256]{1,0:T(8,128)(2,1)S(1)}, u32[]{:S(2)}, u32[]{:S(2)}) %collective-permute-start.1) | collective-permute-done | bytes 3104 | tf_op jit(solution)/shard_map/ppermute | solution.py:196
  2.1 6.4 %collective-permute-start.2 = (bf16[12,256]{1,0:T(8,128)(2,1)S(1)}, bf16[12,256]{1,0:T(8,128)(2,1)S(1)}, u32[]{:S(2)}, u32[]{:S(2)}) collective-permute-start(bf16[12,256]{1,0:T(8,128)(2,1)S(1)} %maximum_select_fusion.1), channel_id=1, source_target_pairs={{0,10},{1,11},{2,8},{3,9},{4,14},{5,15},{6,12},{7,13},{8,2},{9,3},... | collective-permute-start | bytes 18440 | tf_op jit(solution)/shard_map/ppermute | solution.py:198
  8.5 0.1 collective-permute-start
  8.6 2.1 %shard_map.73 = (bf16[112,512]{1,0:T(8,128)(2,1)}, bf16[112,512]{1,0:T(8,128)(2,1)}, bf16[112,512]{1,0:T(8,128)(2,1)}, bf16[112,512]{1,0:T(8,128)(2,1)}) custom-call(s32[4,2,16,1536]{3,2,1,0:T(8,128)} %counts_ref.1, f32[2,3]{1,0:T(2,128)} %attenuation_ref.1, f32[2]{0:T(128)} %flux_ref.1), custom_call_target="tpu_custom_call" | custom-call | tf_op jit(solution)/shard_map/pallas_call | solution.py:202
  10.7 1.1 %collective-permute-start.3 = (bf16[112,512]{1,0:T(8,128)(2,1)}, bf16[112,512]{1,0:T(8,128)(2,1)S(1)}, u32[]{:S(2)}, u32[]{:S(2)}) collective-permute-start(bf16[112,512]{1,0:T(8,128)(2,1)} %get-tuple-element.23), channel_id=1, source_target_pairs={{0,1},{1,0},{2,3},{3,2},{4,5},{5,4},{6,7},{7,6},{8,9},{9,8},{10,11... | collective-permute-start | bytes 344072 | tf_op jit(solution)/shard_map/ppermute | solution.py:220
  11.8 1.5 %collective-permute-start.4 = (bf16[112,512]{1,0:T(8,128)(2,1)}, bf16[112,512]{1,0:T(8,128)(2,1)S(1)}, u32[]{:S(2)}, u32[]{:S(2)}) collective-permute-start(bf16[112,512]{1,0:T(8,128)(2,1)} %get-tuple-element.24), channel_id=1, source_target_pairs={{0,2},{1,3},{2,0},{3,1},{4,6},{5,7},{6,4},{7,5},{8,10},{9,11},{10,... | collective-permute-start | bytes 344072 | tf_op jit(solution)/shard_map/ppermute | solution.py:220
  13.3 1.9 %collective-permute-start.5 = (bf16[112,512]{1,0:T(8,128)(2,1)}, bf16[112,512]{1,0:T(8,128)(2,1)S(1)}, u32[]{:S(2)}, u32[]{:S(2)}) collective-permute-start(bf16[112,512]{1,0:T(8,128)(2,1)} %get-tuple-element.25), channel_id=1, source_target_pairs={{0,3},{1,2},{2,1},{3,0},{4,7},{5,6},{6,5},{7,4},{8,11},{9,10},{10,... | collective-permute-start | bytes 344072 | tf_op jit(solution)/shard_map/ppermute | solution.py:220
  15.2 0.7 %broadcast_in_dim.6 = bf16[16,24,256]{2,1,0:T(8,128)(2,1)} broadcast(bf16[24,256]{1,0:T(8,128)(2,1)S(1)} %pad_maximum_fusion.1), dimensions={1,2} | broadcast | bytes 208896 | tf_op jit(solution)/shard_map/broadcast_in_dim | solution.py:211
  15.9 7.6 %all-to-all-start = ((bf16[16,24,256]{2,1,0:T(8,128)(2,1)}), bf16[16,24,256]{2,1,0:T(8,128)(2,1)S(1)}, u32[]{:S(2)}, u32[]{:S(2)}) async-start(bf16[16,24,256]{2,1,0:T(8,128)(2,1)} %broadcast_in_dim.6), calls=%async_computation | async-start | bytes 393216 | tf_op jit(solution)/shard_map/all_to_all | solution.py:212
  23.5 0.0 collective-permute-done
  23.5 0.0 collective-permute-done.3
  23.6 0.3 collective-permute-done.4
  23.9 0.1 pad_maximum_fusion
  24.0 0.0 copy-start
  24.0 0.1 collective-permute-start.6
  24.2 6.3 %all-to-all-done.volume_ref = bf16[16,24,256]{2,1,0:T(8,128)(2,1)S(1)} async-done(((bf16[16,24,256]{2,1,0:T(8,128)(2,1)}), bf16[16,24,256]{2,1,0:T(8,128)(2,1)S(1)}, u32[]{:S(2)}, u32[]{:S(2)}) %all-to-all-start) | async-done | bytes 196640 | tf_op jit(solution)/shard_map/all_to_all | solution.py:212
  30.5 4.3 %shard_map.74 = f32[16,24,256]{2,1,0:T(8,128)S(1)} custom-call(s32[96,56]{1,0:T(8,128)S(1)} %and_or_fusion.code_ref, bf16[16,24,256]{2,1,0:T(8,128)(2,1)S(1)} %all-to-all-done.volume_ref, bf16[16,256,128]{2,1,0:T(8,128)(2,1)S(1)} %copy-done, bf16[4,112,256]{2,1,0:T(8,128)(2,1)S(1)} %constant_dynamic-slice_fusion.1.mine_ref, ...), custom_call_target="tpu_custom_call" | custom-call | tf_op jit(solution)/shard_map/pallas_call | solution.py:165
  34.8 12.4 %all_to_all.15 = f32[16,24,256]{2,1,0:T(8,128)S(1)} all-to-all(f32[16,24,256]{2,1,0:T(8,128)S(1)} %shard_map.74), channel_id=1, replica_groups={{0,16,32,48,64,80,96,112,128,144,160,176,192,208,224,240},{1,17,33,49,6..., dimensions={0} | all-to-all | bytes 786432 | tf_op jit(solution)/shard_map/all_to_all | solution.py:230
  47.3 0.1 collective-permute-start.7
  47.4 1.2 %collective-permute-done.7 = f32[2,6,256]{2,1,0:T(8,128)S(1)} collective-permute-done((f32[2,6,256]{2,1,0:T(8,128)S(1)}, f32[2,6,256]{2,1,0:T(8,128)S(1)}, u32[]{:S(2)}, u32[]{:S(2)}) %collective-permute-start.7) | collective-permute-done | bytes 12320 | tf_op jit(solution)/shard_map/ppermute | solution.py:235
  48.6 14.9 %all_to_all.16 = f32[8,12,256]{2,1,0:T(8,128)S(1)} all-to-all(f32[8,12,256]{2,1,0:T(8,128)S(1)} %bitcast.20), channel_id=1, replica_groups={{0,1,2,3,8,9,10,11},{4,5,6,7,12,13,14,15},{16,17,18,19,24,25,26,27},{20..., dimensions={0} | all-to-all | bytes 196608 | tf_op jit(solution)/shard_map/all_to_all | solution.py:239
  63.6 0.7 %reshape.37 = f32[1,3,16,256]{3,2,1,0:T(8,128)} reshape(f32[3,4,2,2,256]{4,3,2,1,0:T(2,128)S(1)} %copy.43) | data formatting | bytes 98304 | tf_op jit(solution)/shard_map/reshape | solution.py:242
  (37 shorter events, 0.4 us)
Async XLA Ops:
  0.0 8.5 %copy-start.2 = (s32[4,12,56]{2,0,1:T(4,128)S(1)}, s32[4,12,56]{2,0,1:T(4,128)}, u32[]{:S(2)}) copy-start(s32[4,12,56]{2,0,1:T(4,128)} %param.9) | copy-start | bytes 32260
  0.0 8.5 %copy-start.3 = (s32[4,12,56]{2,0,1:T(4,128)S(1)}, s32[4,12,56]{2,0,1:T(4,128)}, u32[]{:S(2)}) copy-start(s32[4,12,56]{2,0,1:T(4,128)} %param.10) | copy-start | bytes 32260
  0.8 1.3 %collective-permute-start.1 = (bf16[6,256]{1,0:T(8,128)(2,1)S(1)}, bf16[6,256]{1,0:T(8,128)(2,1)S(1)}, u32[]{:S(2)}, u32[]{:S(2)}) collective-permute-start(bf16[6,256]{1,0:T(8,128)(2,1)S(1)} %reshape.34), channel_id=1, source_target_pairs={{0,4},{1,5},{2,6},{3,7},{4,0},{5,1},{6,2},{7,3},{8,12},{9,13},{10,... | collective-permute-start | bytes 9224 | tf_op jit(solution)/shard_map/ppermute | solution.py:196
  2.1 8.6 %collective-permute-start.2 = (bf16[12,256]{1,0:T(8,128)(2,1)S(1)}, bf16[12,256]{1,0:T(8,128)(2,1)S(1)}, u32[]{:S(2)}, u32[]{:S(2)}) collective-permute-start(bf16[12,256]{1,0:T(8,128)(2,1)S(1)} %maximum_select_fusion.1), channel_id=1, source_target_pairs={{0,10},{1,11},{2,8},{3,9},{4,14},{5,15},{6,12},{7,13},{8,2},{9,3},... | collective-permute-start | bytes 18440 | tf_op jit(solution)/shard_map/ppermute | solution.py:198
  8.5 15.0 %collective-permute-start = (s32[48,56]{1,0:T(8,128)S(1)}, s32[48,56]{1,0:T(8,128)S(1)}, u32[]{:S(2)}, u32[]{:S(2)}) collective-permute-start(s32[48,56]{1,0:T(8,128)S(1)} %add.34), channel_id=1, source_target_pairs={{0,4},{1,5},{2,6},{3,7},{4,0},{5,1},{6,2},{7,3},{8,12},{9,13},{10,... | collective-permute-start | bytes 32264 | tf_op jit(solution)/shard_map/ppermute | solution.py:215
  10.7 12.8 %collective-permute-start.3 = (bf16[112,512]{1,0:T(8,128)(2,1)}, bf16[112,512]{1,0:T(8,128)(2,1)S(1)}, u32[]{:S(2)}, u32[]{:S(2)}) collective-permute-start(bf16[112,512]{1,0:T(8,128)(2,1)} %get-tuple-element.23), channel_id=1, source_target_pairs={{0,1},{1,0},{2,3},{3,2},{4,5},{5,4},{6,7},{7,6},{8,9},{9,8},{10,11... | collective-permute-start | bytes 344072 | tf_op jit(solution)/shard_map/ppermute | solution.py:220
  11.8 12.0 %collective-permute-start.4 = (bf16[112,512]{1,0:T(8,128)(2,1)}, bf16[112,512]{1,0:T(8,128)(2,1)S(1)}, u32[]{:S(2)}, u32[]{:S(2)}) collective-permute-start(bf16[112,512]{1,0:T(8,128)(2,1)} %get-tuple-element.24), channel_id=1, source_target_pairs={{0,2},{1,3},{2,0},{3,1},{4,6},{5,7},{6,4},{7,5},{8,10},{9,11},{10,... | collective-permute-start | bytes 344072 | tf_op jit(solution)/shard_map/ppermute | solution.py:220
  13.3 10.6 %collective-permute-start.5 = (bf16[112,512]{1,0:T(8,128)(2,1)}, bf16[112,512]{1,0:T(8,128)(2,1)S(1)}, u32[]{:S(2)}, u32[]{:S(2)}) collective-permute-start(bf16[112,512]{1,0:T(8,128)(2,1)} %get-tuple-element.25), channel_id=1, source_target_pairs={{0,3},{1,2},{2,1},{3,0},{4,7},{5,6},{6,5},{7,4},{8,11},{9,10},{10,... | collective-permute-start | bytes 344072 | tf_op jit(solution)/shard_map/ppermute | solution.py:220
  15.9 8.0 %copy-start.1 = (bf16[112,512]{1,0:T(8,128)(2,1)S(1)}, bf16[112,512]{1,0:T(8,128)(2,1)}, u32[]{:S(2)}) copy-start(bf16[112,512]{1,0:T(8,128)(2,1)} %get-tuple-element.22) | copy-start | bytes 344068
  15.9 14.6 %all-to-all-start = ((bf16[16,24,256]{2,1,0:T(8,128)(2,1)}), bf16[16,24,256]{2,1,0:T(8,128)(2,1)S(1)}, u32[]{:S(2)}, u32[]{:S(2)}) async-start(bf16[16,24,256]{2,1,0:T(8,128)(2,1)} %broadcast_in_dim.6), calls=%async_computation | async-start | bytes 393216 | tf_op jit(solution)/shard_map/all_to_all | solution.py:212
  24.0 6.5 %copy-start = (bf16[16,256,128]{2,1,0:T(8,128)(2,1)S(1)}, bf16[16,256,128]{2,1,0:T(8,128)(2,1)}, u32[]{:S(2)}) copy-start(bf16[16,256,128]{2,1,0:T(8,128)(2,1)} %basis_ref.1) | copy-start | bytes 3145732
  24.0 6.5 %collective-permute-start.6 = (bf16[4,96,256]{2,1,0:T(8,128)(2,1)S(1)}, bf16[4,96,256]{2,1,0:T(8,128)(2,1)S(1)}, u32[]{:S(2)}, u32[]{:S(2)}) collective-permute-start(bf16[4,96,256]{2,1,0:T(8,128)(2,1)S(1)} %constant_dynamic-slice_fusion), channel_id=1, source_target_pairs={{0,4},{1,5},{2,6},{3,7},{4,0},{5,1},{6,2},{7,3},{8,12},{9,13},{10,... | collective-permute-start | bytes 589832 | tf_op jit(solution)/shard_map/ppermute | solution.py:224
  47.3 1.3 %collective-permute-start.7 = (f32[2,6,256]{2,1,0:T(8,128)S(1)}, f32[2,6,256]{2,1,0:T(8,128)S(1)}, u32[]{:S(2)}, u32[]{:S(2)}) collective-permute-start(f32[2,6,256]{2,1,0:T(8,128)S(1)} %select_bitcast_fusion), channel_id=1, source_target_pairs={{0,4},{1,5},{2,6},{3,7},{4,0},{5,1},{6,2},{7,3},{8,12},{9,13},{10,... | collective-permute-start | bytes 36872 | tf_op jit(solution)/shard_map/ppermute | solution.py:235

commit v3 on v2

--- a/solution.py
+++ b/solution.py
@@ -17,6 +17,7 @@
 LINE = 11
 
 SPOTS = 16
+HALF = 32
 HALF = 32
 TILES = 64
 QUARTERS = 4
@@ -88,20 +89,16 @@
         ref[2 * PAIRS :, :] = figures
 
 
-def local_kernel(
-    code_ref,
-    volume_ref,
-    basis_ref,
-    mine_ref,
-    theirs_ref,
-    grad_ref,
-    square_ref,
-    rows_ref,
-    high_ref,
-    low_ref,
-    zhigh_ref,
-    zlow_ref,
-):
+def halves_kernel(mine_ref, theirs_ref, keep_ref, send_ref):
+    first = lax.axis_index("view") & 1 == 0
+    for far, ref in enumerate((mine_ref, theirs_ref)):
+        rows = ref[...].astype(F32)
+        parts = [jnp.concatenate([rows[m * 4 + 2 * c : m * 4 + 2 * c + 2] for m in range(3)], axis=0) for c in range(2)]
+        keep_ref[far] = jnp.where(first, *parts).astype(BF16)
+        send_ref[far] = jnp.where(first, *parts[::-1]).astype(BF16)
+
+
+def forward_kernel(code_ref, volume_ref, basis_ref, chosen_ref, lines_ref, square_ref, rows_ref, high_ref, low_ref):
     rows_ref[...] = volume_ref[...].astype(F32)
     volume = [rows_ref[:, near * CHANNELS + c, :].astype(BF16) for c in range(CHANNELS) for near in range(4)]
     volume = jnp.concatenate(volume, axis=0)
@@ -116,14 +113,17 @@
                 high_ref[row : row + TILES, c * DEPTH : (c + 1) * DEPTH] = high[piece]
                 low_ref[row : row + TILES, c * DEPTH : (c + 1) * DEPTH] = low[piece]
     chosen = select(code_ref, square_ref)
+    chosen_ref[...] = chosen
     part = (lax.broadcasted_iota(jnp.int32, (2 * PAIRS, 128), 1) // TILES).astype(F32)
     turned = jnp.concatenate([chosen, chosen], axis=0).T[: 2 * PAIRS] - part
     picks = jnp.concatenate([(turned == 2 * j).astype(F32).astype(BF16) for j in range(BANK // 2)], axis=1)
-    lines = jnp.dot(picks, high_ref[...], preferred_element_type=F32) + jnp.dot(
+    lines_ref[...] = jnp.dot(picks, high_ref[...], preferred_element_type=F32) + jnp.dot(
         picks, low_ref[...], preferred_element_type=F32
     )
 
-    line = [lines[:, m * SPAN : (m + 1) * SPAN] for m in range(3)]
+
+def residual_kernel(lines_ref, mine_ref, theirs_ref, rounded_ref):
+    line = [lines_ref[:, m * SPAN : (m + 1) * SPAN] for m in range(3)]
     grads = [jnp.zeros((2 * PAIRS, SPAN), F32) for m in range(3)]
     for source in range(QUARTERS):
         figures = mine_ref[source, 2 * PAIRS :, :].astype(F32)
@@ -136,45 +136,65 @@
             photons = jnp.concatenate(photons, axis=0).astype(F32)
             misfit = photons - weight[3] * jnp.exp(-exponent)
             grads = [grads[m] + weight[m] * misfit for m in range(3)]
-    rounded = jnp.concatenate([g.astype(BF16) for g in grads], axis=1)
-
-    chosen = chosen[:, : 2 * PAIRS]
-    for j in range(BANK // 2):
-        places = [(chosen == 2 * j + p).astype(F32).astype(BF16) for p in range(2)]
+    for m in range(3):
+        rounded_ref[:, m * SPAN : (m + 1) * SPAN] = grads[m].astype(BF16)
+
+
+def back_project(rounded, chosen_ref, basis_ref, high_ref, low_ref):
+    own = [chosen_ref[far * 2 * SPOTS : far * 2 * SPOTS + SPOTS, : 2 * PAIRS] for far in range(2)]
+    own = jnp.concatenate(own, axis=0)
+    for j in range(BANK // 4):
+        places = [(own == 4 * j + p).astype(F32).astype(BF16) for p in range(4)]
         summed = jnp.dot(jnp.concatenate(places, axis=0), rounded, preferred_element_type=F32)
         high, low = split(summed)
-        for p in range(2):
-            col = (2 * j + p) * DEPTH
+        for p in range(4):
+            col = (4 * j + p) * DEPTH
             for c in range(CHANNELS):
-                piece = (slice(p * TILES, (p + 1) * TILES), slice(c * DEPTH, (c + 1) * DEPTH))
-                zhigh_ref[c * TILES : (c + 1) * TILES, col : col + DEPTH] = high[piece]
-                zlow_ref[c * TILES : (c + 1) * TILES, col : col + DEPTH] = low[piece]
+                piece = (slice(p * HALF, (p + 1) * HALF), slice(c * DEPTH, (c + 1) * DEPTH))
+                high_ref[c * HALF : (c + 1) * HALF, col : col + DEPTH] = high[piece]
+                low_ref[c * HALF : (c + 1) * HALF, col : col + DEPTH] = low[piece]
     bank = jnp.concatenate([basis_ref[p] for p in range(BANK)], axis=1)
     turn = (((1,), (1,)), ((), ()))
-    total = lax.dot_general(zhigh_ref[...], bank, turn, preferred_element_type=F32) + lax.dot_general(
-        zlow_ref[...], bank, turn, preferred_element_type=F32
-    )
-    for c in range(CHANNELS):
-        for near in range(4):
-            row = c * TILES + near * SPOTS
-            grad_ref[:, near * CHANNELS + c, :] = total[row : row + SPOTS]
-
-
-def local(*operands):
+    return lax.dot_general(high_ref[...], bank, turn, preferred_element_type=F32) + lax.dot_general(
+        low_ref[...], bank, turn, preferred_element_type=F32
+    )
+
+
+def own_kernel(rounded_ref, chosen_ref, basis_ref, total_ref, high_ref, low_ref):
+    total_ref[...] = back_project(rounded_ref[...], chosen_ref, basis_ref, high_ref, low_ref)
+
+
+def other_kernel(rounded_ref, chosen_ref, basis_ref, total_ref, grad_ref, high_ref, low_ref):
+    rounded = jnp.concatenate([rounded_ref[PAIRS:], rounded_ref[:PAIRS]], axis=0)
+    other = back_project(rounded, chosen_ref, basis_ref, high_ref, low_ref)
+    own = total_ref[...]
+    view = lax.axis_index("view")
+    halves = jnp.where(view & 1 == 0, own, other), jnp.where(view & 1 == 0, other, own)
+    for core in range(2):
+        for c in range(CHANNELS):
+            pair = halves[core][c * HALF : (c + 1) * HALF]
+            first, second = pair[:SPOTS], pair[SPOTS:]
+            grad_ref[:, core * CHANNELS + c, :] = jnp.where(view & 2 == 0, first, second)
+            grad_ref[:, BLOCK + core * CHANNELS + c, :] = jnp.where(view & 2 == 0, second, first)
+
+
+FORWARD = [
+    pltpu.VMEM((128, 128), F32),
+    pltpu.VMEM((SPOTS, 2 * BLOCK, WIDTH), F32),
+    pltpu.VMEM((BANK * TILES, CHANNELS * DEPTH), BF16),
+    pltpu.VMEM((BANK * TILES, CHANNELS * DEPTH), BF16),
+]
+BACKWARD = [pltpu.VMEM((CHANNELS * HALF, BANK * DEPTH), BF16)] * 2
+
+
+def call(kernel, out_shape, scratch, *operands):
     vmem = pl.BlockSpec(memory_space=pltpu.VMEM)
     return pl.pallas_call(
-        local_kernel,
-        out_shape=jax.ShapeDtypeStruct((SPOTS, 2 * BLOCK, WIDTH), F32),
+        kernel,
+        out_shape=out_shape,
         in_specs=[vmem] * len(operands),
-        out_specs=vmem,
-        scratch_shapes=[
-            pltpu.VMEM((128, 128), F32),
-            pltpu.VMEM((SPOTS, 2 * BLOCK, WIDTH), F32),
-            pltpu.VMEM((BANK * TILES, CHANNELS * DEPTH), BF16),
-            pltpu.VMEM((BANK * TILES, CHANNELS * DEPTH), BF16),
-            pltpu.VMEM((CHANNELS * TILES, BANK * DEPTH), BF16),
-            pltpu.VMEM((CHANNELS * TILES, BANK * DEPTH), BF16),
-        ],
+        out_specs=jax.tree.map(lambda _: vmem, out_shape),
+        scratch_shapes=scratch,
         compiler_params=pltpu.CompilerParams(vmem_limit_bytes=32 * 2**20),
     )(*operands)
 
@@ -189,13 +209,8 @@
     plane_groups = groups_of(PLANE)
     line_groups = groups_of(255 ^ LINE)
 
-    def eighth(of_core):
-        return lax.dynamic_slice_in_dim(volume[0], quarter * 4 + of_core * 2, 2, 1).reshape(CHANNELS, WIDTH)
-
-    mine = eighth(core)
-    theirs = lax.ppermute(eighth(1 - core), BOTH, partners(CORE))
-    near = jnp.where(core == 0, jnp.concatenate([mine, theirs]), jnp.concatenate([theirs, mine]))
-    stack = jnp.concatenate([near, lax.ppermute(near, BOTH, partners(FAR))], axis=0)
+    mine = lax.dynamic_slice_in_dim(volume[0], quarter * 4, 4, 1).reshape(2 * CHANNELS, WIDTH)
+    theirs = lax.ppermute(mine, BOTH, partners(FAR))
 
     vmem = pl.BlockSpec(memory_space=pltpu.VMEM)
     smem = pl.BlockSpec(memory_space=pltpu.SMEM)
@@ -205,36 +220,61 @@
         in_specs=[vmem, smem, smem],
         out_specs=[vmem] * QUARTERS,
         scratch_shapes=[pltpu.VMEM((16, 2 * PAIRS, DEPTH), F32)],
+        compiler_params=pltpu.CompilerParams(vmem_limit_bytes=8 * 2**20),
     )(counts, attenuation, flux)
 
-    stack, messages = lax.optimization_barrier((stack, messages))
-    stack = jnp.broadcast_to(stack[None], (SPOTS, 2 * BLOCK, WIDTH))
+    mine, theirs = pl.pallas_call(
+        halves_kernel,
+        out_shape=[jax.ShapeDtypeStruct((2, CHANNELS, WIDTH), BF16)] * 2,
+        in_specs=[vmem] * 2,
+        out_specs=[vmem] * 2,
+        compiler_params=pltpu.CompilerParams(vmem_limit_bytes=4 * 2**20),
+        cost_estimate=pl.CostEstimate(flops=0, bytes_accessed=10**8, transcendentals=0),
+    )(mine, theirs)
+    theirs = lax.ppermute(theirs, BOTH, partners(CORE))
+    stack = jnp.stack([mine, theirs], axis=1)
+    stack = jnp.broadcast_to(stack.reshape(1, 2 * BLOCK, WIDTH), (SPOTS, 2 * BLOCK, WIDTH))
     tiles = lax.all_to_all(stack, BOTH, 0, 0, tiled=True, axis_index_groups=plane_groups)
-
-    code = tile_index.reshape(PAIRS, band) + TILES * tile_offset.reshape(PAIRS, band)
-    code = jnp.concatenate([code, lax.ppermute(code, BOTH, partners(CORE))], axis=0)
-    index = code & (TILES - 1)
-    index = (((index >> 1) & 1) ^ far) * 2 * SPOTS + (index & 1) * SPOTS + (index >> 2)
-    code = index | (code & -TILES)
 
     arrived = [lax.ppermute(messages[shift], BOTH, partners(shift)) if shift else messages[0] for shift in range(QUARTERS)]
     arrived = jnp.stack(arrived)
     keep = lax.dynamic_slice_in_dim(arrived, core * SPAN, SPAN, 2)
     other = lax.dynamic_slice_in_dim(arrived[:, : 2 * PAIRS], (1 - core) * SPAN, SPAN, 2)
+
+    code = tile_index.reshape(PAIRS, band) + TILES * tile_offset.reshape(PAIRS, band)
     other = lax.ppermute(other, BOTH, partners(CORE))
-
-    grads = local(code, tiles, basis, keep, other)
-
-    nearer, first = far == 0, core == 0
-    grads, nearer, first = lax.optimization_barrier((grads, nearer, first))
+    code = jnp.concatenate([code, lax.ppermute(code, BOTH, partners(CORE))], axis=0)
+    index = (code & (TILES - 1)) ^ (view & 3)
+    index = ((index >> 1) & 1) * 2 * SPOTS + (index & 1) * SPOTS + (index >> 2)
+    code = index | (code & -TILES)
+
+    wide = CHANNELS * DEPTH
+    chosen, lines = call(
+        forward_kernel,
+        [jax.ShapeDtypeStruct((TILES, 128), F32), jax.ShapeDtypeStruct((2 * PAIRS, wide), F32)],
+        FORWARD,
+        code,
+        tiles,
+        basis,
+    )
+    rounded = call(residual_kernel, jax.ShapeDtypeStruct((2 * PAIRS, wide), BF16), [], lines, keep, other)
+    swapped = lax.ppermute(rounded, BOTH, partners(CORE))
+    total = call(
+        own_kernel, jax.ShapeDtypeStruct((CHANNELS * HALF, WIDTH), F32), BACKWARD, rounded, chosen, basis
+    )
+    grads = call(
+        other_kernel,
+        jax.ShapeDtypeStruct((SPOTS, 2 * BLOCK, WIDTH), F32),
+        BACKWARD,
+        swapped,
+        chosen,
+        basis,
+        total,
+    )
+
     parts = lax.all_to_all(grads, BOTH, 0, 0, tiled=True, axis_index_groups=plane_groups)
-    total = jnp.sum(parts, axis=0)
     scale = 1.0 / (8.0 * math.sqrt(views * lax.axis_size("view")))
-    total = (total * scale).reshape(2, 2, CHANNELS, WIDTH)
-    mine = jnp.where(first, total[:, 0], total[:, 1])
-    theirs = lax.ppermute(jnp.where(first, total[:, 1], total[:, 0]), BOTH, partners(CORE))
-    total = jnp.where(first, jnp.stack([mine, theirs], axis=1), jnp.stack([theirs, mine], axis=1))
-    total = jnp.where(nearer, total, total[::-1]).reshape(2, 1, BLOCK, WIDTH)
+    total = (jnp.sum(parts, axis=0) * scale).reshape(2, 1, BLOCK, WIDTH)
     blocks = jnp.broadcast_to(total, (2, QUARTERS, BLOCK, WIDTH)).reshape(2 * QUARTERS, BLOCK, WIDTH)
     blocks = lax.all_to_all(blocks, BOTH, 0, 0, tiled=True, axis_index_groups=line_groups)
     quarters = blocks[:4] + jnp.concatenate([blocks[6:], blocks[4:6]], axis=0)

time: 64.9 us -> 62.6 us (0.965)
  blocking collectives: 27.3 us -> 25.6 us
  local copies, waits for them, and re-layouts: 2.39 us -> 3.99 us
  waiting for transfers between devices: 8.93 us -> 7.97 us
  Pallas kernels: 6.42 us -> 5.52 us
    all_to_all x1, blocking collectives: 14.9 us -> 12.1 us  [on_device(): lax.all_to_all(blocks, BOTH, 0, 0, tiled=True, axis_index_groups=line_gro...]
    unnamed x9 -> x15, local copies, waits for them, and re-layouts: 0.02 us -> 2.43 us
    pallas_call x1, Pallas kernels: 2.11 us -> 0.77 us  [on_device(): pl.pallas_call(message_kernel, out_shape=[jax.ShapeDtypeStruct((2 * PAIRS...]
    all_to_all x1, blocking collectives: 12.4 us -> 13.6 us  [on_device(): lax.all_to_all(grads, BOTH, 0, 0, tiled=True, axis_index_groups=plane_gro...]
    ppermute x3, waiting for transfers between devices: 2.29 us -> 1.32 us  [the longest x1 1.14 us: on_device(): theirs = lax.ppermute(theirs, BOTH, partners(CORE))]
    dynamic_slice x1, local copies, waits for them, and re-layouts: 0.79 us -> 0.01 us  [on_device(): lax.dynamic_slice_in_dim(volume[0], quarter * 4, 4, 1)]
    pallas_call x1 -> x5, Pallas kernels: 4.31 us -> 4.76 us  [the longest x4 4.74 us: call(): pl.pallas_call(kernel, out_shape=out_shape, in_specs=[vmem] * len(operand...]
  transfers between devices with their start and end apart: 9 -> 9, of which waited for: 4 -> 3; matrix products, arithmetic and copies ran while one was open for 1% -> 1% of each run, Pallas kernels for 3% -> 6%
where the time goes in v3:
time: 62.6 us; the launch traced here: 62.2 us
  blocking collectives  25.6 us (41%)
  starting transfers between devices  18.7 us (30%)
  waiting for transfers between devices  7.97 us (13%)
  Pallas kernels  5.52 us (9%)
  local copies, waits for them, and re-layouts  3.99 us (6%)
    all_to_all x1, blocking collectives, on_device(): lax.all_to_all(grads, BOTH, 0, 0, tiled=True, axis_index_groups=plane_gro...  13.6 us
    all_to_all x1, blocking collectives, on_device(): lax.all_to_all(blocks, BOTH, 0, 0, tiled=True, axis_index_groups=line_gro...  12.1 us
    all_to_all x1, starting transfers between devices, on_device(): lax.all_to_all(stack, BOTH, 0, 0, tiled=True, axis_index_groups=plane_gro...  7.48 us
    all_to_all x1, waiting for transfers between devices, on_device(): lax.all_to_all(stack, BOTH, 0, 0, tiled=True, axis_index_groups=plane_gro...  6.63 us
    ppermute x1, starting transfers between devices, on_device(): theirs = lax.ppermute(mine, BOTH, partners(FAR))  6.39 us
    pallas_call x4, Pallas kernels, call(): pl.pallas_call(kernel, out_shape=out_shape, in_specs=[vmem] * len(operand...  4.74 us
    ppermute x3, starting transfers between devices, on_device(): lax.ppermute(messages[shift], BOTH, partners(shift))  4.47 us
    unnamed x15, local copies, waits for them, and re-layouts  2.43 us
  transfers between devices with their start and end apart: 9, of which 3 were waited for; matrix products, arithmetic and copies ran while one was open for 1% of the time, Pallas kernels for 6%

profile of v3, /device:TPU:2, one launch (start us, length us, event | category | flops | bytes accessed | tf_op | source)
XLA Modules:
  0.0 62.2 jit_solution(17750411681870365130)
XLA Ops:
  0.0 0.7 %copy-done = bf16[1,3,16,256]{3,2,1,0:T(8,128)(2,1)S(1)} copy-done((bf16[1,3,16,256]{3,2,1,0:T(8,128)(2,1)S(1)}, bf16[1,3,16,256]{3,2,1,0:T(8,128)(2,1)}, u32[]{:S(2)}) %copy-start) | copy-done | bytes 24600
  0.8 6.4 %collective-permute-start.1 = (bf16[12,256]{1,0:T(8,128)(2,1)S(1)}, bf16[12,256]{1,0:T(8,128)(2,1)S(1)}, u32[]{:S(2)}, u32[]{:S(2)}) collective-permute-start(bf16[12,256]{1,0:T(8,128)(2,1)S(1)} %reshape.29.mine_ref), channel_id=1, source_target_pairs={{0,10},{1,11},{2,8},{3,9},{4,14},{5,15},{6,12},{7,13},{8,2},{9,3},... | collective-permute-start | bytes 18440 | tf_op jit(solution)/shard_map/ppermute | solution.py:213
  7.2 0.1 collective-permute-start
  7.3 0.5 copy-done.3
  7.9 1.1 %copy-done.2 = s32[4,2,16,1536]{3,2,1,0:T(8,128)S(1)} copy-done((s32[4,2,16,1536]{3,2,1,0:T(8,128)S(1)}, s32[4,2,16,1536]{3,2,1,0:T(8,128)}, u32[]{:S(2)}) %copy-start.2) | copy-done | bytes 786456
  9.0 0.8 %shard_map.75 = (bf16[112,512]{1,0:T(8,128)(2,1)S(1)}, bf16[112,512]{1,0:T(8,128)(2,1)S(1)}, bf16[112,512]{1,0:T(8,128)(2,1)S(1)}, bf16[112,512]{1,0:T(8,128)(2,1)S(1)}) custom-call(s32[4,2,16,1536]{3,2,1,0:T(8,128)S(1)} %copy-done.2, f32[2,3]{1,0:T(2,128)S(1)} %copy-done.3, f32[2]{0:T(128)S(1)} %copy-done.4), custom_call_target="tpu_custom_call" | custom-call | tf_op jit(solution)/shard_map/pallas_call | solution.py:217
  9.8 1.1 %collective-permute-start.3 = (bf16[112,512]{1,0:T(8,128)(2,1)S(1)}, bf16[112,512]{1,0:T(8,128)(2,1)S(1)}, u32[]{:S(2)}, u32[]{:S(2)}) collective-permute-start(bf16[112,512]{1,0:T(8,128)(2,1)S(1)} %get-tuple-element.17), channel_id=1, source_target_pairs={{0,1},{1,0},{2,3},{3,2},{4,5},{5,4},{6,7},{7,6},{8,9},{9,8},{10,11... | collective-permute-start | bytes 344072 | tf_op jit(solution)/shard_map/ppermute | solution.py:239
  10.9 1.5 %collective-permute-start.4 = (bf16[112,512]{1,0:T(8,128)(2,1)S(1)}, bf16[112,512]{1,0:T(8,128)(2,1)S(1)}, u32[]{:S(2)}, u32[]{:S(2)}) collective-permute-start(bf16[112,512]{1,0:T(8,128)(2,1)S(1)} %get-tuple-element.18), channel_id=1, source_target_pairs={{0,2},{1,3},{2,0},{3,1},{4,6},{5,7},{6,4},{7,5},{8,10},{9,11},{10,... | collective-permute-start | bytes 344072 | tf_op jit(solution)/shard_map/ppermute | solution.py:239
  12.3 1.9 %collective-permute-start.5 = (bf16[112,512]{1,0:T(8,128)(2,1)S(1)}, bf16[112,512]{1,0:T(8,128)(2,1)S(1)}, u32[]{:S(2)}, u32[]{:S(2)}) collective-permute-start(bf16[112,512]{1,0:T(8,128)(2,1)S(1)} %get-tuple-element.19), channel_id=1, source_target_pairs={{0,3},{1,2},{2,1},{3,0},{4,7},{5,6},{6,5},{7,4},{8,11},{9,10},{10,... | collective-permute-start | bytes 344072 | tf_op jit(solution)/shard_map/ppermute | solution.py:239
  14.3 0.1 collective-permute-start.2
  14.4 1.1 %collective-permute-done.2 = bf16[2,6,256]{2,1,0:T(8,128)(2,1)S(1)} collective-permute-done((bf16[2,6,256]{2,1,0:T(8,128)(2,1)S(1)}, bf16[2,6,256]{2,1,0:T(8,128)(2,1)S(1)}, u32[]{:S(2)}, u32[]{:S(2)}) %collective-permute-start.2) | collective-permute-done | bytes 6176 | tf_op jit(solution)/shard_map/ppermute | solution.py:234
  15.6 0.7 %broadcast_in_dim.13 = bf16[16,24,256]{2,1,0:T(8,128)(2,1)} broadcast(bf16[24,256]{1,0:T(8,128)(2,1)S(1)} %broadcast_in_dim.12), dimensions={1,2} | broadcast | bytes 208896 | tf_op jit(solution)/shard_map/broadcast_in_dim | solution.py:236
  16.3 7.5 %all-to-all-start = ((bf16[16,24,256]{2,1,0:T(8,128)(2,1)}), bf16[16,24,256]{2,1,0:T(8,128)(2,1)S(1)}, u32[]{:S(2)}, u32[]{:S(2)}) async-start(bf16[16,24,256]{2,1,0:T(8,128)(2,1)} %broadcast_in_dim.13), calls=%async_computation | async-start | bytes 393216 | tf_op jit(solution)/shard_map/all_to_all | solution.py:237
  23.9 0.1 collective-permute-start.6
  24.1 6.6 %all-to-all-done.volume_ref = bf16[16,24,256]{2,1,0:T(8,128)(2,1)S(1)} async-done(((bf16[16,24,256]{2,1,0:T(8,128)(2,1)}), bf16[16,24,256]{2,1,0:T(8,128)(2,1)S(1)}, u32[]{:S(2)}, u32[]{:S(2)}) %all-to-all-start) | async-done | bytes 196640 | tf_op jit(solution)/shard_map/all_to_all | solution.py:237
  30.7 1.9 %shard_map.74 = (f32[64,128]{1,0:T(8,128)S(1)}, f32[96,768]{1,0:T(8,128)S(1)}) custom-call(s32[96,56]{1,0:T(8,128)S(1)} %and_or_fusion.code_ref, bf16[16,24,256]{2,1,0:T(8,128)(2,1)S(1)} %all-to-all-done.volume_ref, bf16[16,256,128]{2,1,0:T(8,128)(2,1)S(1)} %copy-done.1), custom_call_target="tpu_custom_call" | custom-call | tf_op jit(solution)/shard_map/pallas_call | solution.py:192
  32.6 0.4 shard_map.76.rounded_ref
  33.1 0.1 collective-permute-start.7
  33.2 1.2 %shard_map.77.total_ref = f32[192,256]{1,0:T(8,128)S(1)} custom-call(bf16[96,768]{1,0:T(8,128)(2,1)S(1)} %shard_map.76.rounded_ref, f32[64,128]{1,0:T(8,128)S(1)} %get-tuple-element.20.chosen_ref, bf16[16,256,128]{2,1,0:T(8,128)(2,1)S(1)} %copy-done.1), custom_call_target="tpu_custom_call" | custom-call | tf_op jit(solution)/shard_map/pallas_call | solution.py:192
  34.4 0.2 collective-permute-done.7.rounded_ref
  34.5 1.3 %shard_map.78 = f32[16,24,256]{2,1,0:T(8,128)S(1)} custom-call(bf16[96,768]{1,0:T(8,128)(2,1)S(1)} %collective-permute-done.7.rounded_ref, f32[64,128]{1,0:T(8,128)S(1)} %get-tuple-element.20.chosen_ref, bf16[16,256,128]{2,1,0:T(8,128)(2,1)S(1)} %copy-done.1, f32[192,256]{1,0:T(8,128)S(1)} %shard_map.77.total_ref), custom_call_target="tpu_custom_call" | custom-call | tf_op jit(solution)/shard_map/pallas_call | solution.py:192
  35.8 13.6 %all_to_all.15 = f32[16,24,256]{2,1,0:T(8,128)S(1)} all-to-all(f32[16,24,256]{2,1,0:T(8,128)S(1)} %shard_map.78), channel_id=1, replica_groups={{0,16,32,48,64,80,96,112,128,144,160,176,192,208,224,240},{1,17,33,49,6..., dimensions={0} | all-to-all | bytes 786432 | tf_op jit(solution)/shard_map/all_to_all | solution.py:275
  49.4 12.1 %all_to_all.16 = f32[8,12,256]{2,1,0:T(8,128)S(1)} all-to-all(f32[8,12,256]{2,1,0:T(8,128)S(1)} %bitcast.12), channel_id=1, replica_groups={{0,1,2,3,8,9,10,11},{4,5,6,7,12,13,14,15},{16,17,18,19,24,25,26,27},{20..., dimensions={0} | all-to-all | bytes 196608 | tf_op jit(solution)/shard_map/all_to_all | solution.py:279
  61.6 0.7 %reshape.32 = f32[1,3,16,256]{3,2,1,0:T(8,128)} reshape(f32[3,4,2,2,256]{4,3,2,1,0:T(2,128)S(1)} %copy.24) | data formatting | bytes 98304 | tf_op jit(solution)/shard_map/reshape | solution.py:282
  (41 shorter events, 0.4 us)
Async XLA Ops:
  0.0 0.7 %copy-start = (bf16[1,3,16,256]{3,2,1,0:T(8,128)(2,1)S(1)}, bf16[1,3,16,256]{3,2,1,0:T(8,128)(2,1)}, u32[]{:S(2)}) copy-start(bf16[1,3,16,256]{3,2,1,0:T(8,128)(2,1)} %param.7) | copy-start | bytes 73732
  0.0 7.2 %copy-start.6 = (s32[4,12,56]{2,0,1:T(4,128)S(1)}, s32[4,12,56]{2,0,1:T(4,128)}, u32[]{:S(2)}) copy-start(s32[4,12,56]{2,0,1:T(4,128)} %param.10) | copy-start | bytes 32260
  0.0 7.2 %copy-start.5 = (s32[4,12,56]{2,0,1:T(4,128)S(1)}, s32[4,12,56]{2,0,1:T(4,128)}, u32[]{:S(2)}) copy-start(s32[4,12,56]{2,0,1:T(4,128)} %param.9) | copy-start | bytes 32260
  0.8 13.5 %collective-permute-start.1 = (bf16[12,256]{1,0:T(8,128)(2,1)S(1)}, bf16[12,256]{1,0:T(8,128)(2,1)S(1)}, u32[]{:S(2)}, u32[]{:S(2)}) collective-permute-start(bf16[12,256]{1,0:T(8,128)(2,1)S(1)} %reshape.29.mine_ref), channel_id=1, source_target_pairs={{0,10},{1,11},{2,8},{3,9},{4,14},{5,15},{6,12},{7,13},{8,2},{9,3},... | collective-permute-start | bytes 18440 | tf_op jit(solution)/shard_map/ppermute | solution.py:213
  7.2 0.7 %copy-start.3 = (f32[2,3]{1,0:T(2,128)S(1)}, f32[2,3]{1,0:T(2,128)}, u32[]{:S(2)}) copy-start(f32[2,3]{1,0:T(2,128)} %attenuation_ref.1) | copy-start | bytes 76
  7.2 0.7 %copy-start.4 = (f32[2]{0:T(128)S(1)}, f32[2]{0:T(128)}, u32[]{:S(2)}) copy-start(f32[2]{0:T(128)} %flux_ref.1) | copy-start | bytes 28
  7.2 7.2 %collective-permute-start = (s32[48,56]{1,0:T(8,128)S(1)}, s32[48,56]{1,0:T(8,128)S(1)}, u32[]{:S(2)}, u32[]{:S(2)}) collective-permute-start(s32[48,56]{1,0:T(8,128)S(1)} %add.25), channel_id=1, source_target_pairs={{0,4},{1,5},{2,6},{3,7},{4,0},{5,1},{6,2},{7,3},{8,12},{9,13},{10,... | collective-permute-start | bytes 32264 | tf_op jit(solution)/shard_map/ppermute | solution.py:246
  7.9 1.1 %copy-start.2 = (s32[4,2,16,1536]{3,2,1,0:T(8,128)S(1)}, s32[4,2,16,1536]{3,2,1,0:T(8,128)}, u32[]{:S(2)}) copy-start(s32[4,2,16,1536]{3,2,1,0:T(8,128)} %counts_ref.1) | copy-start | bytes 2359300
  9.8 14.0 %collective-permute-start.3 = (bf16[112,512]{1,0:T(8,128)(2,1)S(1)}, bf16[112,512]{1,0:T(8,128)(2,1)S(1)}, u32[]{:S(2)}, u32[]{:S(2)}) collective-permute-start(bf16[112,512]{1,0:T(8,128)(2,1)S(1)} %get-tuple-element.17), channel_id=1, source_target_pairs={{0,1},{1,0},{2,3},{3,2},{4,5},{5,4},{6,7},{7,6},{8,9},{9,8},{10,11... | collective-permute-start | bytes 344072 | tf_op jit(solution)/shard_map/ppermute | solution.py:239
  10.9 12.9 %collective-permute-start.4 = (bf16[112,512]{1,0:T(8,128)(2,1)S(1)}, bf16[112,512]{1,0:T(8,128)(2,1)S(1)}, u32[]{:S(2)}, u32[]{:S(2)}) collective-permute-start(bf16[112,512]{1,0:T(8,128)(2,1)S(1)} %get-tuple-element.18), channel_id=1, source_target_pairs={{0,2},{1,3},{2,0},{3,1},{4,6},{5,7},{6,4},{7,5},{8,10},{9,11},{10,... | collective-permute-start | bytes 344072 | tf_op jit(solution)/shard_map/ppermute | solution.py:239
  12.3 11.4 %collective-permute-start.5 = (bf16[112,512]{1,0:T(8,128)(2,1)S(1)}, bf16[112,512]{1,0:T(8,128)(2,1)S(1)}, u32[]{:S(2)}, u32[]{:S(2)}) collective-permute-start(bf16[112,512]{1,0:T(8,128)(2,1)S(1)} %get-tuple-element.19), channel_id=1, source_target_pairs={{0,3},{1,2},{2,1},{3,0},{4,7},{5,6},{6,5},{7,4},{8,11},{9,10},{10,... | collective-permute-start | bytes 344072 | tf_op jit(solution)/shard_map/ppermute | solution.py:239
  14.3 1.3 %collective-permute-start.2 = (bf16[2,6,256]{2,1,0:T(8,128)(2,1)S(1)}, bf16[2,6,256]{2,1,0:T(8,128)(2,1)S(1)}, u32[]{:S(2)}, u32[]{:S(2)}) collective-permute-start(bf16[2,6,256]{2,1,0:T(8,128)(2,1)S(1)} %get-tuple-element.14), channel_id=1, source_target_pairs={{0,4},{1,5},{2,6},{3,7},{4,0},{5,1},{6,2},{7,3},{8,12},{9,13},{10,... | collective-permute-start | bytes 18440 | tf_op jit(solution)/shard_map/ppermute | solution.py:234
  16.3 14.5 %all-to-all-start = ((bf16[16,24,256]{2,1,0:T(8,128)(2,1)}), bf16[16,24,256]{2,1,0:T(8,128)(2,1)S(1)}, u32[]{:S(2)}, u32[]{:S(2)}) async-start(bf16[16,24,256]{2,1,0:T(8,128)(2,1)} %broadcast_in_dim.13), calls=%async_computation | async-start | bytes 393216 | tf_op jit(solution)/shard_map/all_to_all | solution.py:237
  23.9 6.9 %copy-start.1 = (bf16[16,256,128]{2,1,0:T(8,128)(2,1)S(1)}, bf16[16,256,128]{2,1,0:T(8,128)(2,1)}, u32[]{:S(2)}) copy-start(bf16[16,256,128]{2,1,0:T(8,128)(2,1)} %basis_ref.5) | copy-start | bytes 3145732
  23.9 8.7 %collective-permute-start.6 = (bf16[4,96,256]{2,1,0:T(8,128)(2,1)S(1)}, bf16[4,96,256]{2,1,0:T(8,128)(2,1)S(1)}, u32[]{:S(2)}, u32[]{:S(2)}) collective-permute-start(bf16[4,96,256]{2,1,0:T(8,128)(2,1)S(1)} %constant_dynamic-slice_fusion), channel_id=1, source_target_pairs={{0,4},{1,5},{2,6},{3,7},{4,0},{5,1},{6,2},{7,3},{8,12},{9,13},{10,... | collective-permute-start | bytes 589832 | tf_op jit(solution)/shard_map/ppermute | solution.py:245
  33.1 1.5 %collective-permute-start.7 = (bf16[96,768]{1,0:T(8,128)(2,1)S(1)}, bf16[96,768]{1,0:T(8,128)(2,1)S(1)}, u32[]{:S(2)}, u32[]{:S(2)}) collective-permute-start(bf16[96,768]{1,0:T(8,128)(2,1)S(1)} %shard_map.76.rounded_ref), channel_id=1, source_target_pairs={{0,4},{1,5},{2,6},{3,7},{4,0},{5,1},{6,2},{7,3},{8,12},{9,13},{10,... | collective-permute-start | bytes 442376 | tf_op jit(solution)/shard_map/ppermute | solution.py:261

commit v4 on v3

--- a/solution.py
+++ b/solution.py
@@ -98,28 +98,25 @@
         send_ref[far] = jnp.where(first, *parts[::-1]).astype(BF16)
 
 
-def forward_kernel(code_ref, volume_ref, basis_ref, chosen_ref, lines_ref, square_ref, rows_ref, high_ref, low_ref):
+def forward_kernel(code_ref, volume_ref, basis_ref, chosen_ref, lines_ref, square_ref, rows_ref, parts_ref):
     rows_ref[...] = volume_ref[...].astype(F32)
     volume = [rows_ref[:, near * CHANNELS + c, :].astype(BF16) for c in range(CHANNELS) for near in range(4)]
     volume = jnp.concatenate(volume, axis=0)
     for j in range(BANK // 2):
         both = jnp.concatenate([basis_ref[2 * j], basis_ref[2 * j + 1]], axis=1)
         table = jnp.dot(volume, both, preferred_element_type=F32)
-        high, low = split(table)
-        for p in range(2):
-            row = (2 * j + p) * TILES
-            for c in range(CHANNELS):
-                piece = (slice(c * TILES, (c + 1) * TILES), slice(p * DEPTH, (p + 1) * DEPTH))
-                high_ref[row : row + TILES, c * DEPTH : (c + 1) * DEPTH] = high[piece]
-                low_ref[row : row + TILES, c * DEPTH : (c + 1) * DEPTH] = low[piece]
+        for part, value in enumerate(split(table)):
+            for p in range(2):
+                row = (part * BANK + 2 * j + p) * TILES
+                for c in range(CHANNELS):
+                    piece = value[c * TILES : (c + 1) * TILES, p * DEPTH : (p + 1) * DEPTH]
+                    parts_ref[row : row + TILES, c * DEPTH : (c + 1) * DEPTH] = piece
     chosen = select(code_ref, square_ref)
     chosen_ref[...] = chosen
     part = (lax.broadcasted_iota(jnp.int32, (2 * PAIRS, 128), 1) // TILES).astype(F32)
     turned = jnp.concatenate([chosen, chosen], axis=0).T[: 2 * PAIRS] - part
-    picks = jnp.concatenate([(turned == 2 * j).astype(F32).astype(BF16) for j in range(BANK // 2)], axis=1)
-    lines_ref[...] = jnp.dot(picks, high_ref[...], preferred_element_type=F32) + jnp.dot(
-        picks, low_ref[...], preferred_element_type=F32
-    )
+    picks = [(turned == 2 * j).astype(F32).astype(BF16) for j in range(BANK // 2)]
+    lines_ref[...] = jnp.dot(jnp.concatenate(picks * 2, axis=1), parts_ref[...], preferred_element_type=F32)
 
 
 def residual_kernel(lines_ref, mine_ref, theirs_ref, rounded_ref):
@@ -140,33 +137,32 @@
         rounded_ref[:, m * SPAN : (m + 1) * SPAN] = grads[m].astype(BF16)
 
 
-def back_project(rounded, chosen_ref, basis_ref, high_ref, low_ref):
+def back_project(rounded, chosen_ref, basis_ref, parts_ref):
     own = [chosen_ref[far * 2 * SPOTS : far * 2 * SPOTS + SPOTS, : 2 * PAIRS] for far in range(2)]
     own = jnp.concatenate(own, axis=0)
     for j in range(BANK // 4):
         places = [(own == 4 * j + p).astype(F32).astype(BF16) for p in range(4)]
         summed = jnp.dot(jnp.concatenate(places, axis=0), rounded, preferred_element_type=F32)
-        high, low = split(summed)
-        for p in range(4):
-            col = (4 * j + p) * DEPTH
-            for c in range(CHANNELS):
-                piece = (slice(p * HALF, (p + 1) * HALF), slice(c * DEPTH, (c + 1) * DEPTH))
-                high_ref[c * HALF : (c + 1) * HALF, col : col + DEPTH] = high[piece]
-                low_ref[c * HALF : (c + 1) * HALF, col : col + DEPTH] = low[piece]
+        for part, value in enumerate(split(summed)):
+            for p in range(4):
+                col = (4 * j + p) * DEPTH
+                for c in range(CHANNELS):
+                    row = (part * CHANNELS + c) * HALF
+                    piece = value[p * HALF : (p + 1) * HALF, c * DEPTH : (c + 1) * DEPTH]
+                    parts_ref[row : row + HALF, col : col + DEPTH] = piece
     bank = jnp.concatenate([basis_ref[p] for p in range(BANK)], axis=1)
     turn = (((1,), (1,)), ((), ()))
-    return lax.dot_general(high_ref[...], bank, turn, preferred_element_type=F32) + lax.dot_general(
-        low_ref[...], bank, turn, preferred_element_type=F32
-    )
-
-
-def own_kernel(rounded_ref, chosen_ref, basis_ref, total_ref, high_ref, low_ref):
-    total_ref[...] = back_project(rounded_ref[...], chosen_ref, basis_ref, high_ref, low_ref)
-
-
-def other_kernel(rounded_ref, chosen_ref, basis_ref, total_ref, grad_ref, high_ref, low_ref):
+    total = lax.dot_general(parts_ref[...], bank, turn, preferred_element_type=F32)
+    return total[: CHANNELS * HALF] + total[CHANNELS * HALF :]
+
+
+def own_kernel(rounded_ref, chosen_ref, basis_ref, total_ref, parts_ref):
+    total_ref[...] = back_project(rounded_ref[...], chosen_ref, basis_ref, parts_ref)
+
+
+def other_kernel(rounded_ref, chosen_ref, basis_ref, total_ref, grad_ref, parts_ref):
     rounded = jnp.concatenate([rounded_ref[PAIRS:], rounded_ref[:PAIRS]], axis=0)
-    other = back_project(rounded, chosen_ref, basis_ref, high_ref, low_ref)
+    other = back_project(rounded, chosen_ref, basis_ref, parts_ref)
     own = total_ref[...]
     view = lax.axis_index("view")
     halves = jnp.where(view & 1 == 0, own, other), jnp.where(view & 1 == 0, other, own)
@@ -181,10 +177,9 @@
 FORWARD = [
     pltpu.VMEM((128, 128), F32),
     pltpu.VMEM((SPOTS, 2 * BLOCK, WIDTH), F32),
-    pltpu.VMEM((BANK * TILES, CHANNELS * DEPTH), BF16),
-    pltpu.VMEM((BANK * TILES, CHANNELS * DEPTH), BF16),
+    pltpu.VMEM((2 * BANK * TILES, CHANNELS * DEPTH), BF16),
 ]
-BACKWARD = [pltpu.VMEM((CHANNELS * HALF, BANK * DEPTH), BF16)] * 2
+BACKWARD = [pltpu.VMEM((2 * CHANNELS * HALF, BANK * DEPTH), BF16)]
 
 
 def call(kernel, out_shape, scratch, *operands):
@@ -242,6 +237,7 @@
     other = lax.dynamic_slice_in_dim(arrived[:, : 2 * PAIRS], (1 - core) * SPAN, SPAN, 2)
 
     code = tile_index.reshape(PAIRS, band) + TILES * tile_offset.reshape(PAIRS, band)
+    other, code = lax.optimization_barrier((other, code))
     other = lax.ppermute(other, BOTH, partners(CORE))
     code = jnp.concatenate([code, lax.ppermute(code, BOTH, partners(CORE))], axis=0)
     index = (code & (TILES - 1)) ^ (view & 3)

time: 62.6 us -> 61.5 us (0.982)
    all_to_all x1, waiting for transfers between devices: 6.63 us -> 5.49 us  [on_device(): lax.all_to_all(stack, BOTH, 0, 0, tiled=True, axis_index_groups=plane_gro...]
  transfers between devices with their start and end apart: 9 -> 9, of which waited for: 3 -> 4; matrix products, arithmetic and copies ran while one was open for 1% -> 1% of each run, Pallas kernels for 6% -> 6%
where the time goes in v4:
time: 61.5 us; the launch traced here: 61.2 us
  blocking collectives  25.4 us (41%)
  starting transfers between devices  19.2 us (31%)
  waiting for transfers between devices  7.54 us (12%)
  Pallas kernels  5.11 us (8%)
  local copies, waits for them, and re-layouts  3.46 us (6%)
    all_to_all x1, blocking collectives, on_device(): lax.all_to_all(grads, BOTH, 0, 0, tiled=True, axis_index_groups=plane_gro...  13.4 us
    all_to_all x1, blocking collectives, on_device(): lax.all_to_all(blocks, BOTH, 0, 0, tiled=True, axis_index_groups=line_gro...  12.1 us
    all_to_all x1, starting transfers between devices, on_device(): lax.all_to_all(stack, BOTH, 0, 0, tiled=True, axis_index_groups=plane_gro...  7.48 us
    ppermute x1, starting transfers between devices, on_device(): theirs = lax.ppermute(mine, BOTH, partners(FAR))  6.39 us
    all_to_all x1, waiting for transfers between devices, on_device(): lax.all_to_all(stack, BOTH, 0, 0, tiled=True, axis_index_groups=plane_gro...  5.49 us
    ppermute x3, starting transfers between devices, on_device(): lax.ppermute(messages[shift], BOTH, partners(shift))  4.47 us
    pallas_call x4, Pallas kernels, call(): pl.pallas_call(kernel, out_shape=out_shape, in_specs=[vmem] * len(operand...  4.33 us
    unnamed x15, local copies, waits for them, and re-layouts  1.9 us
  transfers between devices with their start and end apart: 9, of which 4 were waited for; matrix products, arithmetic and copies ran while one was open for 1% of the time, Pallas kernels for 6%

profile of v4, /device:TPU:2, one launch (start us, length us, event | category | flops | bytes accessed | tf_op | source)
XLA Modules:
  0.0 61.2 jit_solution(3776584370659275810)
XLA Ops:
  0.0 0.7 %copy-done = bf16[1,3,16,256]{3,2,1,0:T(8,128)(2,1)S(1)} copy-done((bf16[1,3,16,256]{3,2,1,0:T(8,128)(2,1)S(1)}, bf16[1,3,16,256]{3,2,1,0:T(8,128)(2,1)}, u32[]{:S(2)}) %copy-start) | copy-done | bytes 24600
  0.8 6.4 %collective-permute-start.4 = (bf16[12,256]{1,0:T(8,128)(2,1)S(1)}, bf16[12,256]{1,0:T(8,128)(2,1)S(1)}, u32[]{:S(2)}, u32[]{:S(2)}) collective-permute-start(bf16[12,256]{1,0:T(8,128)(2,1)S(1)} %reshape.29.mine_ref), channel_id=1, source_target_pairs={{0,10},{1,11},{2,8},{3,9},{4,14},{5,15},{6,12},{7,13},{8,2},{9,3},... | collective-permute-start | bytes 18440 | tf_op jit(solution)/shard_map/ppermute | solution.py:208
  7.2 1.1 %copy-done.2 = s32[4,2,16,1536]{3,2,1,0:T(8,128)S(1)} copy-done((s32[4,2,16,1536]{3,2,1,0:T(8,128)S(1)}, s32[4,2,16,1536]{3,2,1,0:T(8,128)}, u32[]{:S(2)}) %copy-start.2) | copy-done | bytes 786456
  8.3 0.8 %shard_map.73 = (bf16[112,512]{1,0:T(8,128)(2,1)S(1)}, bf16[112,512]{1,0:T(8,128)(2,1)S(1)}, bf16[112,512]{1,0:T(8,128)(2,1)S(1)}, bf16[112,512]{1,0:T(8,128)(2,1)S(1)}) custom-call(s32[4,2,16,1536]{3,2,1,0:T(8,128)S(1)} %copy-done.2, f32[2,3]{1,0:T(2,128)S(1)} %copy-done.3, f32[2]{0:T(128)S(1)} %copy-done.4), custom_call_target="tpu_custom_call" | custom-call | tf_op jit(solution)/shard_map/pallas_call | solution.py:212
  9.1 2.0 %collective-permute-start.2 = (bf16[112,512]{1,0:T(8,128)(2,1)S(1)}, bf16[112,512]{1,0:T(8,128)(2,1)S(1)}, u32[]{:S(2)}, u32[]{:S(2)}) collective-permute-start(bf16[112,512]{1,0:T(8,128)(2,1)S(1)} %get-tuple-element.18), channel_id=1, source_target_pairs={{0,3},{1,2},{2,1},{3,0},{4,7},{5,6},{6,5},{7,4},{8,11},{9,10},{10,... | collective-permute-start | bytes 344072 | tf_op jit(solution)/shard_map/ppermute | solution.py:234
  11.1 0.6 collective-permute-start.1
  11.7 1.9 %collective-permute-start = (bf16[112,512]{1,0:T(8,128)(2,1)S(1)}, bf16[112,512]{1,0:T(8,128)(2,1)S(1)}, u32[]{:S(2)}, u32[]{:S(2)}) collective-permute-start(bf16[112,512]{1,0:T(8,128)(2,1)S(1)} %get-tuple-element.16), channel_id=1, source_target_pairs={{0,1},{1,0},{2,3},{3,2},{4,5},{5,4},{6,7},{7,6},{8,9},{9,8},{10,11... | collective-permute-start | bytes 344072 | tf_op jit(solution)/shard_map/ppermute | solution.py:234
  13.6 0.1 collective-permute-start.5
  13.8 1.1 %collective-permute-done.5 = bf16[2,6,256]{2,1,0:T(8,128)(2,1)S(1)} collective-permute-done((bf16[2,6,256]{2,1,0:T(8,128)(2,1)S(1)}, bf16[2,6,256]{2,1,0:T(8,128)(2,1)S(1)}, u32[]{:S(2)}, u32[]{:S(2)}) %collective-permute-start.5) | collective-permute-done | bytes 6176 | tf_op jit(solution)/shard_map/ppermute | solution.py:229
  14.9 0.7 %broadcast_in_dim.13 = bf16[16,24,256]{2,1,0:T(8,128)(2,1)} broadcast(bf16[24,256]{1,0:T(8,128)(2,1)S(1)} %broadcast_in_dim.12), dimensions={1,2} | broadcast | bytes 208896 | tf_op jit(solution)/shard_map/broadcast_in_dim | solution.py:231
  15.6 7.5 %all-to-all-start = ((bf16[16,24,256]{2,1,0:T(8,128)(2,1)}), bf16[16,24,256]{2,1,0:T(8,128)(2,1)S(1)}, u32[]{:S(2)}, u32[]{:S(2)}) async-start(bf16[16,24,256]{2,1,0:T(8,128)(2,1)} %broadcast_in_dim.13), calls=%async_computation | async-start | bytes 393216 | tf_op jit(solution)/shard_map/all_to_all | solution.py:232
  23.2 0.1 collective-permute-start.3
  23.4 0.6 collective-permute-start.6
  24.0 0.6 collective-permute-done.3
  24.6 5.5 %all-to-all-done.volume_ref = bf16[16,24,256]{2,1,0:T(8,128)(2,1)S(1)} async-done(((bf16[16,24,256]{2,1,0:T(8,128)(2,1)}), bf16[16,24,256]{2,1,0:T(8,128)(2,1)S(1)}, u32[]{:S(2)}, u32[]{:S(2)}) %all-to-all-start) | async-done | bytes 196640 | tf_op jit(solution)/shard_map/all_to_all | solution.py:232
  30.1 1.8 %shard_map.75 = (f32[64,128]{1,0:T(8,128)S(1)}, f32[96,768]{1,0:T(8,128)S(1)}) custom-call(s32[96,56]{1,0:T(8,128)S(1)} %and_or_fusion.code_ref, bf16[16,24,256]{2,1,0:T(8,128)(2,1)S(1)} %all-to-all-done.volume_ref, bf16[16,256,128]{2,1,0:T(8,128)(2,1)S(1)} %copy-done.1), custom_call_target="tpu_custom_call" | custom-call | tf_op jit(solution)/shard_map/pallas_call | solution.py:187
  31.9 0.4 shard_map.76.rounded_ref
  32.4 0.1 collective-permute-start.7
  32.5 1.0 %shard_map.77.total_ref = f32[192,256]{1,0:T(8,128)S(1)} custom-call(bf16[96,768]{1,0:T(8,128)(2,1)S(1)} %shard_map.76.rounded_ref, f32[64,128]{1,0:T(8,128)S(1)} %get-tuple-element.24.chosen_ref, bf16[16,256,128]{2,1,0:T(8,128)(2,1)S(1)} %copy-done.1), custom_call_target="tpu_custom_call" | custom-call | tf_op jit(solution)/shard_map/pallas_call | solution.py:187
  33.4 0.4 collective-permute-done.7.rounded_ref
  33.8 1.1 %shard_map.78 = f32[16,24,256]{2,1,0:T(8,128)S(1)} custom-call(bf16[96,768]{1,0:T(8,128)(2,1)S(1)} %collective-permute-done.7.rounded_ref, f32[64,128]{1,0:T(8,128)S(1)} %get-tuple-element.24.chosen_ref, bf16[16,256,128]{2,1,0:T(8,128)(2,1)S(1)} %copy-done.1, f32[192,256]{1,0:T(8,128)S(1)} %shard_map.77.total_ref), custom_call_target="tpu_custom_call" | custom-call | tf_op jit(solution)/shard_map/pallas_call | solution.py:187
  34.9 13.4 %all_to_all.15 = f32[16,24,256]{2,1,0:T(8,128)S(1)} all-to-all(f32[16,24,256]{2,1,0:T(8,128)S(1)} %shard_map.78), channel_id=1, replica_groups={{0,16,32,48,64,80,96,112,128,144,160,176,192,208,224,240},{1,17,33,49,6..., dimensions={0} | all-to-all | bytes 786432 | tf_op jit(solution)/shard_map/all_to_all | solution.py:271
  48.4 12.1 %all_to_all.16 = f32[8,12,256]{2,1,0:T(8,128)S(1)} all-to-all(f32[8,12,256]{2,1,0:T(8,128)S(1)} %bitcast.12), channel_id=1, replica_groups={{0,1,2,3,8,9,10,11},{4,5,6,7,12,13,14,15},{16,17,18,19,24,25,26,27},{20..., dimensions={0} | all-to-all | bytes 196608 | tf_op jit(solution)/shard_map/all_to_all | solution.py:275
  60.5 0.7 %reshape.32 = f32[1,3,16,256]{3,2,1,0:T(8,128)} reshape(f32[3,4,2,2,256]{4,3,2,1,0:T(2,128)S(1)} %copy.24) | data formatting | bytes 98304 | tf_op jit(solution)/shard_map/reshape | solution.py:278
  (41 shorter events, 0.4 us)
Async XLA Ops:
  0.0 0.7 %copy-start = (bf16[1,3,16,256]{3,2,1,0:T(8,128)(2,1)S(1)}, bf16[1,3,16,256]{3,2,1,0:T(8,128)(2,1)}, u32[]{:S(2)}) copy-start(bf16[1,3,16,256]{3,2,1,0:T(8,128)(2,1)} %param.7) | copy-start | bytes 73732
  0.8 6.4 %copy-start.3 = (f32[2,3]{1,0:T(2,128)S(1)}, f32[2,3]{1,0:T(2,128)}, u32[]{:S(2)}) copy-start(f32[2,3]{1,0:T(2,128)} %attenuation_ref.1) | copy-start | bytes 76
  0.8 6.4 %copy-start.4 = (f32[2]{0:T(128)S(1)}, f32[2]{0:T(128)}, u32[]{:S(2)}) copy-start(f32[2]{0:T(128)} %flux_ref.1) | copy-start | bytes 28
  0.8 12.8 %collective-permute-start.4 = (bf16[12,256]{1,0:T(8,128)(2,1)S(1)}, bf16[12,256]{1,0:T(8,128)(2,1)S(1)}, u32[]{:S(2)}, u32[]{:S(2)}) collective-permute-start(bf16[12,256]{1,0:T(8,128)(2,1)S(1)} %reshape.29.mine_ref), channel_id=1, source_target_pairs={{0,10},{1,11},{2,8},{3,9},{4,14},{5,15},{6,12},{7,13},{8,2},{9,3},... | collective-permute-start | bytes 18440 | tf_op jit(solution)/shard_map/ppermute | solution.py:208
  7.2 1.1 %copy-start.2 = (s32[4,2,16,1536]{3,2,1,0:T(8,128)S(1)}, s32[4,2,16,1536]{3,2,1,0:T(8,128)}, u32[]{:S(2)}) copy-start(s32[4,2,16,1536]{3,2,1,0:T(8,128)} %counts_ref.1) | copy-start | bytes 2359300
  8.3 5.4 %copy-start.5 = (s32[4,12,56]{2,0,1:T(4,128)S(1)}, s32[4,12,56]{2,0,1:T(4,128)}, u32[]{:S(2)}) copy-start(s32[4,12,56]{2,0,1:T(4,128)} %param.9) | copy-start | bytes 32260
  8.3 5.4 %copy-start.6 = (s32[4,12,56]{2,0,1:T(4,128)S(1)}, s32[4,12,56]{2,0,1:T(4,128)}, u32[]{:S(2)}) copy-start(s32[4,12,56]{2,0,1:T(4,128)} %param.10) | copy-start | bytes 32260
  9.1 14.0 %collective-permute-start.2 = (bf16[112,512]{1,0:T(8,128)(2,1)S(1)}, bf16[112,512]{1,0:T(8,128)(2,1)S(1)}, u32[]{:S(2)}, u32[]{:S(2)}) collective-permute-start(bf16[112,512]{1,0:T(8,128)(2,1)S(1)} %get-tuple-element.18), channel_id=1, source_target_pairs={{0,3},{1,2},{2,1},{3,0},{4,7},{5,6},{6,5},{7,4},{8,11},{9,10},{10,... | collective-permute-start | bytes 344072 | tf_op jit(solution)/shard_map/ppermute | solution.py:234
  11.1 12.0 %collective-permute-start.1 = (bf16[112,512]{1,0:T(8,128)(2,1)S(1)}, bf16[112,512]{1,0:T(8,128)(2,1)S(1)}, u32[]{:S(2)}, u32[]{:S(2)}) collective-permute-start(bf16[112,512]{1,0:T(8,128)(2,1)S(1)} %get-tuple-element.17), channel_id=1, source_target_pairs={{0,2},{1,3},{2,0},{3,1},{4,6},{5,7},{6,4},{7,5},{8,10},{9,11},{10,... | collective-permute-start | bytes 344072 | tf_op jit(solution)/shard_map/ppermute | solution.py:234
  11.7 11.4 %collective-permute-start = (bf16[112,512]{1,0:T(8,128)(2,1)S(1)}, bf16[112,512]{1,0:T(8,128)(2,1)S(1)}, u32[]{:S(2)}, u32[]{:S(2)}) collective-permute-start(bf16[112,512]{1,0:T(8,128)(2,1)S(1)} %get-tuple-element.16), channel_id=1, source_target_pairs={{0,1},{1,0},{2,3},{3,2},{4,5},{5,4},{6,7},{7,6},{8,9},{9,8},{10,11... | collective-permute-start | bytes 344072 | tf_op jit(solution)/shard_map/ppermute | solution.py:234
  13.6 1.3 %collective-permute-start.5 = (bf16[2,6,256]{2,1,0:T(8,128)(2,1)S(1)}, bf16[2,6,256]{2,1,0:T(8,128)(2,1)S(1)}, u32[]{:S(2)}, u32[]{:S(2)}) collective-permute-start(bf16[2,6,256]{2,1,0:T(8,128)(2,1)S(1)} %get-tuple-element.21), channel_id=1, source_target_pairs={{0,4},{1,5},{2,6},{3,7},{4,0},{5,1},{6,2},{7,3},{8,12},{9,13},{10,... | collective-permute-start | bytes 18440 | tf_op jit(solution)/shard_map/ppermute | solution.py:229
  15.6 14.5 %all-to-all-start = ((bf16[16,24,256]{2,1,0:T(8,128)(2,1)}), bf16[16,24,256]{2,1,0:T(8,128)(2,1)S(1)}, u32[]{:S(2)}, u32[]{:S(2)}) async-start(bf16[16,24,256]{2,1,0:T(8,128)(2,1)} %broadcast_in_dim.13), calls=%async_computation | async-start | bytes 393216 | tf_op jit(solution)/shard_map/all_to_all | solution.py:232
  23.2 6.9 %copy-start.1 = (bf16[16,256,128]{2,1,0:T(8,128)(2,1)S(1)}, bf16[16,256,128]{2,1,0:T(8,128)(2,1)}, u32[]{:S(2)}) copy-start(bf16[16,256,128]{2,1,0:T(8,128)(2,1)} %basis_ref.5) | copy-start | bytes 3145732
  23.2 1.3 %collective-permute-start.3 = (s32[48,56]{1,0:T(8,128)S(1)}, s32[48,56]{1,0:T(8,128)S(1)}, u32[]{:S(2)}, u32[]{:S(2)}) collective-permute-start(s32[48,56]{1,0:T(8,128)S(1)} %add.26), channel_id=1, source_target_pairs={{0,4},{1,5},{2,6},{3,7},{4,0},{5,1},{6,2},{7,3},{8,12},{9,13},{10,... | collective-permute-start | bytes 32264 | tf_op jit(solution)/shard_map/ppermute | solution.py:242
  23.4 8.5 %collective-permute-start.6 = (bf16[4,96,256]{2,1,0:T(8,128)(2,1)S(1)}, bf16[4,96,256]{2,1,0:T(8,128)(2,1)S(1)}, u32[]{:S(2)}, u32[]{:S(2)}) collective-permute-start(bf16[4,96,256]{2,1,0:T(8,128)(2,1)S(1)} %constant_dynamic-slice_fusion.2), channel_id=1, source_target_pairs={{0,4},{1,5},{2,6},{3,7},{4,0},{5,1},{6,2},{7,3},{8,12},{9,13},{10,... | collective-permute-start | bytes 589832 | tf_op jit(solution)/shard_map/ppermute | solution.py:241
  32.4 1.5 %collective-permute-start.7 = (bf16[96,768]{1,0:T(8,128)(2,1)S(1)}, bf16[96,768]{1,0:T(8,128)(2,1)S(1)}, u32[]{:S(2)}, u32[]{:S(2)}) collective-permute-start(bf16[96,768]{1,0:T(8,128)(2,1)S(1)} %shard_map.76.rounded_ref), channel_id=1, source_target_pairs={{0,4},{1,5},{2,6},{3,7},{4,0},{5,1},{6,2},{7,3},{8,12},{9,13},{10,... | collective-permute-start | bytes 442376 | tf_op jit(solution)/shard_map/ppermute | solution.py:257

commit v5 on v4

--- a/solution.py
+++ b/solution.py
@@ -1,3 +1,4 @@
+import functools
 import math
 
 import jax
@@ -28,6 +29,7 @@
 DEPTH = 128
 SPAN = 2 * DEPTH
 BLOCK = 2 * CHANNELS
+ROWS = 32
 
 
 def partners(mask):
@@ -98,7 +100,9 @@
         send_ref[far] = jnp.where(first, *parts[::-1]).astype(BF16)
 
 
-def forward_kernel(code_ref, volume_ref, basis_ref, chosen_ref, lines_ref, square_ref, rows_ref, parts_ref):
+def forward_kernel(
+    code_ref, volume_ref, basis_ref, mine_ref, theirs_ref, chosen_ref, rounded_ref, square_ref, rows_ref, parts_ref
+):
     rows_ref[...] = volume_ref[...].astype(F32)
     volume = [rows_ref[:, near * CHANNELS + c, :].astype(BF16) for c in range(CHANNELS) for near in range(4)]
     volume = jnp.concatenate(volume, axis=0)
@@ -116,11 +120,9 @@
     part = (lax.broadcasted_iota(jnp.int32, (2 * PAIRS, 128), 1) // TILES).astype(F32)
     turned = jnp.concatenate([chosen, chosen], axis=0).T[: 2 * PAIRS] - part
     picks = [(turned == 2 * j).astype(F32).astype(BF16) for j in range(BANK // 2)]
-    lines_ref[...] = jnp.dot(jnp.concatenate(picks * 2, axis=1), parts_ref[...], preferred_element_type=F32)
-
-
-def residual_kernel(lines_ref, mine_ref, theirs_ref, rounded_ref):
-    line = [lines_ref[:, m * SPAN : (m + 1) * SPAN] for m in range(3)]
+    lines = jnp.dot(jnp.concatenate(picks * 2, axis=1), parts_ref[...], preferred_element_type=F32)
+
+    line = [lines[:, m * SPAN : (m + 1) * SPAN] for m in range(3)]
     grads = [jnp.zeros((2 * PAIRS, SPAN), F32) for m in range(3)]
     for source in range(QUARTERS):
         figures = mine_ref[source, 2 * PAIRS :, :].astype(F32)
@@ -160,18 +162,42 @@
     total_ref[...] = back_project(rounded_ref[...], chosen_ref, basis_ref, parts_ref)
 
 
-def other_kernel(rounded_ref, chosen_ref, basis_ref, total_ref, grad_ref, parts_ref):
+def other_kernel(rounded_ref, chosen_ref, basis_ref, total_ref, grad_ref, parts_ref, rows_ref):
     rounded = jnp.concatenate([rounded_ref[PAIRS:], rounded_ref[:PAIRS]], axis=0)
     other = back_project(rounded, chosen_ref, basis_ref, parts_ref)
     own = total_ref[...]
     view = lax.axis_index("view")
     halves = jnp.where(view & 1 == 0, own, other), jnp.where(view & 1 == 0, other, own)
+    lanes = lax.broadcasted_iota(jnp.int32, (SPOTS, WIDTH), 1)
+    powers = jnp.zeros((SPOTS, WIDTH), F32)
     for core in range(2):
         for c in range(CHANNELS):
             pair = halves[core][c * HALF : (c + 1) * HALF]
-            first, second = pair[:SPOTS], pair[SPOTS:]
-            grad_ref[:, core * CHANNELS + c, :] = jnp.where(view & 2 == 0, first, second)
-            grad_ref[:, BLOCK + core * CHANNELS + c, :] = jnp.where(view & 2 == 0, second, first)
+            largest = jnp.max(jnp.abs(pair), axis=1, keepdims=True)
+            power = jnp.ceil(jnp.log2(jnp.maximum(largest, 1e-30)) - 14.9)
+            pair = jnp.floor(pair * jnp.exp2(-power) + 0.5)
+            power = jnp.broadcast_to(power, (HALF, WIDTH))
+            for far in range(2):
+                row = far * BLOCK + core * CHANNELS + c
+                rows_ref[:, row, :] = jnp.where(view & 2 == 2 * far, pair[:SPOTS], pair[SPOTS:])
+                powers = jnp.where(lanes == row, jnp.where(view & 2 == 2 * far, power[:SPOTS], power[SPOTS:]), powers)
+    for row in range(2 * BLOCK, ROWS):
+        rows_ref[:, row, :] = powers
+    grad_ref[...] = rows_ref[...].astype(jnp.int32).astype(jnp.int16)
+
+
+def sum_kernel(scale, parts_ref, blocks_ref):
+    total = jnp.zeros((2 * BLOCK, WIDTH), F32)
+    shape = (2 * BLOCK, WIDTH)
+    own = lax.broadcasted_iota(jnp.int32, shape, 0) == lax.broadcasted_iota(jnp.int32, shape, 1)
+    for spot in range(SPOTS):
+        part = parts_ref[spot].astype(jnp.int32).astype(F32)
+        powers = jnp.broadcast_to(part[2 * BLOCK : 2 * BLOCK + 1], shape)
+        power = jnp.sum(jnp.where(own, powers, 0.0), axis=1, keepdims=True)
+        total += part[: 2 * BLOCK] * jnp.exp2(power)
+    total = total * scale
+    for place in range(2 * QUARTERS):
+        blocks_ref[place] = total[:BLOCK] if place < QUARTERS else total[BLOCK:]
 
 
 FORWARD = [
@@ -231,7 +257,7 @@
     stack = jnp.broadcast_to(stack.reshape(1, 2 * BLOCK, WIDTH), (SPOTS, 2 * BLOCK, WIDTH))
     tiles = lax.all_to_all(stack, BOTH, 0, 0, tiled=True, axis_index_groups=plane_groups)
 
-    arrived = [lax.ppermute(messages[shift], BOTH, partners(shift)) if shift else messages[0] for shift in range(QUARTERS)]
+    arrived = [lax.ppermute(messages[shift], BOTH, partners(shift)) for shift in (3, 2, 1)] + [messages[0]]
     arrived = jnp.stack(arrived)
     keep = lax.dynamic_slice_in_dim(arrived, core * SPAN, SPAN, 2)
     other = lax.dynamic_slice_in_dim(arrived[:, : 2 * PAIRS], (1 - core) * SPAN, SPAN, 2)
@@ -245,23 +271,24 @@
     code = index | (code & -TILES)
 
     wide = CHANNELS * DEPTH
-    chosen, lines = call(
+    chosen, rounded = call(
         forward_kernel,
-        [jax.ShapeDtypeStruct((TILES, 128), F32), jax.ShapeDtypeStruct((2 * PAIRS, wide), F32)],
+        [jax.ShapeDtypeStruct((TILES, 128), F32), jax.ShapeDtypeStruct((2 * PAIRS, wide), BF16)],
         FORWARD,
         code,
         tiles,
         basis,
-    )
-    rounded = call(residual_kernel, jax.ShapeDtypeStruct((2 * PAIRS, wide), BF16), [], lines, keep, other)
+        keep,
+        other,
+    )
     swapped = lax.ppermute(rounded, BOTH, partners(CORE))
     total = call(
         own_kernel, jax.ShapeDtypeStruct((CHANNELS * HALF, WIDTH), F32), BACKWARD, rounded, chosen, basis
     )
     grads = call(
         other_kernel,
-        jax.ShapeDtypeStruct((SPOTS, 2 * BLOCK, WIDTH), F32),
-        BACKWARD,
+        jax.ShapeDtypeStruct((SPOTS, ROWS, WIDTH), jnp.int16),
+        BACKWARD + [pltpu.VMEM((SPOTS, ROWS, WIDTH), F32)],
         swapped,
         chosen,
         basis,
@@ -270,8 +297,13 @@
 
     parts = lax.all_to_all(grads, BOTH, 0, 0, tiled=True, axis_index_groups=plane_groups)
     scale = 1.0 / (8.0 * math.sqrt(views * lax.axis_size("view")))
-    total = (jnp.sum(parts, axis=0) * scale).reshape(2, 1, BLOCK, WIDTH)
-    blocks = jnp.broadcast_to(total, (2, QUARTERS, BLOCK, WIDTH)).reshape(2 * QUARTERS, BLOCK, WIDTH)
+    blocks = pl.pallas_call(
+        functools.partial(sum_kernel, scale),
+        out_shape=jax.ShapeDtypeStruct((2 * QUARTERS, BLOCK, WIDTH), F32),
+        in_specs=[vmem],
+        out_specs=vmem,
+        compiler_params=pltpu.CompilerParams(vmem_limit_bytes=8 * 2**20),
+    )(parts)
     blocks = lax.all_to_all(blocks, BOTH, 0, 0, tiled=True, axis_index_groups=line_groups)
     quarters = blocks[:4] + jnp.concatenate([blocks[6:], blocks[4:6]], axis=0)
     quarters = quarters.reshape(QUARTERS, 2, 3, 2, WIDTH).transpose(2, 0, 1, 3, 4)

time: 61.5 us -> 60.3 us (0.980)
  blocking collectives: 25.4 us -> 24 us
    all_to_all x1, blocking collectives: 13.4 us -> 12 us  [on_device(): lax.all_to_all(grads, BOTH, 0, 0, tiled=True, axis_index_groups=plane_gro...]
    pallas_call x4 -> x3, Pallas kernels: 4.33 us -> 4.51 us  [call(): pl.pallas_call(kernel, out_shape=out_shape, in_specs=[vmem] * len(operand...]
  transfers between devices with their start and end apart: 9 -> 9, of which waited for: 4 -> 4; matrix products, arithmetic and copies ran while one was open for 1% -> 1% of each run, Pallas kernels for 6% -> 3%
where the time goes in v5:
time: 60.3 us; the launch traced here: 60 us
  blocking collectives  24 us (40%)
  starting transfers between devices  19.2 us (32%)
  waiting for transfers between devices  7.54 us (13%)
  Pallas kernels  5.43 us (9%)
  local copies, waits for them, and re-layouts  3.43 us (6%)
    all_to_all x1, blocking collectives, on_device(): lax.all_to_all(blocks, BOTH, 0, 0, tiled=True, axis_index_groups=line_gro...  12.1 us
    all_to_all x1, blocking collectives, on_device(): lax.all_to_all(grads, BOTH, 0, 0, tiled=True, axis_index_groups=plane_gro...  12 us
    all_to_all x1, starting transfers between devices, on_device(): lax.all_to_all(stack, BOTH, 0, 0, tiled=True, axis_index_groups=plane_gro...  7.48 us
    ppermute x1, starting transfers between devices, on_device(): theirs = lax.ppermute(mine, BOTH, partners(FAR))  6.39 us
    all_to_all x1, waiting for transfers between devices, on_device(): lax.all_to_all(stack, BOTH, 0, 0, tiled=True, axis_index_groups=plane_gro...  5.49 us
    pallas_call x3, Pallas kernels, call(): pl.pallas_call(kernel, out_shape=out_shape, in_specs=[vmem] * len(operand...  4.51 us
    ppermute x3, starting transfers between devices, on_device(): lax.ppermute(messages[shift], BOTH, partners(shift))  4.47 us
    unnamed x15, local copies, waits for them, and re-layouts  1.9 us
  transfers between devices with their start and end apart: 9, of which 4 were waited for; matrix products, arithmetic and copies ran while one was open for 1% of the time, Pallas kernels for 3%

profile of v5, /device:TPU:2, one launch (start us, length us, event | category | flops | bytes accessed | tf_op | source)
XLA Modules:
  0.0 60.0 jit_solution(18136208351182297006)
XLA Ops:
  0.0 0.7 %copy-done = bf16[1,3,16,256]{3,2,1,0:T(8,128)(2,1)S(1)} copy-done((bf16[1,3,16,256]{3,2,1,0:T(8,128)(2,1)S(1)}, bf16[1,3,16,256]{3,2,1,0:T(8,128)(2,1)}, u32[]{:S(2)}) %copy-start) | copy-done | bytes 24600
  0.8 6.4 %collective-permute-start.4 = (bf16[12,256]{1,0:T(8,128)(2,1)S(1)}, bf16[12,256]{1,0:T(8,128)(2,1)S(1)}, u32[]{:S(2)}, u32[]{:S(2)}) collective-permute-start(bf16[12,256]{1,0:T(8,128)(2,1)S(1)} %reshape.18.mine_ref), channel_id=1, source_target_pairs={{0,10},{1,11},{2,8},{3,9},{4,14},{5,15},{6,12},{7,13},{8,2},{9,3},... | collective-permute-start | bytes 18440 | tf_op jit(solution)/shard_map/ppermute | solution.py:234
  7.2 1.1 %copy-done.2 = s32[4,2,16,1536]{3,2,1,0:T(8,128)S(1)} copy-done((s32[4,2,16,1536]{3,2,1,0:T(8,128)S(1)}, s32[4,2,16,1536]{3,2,1,0:T(8,128)}, u32[]{:S(2)}) %copy-start.2) | copy-done | bytes 786456
  8.3 0.8 %shard_map.73 = (bf16[112,512]{1,0:T(8,128)(2,1)S(1)}, bf16[112,512]{1,0:T(8,128)(2,1)S(1)}, bf16[112,512]{1,0:T(8,128)(2,1)S(1)}, bf16[112,512]{1,0:T(8,128)(2,1)S(1)}) custom-call(s32[4,2,16,1536]{3,2,1,0:T(8,128)S(1)} %copy-done.2, f32[2,3]{1,0:T(2,128)S(1)} %copy-done.3, f32[2]{0:T(128)S(1)} %copy-done.4), custom_call_target="tpu_custom_call" | custom-call | tf_op jit(solution)/shard_map/pallas_call | solution.py:238
  9.1 1.1 %collective-permute-start.2 = (bf16[112,512]{1,0:T(8,128)(2,1)S(1)}, bf16[112,512]{1,0:T(8,128)(2,1)S(1)}, u32[]{:S(2)}, u32[]{:S(2)}) collective-permute-start(bf16[112,512]{1,0:T(8,128)(2,1)S(1)} %get-tuple-element.17), channel_id=1, source_target_pairs={{0,1},{1,0},{2,3},{3,2},{4,5},{5,4},{6,7},{7,6},{8,9},{9,8},{10,11... | collective-permute-start | bytes 344072 | tf_op jit(solution)/shard_map/ppermute | solution.py:260
  10.2 1.5 %collective-permute-start.1 = (bf16[112,512]{1,0:T(8,128)(2,1)S(1)}, bf16[112,512]{1,0:T(8,128)(2,1)S(1)}, u32[]{:S(2)}, u32[]{:S(2)}) collective-permute-start(bf16[112,512]{1,0:T(8,128)(2,1)S(1)} %get-tuple-element.16), channel_id=1, source_target_pairs={{0,2},{1,3},{2,0},{3,1},{4,6},{5,7},{6,4},{7,5},{8,10},{9,11},{10,... | collective-permute-start | bytes 344072 | tf_op jit(solution)/shard_map/ppermute | solution.py:260
  11.7 1.9 %collective-permute-start = (bf16[112,512]{1,0:T(8,128)(2,1)S(1)}, bf16[112,512]{1,0:T(8,128)(2,1)S(1)}, u32[]{:S(2)}, u32[]{:S(2)}) collective-permute-start(bf16[112,512]{1,0:T(8,128)(2,1)S(1)} %get-tuple-element.15), channel_id=1, source_target_pairs={{0,3},{1,2},{2,1},{3,0},{4,7},{5,6},{6,5},{7,4},{8,11},{9,10},{10,... | collective-permute-start | bytes 344072 | tf_op jit(solution)/shard_map/ppermute | solution.py:260
  13.6 0.1 collective-permute-start.5
  13.8 1.1 %collective-permute-done.5 = bf16[2,6,256]{2,1,0:T(8,128)(2,1)S(1)} collective-permute-done((bf16[2,6,256]{2,1,0:T(8,128)(2,1)S(1)}, bf16[2,6,256]{2,1,0:T(8,128)(2,1)S(1)}, u32[]{:S(2)}, u32[]{:S(2)}) %collective-permute-start.5) | collective-permute-done | bytes 6176 | tf_op jit(solution)/shard_map/ppermute | solution.py:255
  14.9 0.7 %broadcast_in_dim.8 = bf16[16,24,256]{2,1,0:T(8,128)(2,1)} broadcast(bf16[24,256]{1,0:T(8,128)(2,1)S(1)} %broadcast_in_dim.7), dimensions={1,2} | broadcast | bytes 208896 | tf_op jit(solution)/shard_map/broadcast_in_dim | solution.py:257
  15.6 7.5 %all-to-all-start = ((bf16[16,24,256]{2,1,0:T(8,128)(2,1)}), bf16[16,24,256]{2,1,0:T(8,128)(2,1)S(1)}, u32[]{:S(2)}, u32[]{:S(2)}) async-start(bf16[16,24,256]{2,1,0:T(8,128)(2,1)} %broadcast_in_dim.8), calls=%async_computation | async-start | bytes 393216 | tf_op jit(solution)/shard_map/all_to_all | solution.py:258
  23.2 0.1 collective-permute-start.3
  23.4 0.6 collective-permute-start.6
  23.9 0.6 collective-permute-done.3
  24.5 5.5 %all-to-all-done.volume_ref = bf16[16,24,256]{2,1,0:T(8,128)(2,1)S(1)} async-done(((bf16[16,24,256]{2,1,0:T(8,128)(2,1)}), bf16[16,24,256]{2,1,0:T(8,128)(2,1)S(1)}, u32[]{:S(2)}, u32[]{:S(2)}) %all-to-all-start) | async-done | bytes 196640 | tf_op jit(solution)/shard_map/all_to_all | solution.py:258
  30.0 2.2 %shard_map.75 = (f32[64,128]{1,0:T(8,128)S(1)}, bf16[96,768]{1,0:T(8,128)(2,1)S(1)}) custom-call(s32[96,56]{1,0:T(8,128)S(1)} %and_or_fusion.code_ref, bf16[16,24,256]{2,1,0:T(8,128)(2,1)S(1)} %all-to-all-done.volume_ref, bf16[16,256,128]{2,1,0:T(8,128)(2,1)S(1)} %copy-done.1, bf16[4,112,256]{2,1,0:T(8,128)(2,1)S(1)} %constant_dynamic-slice_fusion.mine_ref, ...), custom_call_target="tpu_custom_call" | custom-call | tf_op jit(solution)/shard_map/pallas_call | solution.py:213
  32.3 0.1 collective-permute-start.7
  32.4 1.0 %shard_map.76.total_ref = f32[192,256]{1,0:T(8,128)S(1)} custom-call(bf16[96,768]{1,0:T(8,128)(2,1)S(1)} %get-tuple-element.23.rounded_ref, f32[64,128]{1,0:T(8,128)S(1)} %get-tuple-element.24.chosen_ref, bf16[16,256,128]{2,1,0:T(8,128)(2,1)S(1)} %copy-done.1), custom_call_target="tpu_custom_call" | custom-call | tf_op jit(solution)/shard_map/pallas_call | solution.py:213
  33.3 0.4 collective-permute-done.7.rounded_ref
  33.7 1.3 %shard_map.77 = s16[16,32,256]{2,1,0:T(8,128)(2,1)S(1)} custom-call(bf16[96,768]{1,0:T(8,128)(2,1)S(1)} %collective-permute-done.7.rounded_ref, f32[64,128]{1,0:T(8,128)S(1)} %get-tuple-element.24.chosen_ref, bf16[16,256,128]{2,1,0:T(8,128)(2,1)S(1)} %copy-done.1, f32[192,256]{1,0:T(8,128)S(1)} %shard_map.76.total_ref), custom_call_target="tpu_custom_call" | custom-call | tf_op jit(solution)/shard_map/pallas_call | solution.py:213
  35.1 12.0 %all_to_all.15.parts_ref = s16[16,32,256]{2,1,0:T(8,128)(2,1)S(1)} all-to-all(s16[16,32,256]{2,1,0:T(8,128)(2,1)S(1)} %shard_map.77), channel_id=1, replica_groups={{0,16,32,48,64,80,96,112,128,144,160,176,192,208,224,240},{1,17,33,49,6..., dimensions={0} | all-to-all | bytes 524288 | tf_op jit(solution)/shard_map/all_to_all | solution.py:298
  47.0 0.1 shard_map.78
  47.2 12.1 %all_to_all.16 = f32[8,12,256]{2,1,0:T(8,128)S(1)} all-to-all(f32[8,12,256]{2,1,0:T(8,128)S(1)} %shard_map.78), channel_id=1, replica_groups={{0,1,2,3,8,9,10,11},{4,5,6,7,12,13,14,15},{16,17,18,19,24,25,26,27},{20..., dimensions={0} | all-to-all | bytes 196608 | tf_op jit(solution)/shard_map/all_to_all | solution.py:307
  59.3 0.7 %reshape.20 = f32[1,3,16,256]{3,2,1,0:T(8,128)} reshape(f32[3,4,2,2,256]{4,3,2,1,0:T(2,128)S(1)} %copy.21) | data formatting | bytes 98304 | tf_op jit(solution)/shard_map/reshape | solution.py:310
  (37 shorter events, 0.4 us)
Async XLA Ops:
  0.0 0.7 %copy-start = (bf16[1,3,16,256]{3,2,1,0:T(8,128)(2,1)S(1)}, bf16[1,3,16,256]{3,2,1,0:T(8,128)(2,1)}, u32[]{:S(2)}) copy-start(bf16[1,3,16,256]{3,2,1,0:T(8,128)(2,1)} %param.7) | copy-start | bytes 73732
  0.8 6.4 %copy-start.3 = (f32[2,3]{1,0:T(2,128)S(1)}, f32[2,3]{1,0:T(2,128)}, u32[]{:S(2)}) copy-start(f32[2,3]{1,0:T(2,128)} %attenuation_ref.1) | copy-start | bytes 76
  0.8 6.4 %copy-start.4 = (f32[2]{0:T(128)S(1)}, f32[2]{0:T(128)}, u32[]{:S(2)}) copy-start(f32[2]{0:T(128)} %flux_ref.1) | copy-start | bytes 28
  0.8 12.8 %collective-permute-start.4 = (bf16[12,256]{1,0:T(8,128)(2,1)S(1)}, bf16[12,256]{1,0:T(8,128)(2,1)S(1)}, u32[]{:S(2)}, u32[]{:S(2)}) collective-permute-start(bf16[12,256]{1,0:T(8,128)(2,1)S(1)} %reshape.18.mine_ref), channel_id=1, source_target_pairs={{0,10},{1,11},{2,8},{3,9},{4,14},{5,15},{6,12},{7,13},{8,2},{9,3},... | collective-permute-start | bytes 18440 | tf_op jit(solution)/shard_map/ppermute | solution.py:234
  7.2 1.1 %copy-start.2 = (s32[4,2,16,1536]{3,2,1,0:T(8,128)S(1)}, s32[4,2,16,1536]{3,2,1,0:T(8,128)}, u32[]{:S(2)}) copy-start(s32[4,2,16,1536]{3,2,1,0:T(8,128)} %counts_ref.1) | copy-start | bytes 2359300
  8.3 5.4 %copy-start.5 = (s32[4,12,56]{2,0,1:T(4,128)S(1)}, s32[4,12,56]{2,0,1:T(4,128)}, u32[]{:S(2)}) copy-start(s32[4,12,56]{2,0,1:T(4,128)} %param.9) | copy-start | bytes 32260
  8.3 5.4 %copy-start.6 = (s32[4,12,56]{2,0,1:T(4,128)S(1)}, s32[4,12,56]{2,0,1:T(4,128)}, u32[]{:S(2)}) copy-start(s32[4,12,56]{2,0,1:T(4,128)} %param.10) | copy-start | bytes 32260
  9.1 14.0 %collective-permute-start.2 = (bf16[112,512]{1,0:T(8,128)(2,1)S(1)}, bf16[112,512]{1,0:T(8,128)(2,1)S(1)}, u32[]{:S(2)}, u32[]{:S(2)}) collective-permute-start(bf16[112,512]{1,0:T(8,128)(2,1)S(1)} %get-tuple-element.17), channel_id=1, source_target_pairs={{0,1},{1,0},{2,3},{3,2},{4,5},{5,4},{6,7},{7,6},{8,9},{9,8},{10,11... | collective-permute-start | bytes 344072 | tf_op jit(solution)/shard_map/ppermute | solution.py:260
  10.2 12.9 %collective-permute-start.1 = (bf16[112,512]{1,0:T(8,128)(2,1)S(1)}, bf16[112,512]{1,0:T(8,128)(2,1)S(1)}, u32[]{:S(2)}, u32[]{:S(2)}) collective-permute-start(bf16[112,512]{1,0:T(8,128)(2,1)S(1)} %get-tuple-element.16), channel_id=1, source_target_pairs={{0,2},{1,3},{2,0},{3,1},{4,6},{5,7},{6,4},{7,5},{8,10},{9,11},{10,... | collective-permute-start | bytes 344072 | tf_op jit(solution)/shard_map/ppermute | solution.py:260
  11.7 11.4 %collective-permute-start = (bf16[112,512]{1,0:T(8,128)(2,1)S(1)}, bf16[112,512]{1,0:T(8,128)(2,1)S(1)}, u32[]{:S(2)}, u32[]{:S(2)}) collective-permute-start(bf16[112,512]{1,0:T(8,128)(2,1)S(1)} %get-tuple-element.15), channel_id=1, source_target_pairs={{0,3},{1,2},{2,1},{3,0},{4,7},{5,6},{6,5},{7,4},{8,11},{9,10},{10,... | collective-permute-start | bytes 344072 | tf_op jit(solution)/shard_map/ppermute | solution.py:260
  13.6 1.3 %collective-permute-start.5 = (bf16[2,6,256]{2,1,0:T(8,128)(2,1)S(1)}, bf16[2,6,256]{2,1,0:T(8,128)(2,1)S(1)}, u32[]{:S(2)}, u32[]{:S(2)}) collective-permute-start(bf16[2,6,256]{2,1,0:T(8,128)(2,1)S(1)} %get-tuple-element.21), channel_id=1, source_target_pairs={{0,4},{1,5},{2,6},{3,7},{4,0},{5,1},{6,2},{7,3},{8,12},{9,13},{10,... | collective-permute-start | bytes 18440 | tf_op jit(solution)/shard_map/ppermute | solution.py:255
  15.6 14.5 %all-to-all-start = ((bf16[16,24,256]{2,1,0:T(8,128)(2,1)}), bf16[16,24,256]{2,1,0:T(8,128)(2,1)S(1)}, u32[]{:S(2)}, u32[]{:S(2)}) async-start(bf16[16,24,256]{2,1,0:T(8,128)(2,1)} %broadcast_in_dim.8), calls=%async_computation | async-start | bytes 393216 | tf_op jit(solution)/shard_map/all_to_all | solution.py:258
  23.1 6.9 %copy-start.1 = (bf16[16,256,128]{2,1,0:T(8,128)(2,1)S(1)}, bf16[16,256,128]{2,1,0:T(8,128)(2,1)}, u32[]{:S(2)}) copy-start(bf16[16,256,128]{2,1,0:T(8,128)(2,1)} %basis_ref.5) | copy-start | bytes 3145732
  23.2 1.3 %collective-permute-start.3 = (s32[48,56]{1,0:T(8,128)S(1)}, s32[48,56]{1,0:T(8,128)S(1)}, u32[]{:S(2)}, u32[]{:S(2)}) collective-permute-start(s32[48,56]{1,0:T(8,128)S(1)} %add.26), channel_id=1, source_target_pairs={{0,4},{1,5},{2,6},{3,7},{4,0},{5,1},{6,2},{7,3},{8,12},{9,13},{10,... | collective-permute-start | bytes 32264 | tf_op jit(solution)/shard_map/ppermute | solution.py:268
  23.4 6.7 %collective-permute-start.6 = (bf16[4,96,256]{2,1,0:T(8,128)(2,1)S(1)}, bf16[4,96,256]{2,1,0:T(8,128)(2,1)S(1)}, u32[]{:S(2)}, u32[]{:S(2)}) collective-permute-start(bf16[4,96,256]{2,1,0:T(8,128)(2,1)S(1)} %constant_dynamic-slice_fusion.2), channel_id=1, source_target_pairs={{0,4},{1,5},{2,6},{3,7},{4,0},{5,1},{6,2},{7,3},{8,12},{9,13},{10,... | collective-permute-start | bytes 589832 | tf_op jit(solution)/shard_map/ppermute | solution.py:267
  32.3 1.5 %collective-permute-start.7 = (bf16[96,768]{1,0:T(8,128)(2,1)S(1)}, bf16[96,768]{1,0:T(8,128)(2,1)S(1)}, u32[]{:S(2)}, u32[]{:S(2)}) collective-permute-start(bf16[96,768]{1,0:T(8,128)(2,1)S(1)} %get-tuple-element.23.rounded_ref), channel_id=1, source_target_pairs={{0,4},{1,5},{2,6},{3,7},{4,0},{5,1},{6,2},{7,3},{8,12},{9,13},{10,... | collective-permute-start | bytes 442376 | tf_op jit(solution)/shard_map/ppermute | solution.py:284

commit v6 on v5

--- a/solution.py
+++ b/solution.py
@@ -29,7 +29,7 @@
 DEPTH = 128
 SPAN = 2 * DEPTH
 BLOCK = 2 * CHANNELS
-ROWS = 32
+ROWS = 4 * BLOCK + 8
 
 
 def partners(mask):
@@ -56,6 +56,20 @@
         row = code[step : step + 1, :]
         chosen = jnp.where(labels == (row & (TILES - 1)), row >> 6, chosen)
     return chosen.astype(F32)
+
+
+def prepare_kernel(code_ref, basis_ref, chosen_ref, picks_ref, bank_ref, square_ref):
+    chosen = select(code_ref, square_ref)
+    chosen_ref[...] = chosen
+    part = (lax.broadcasted_iota(jnp.int32, (2 * PAIRS, 128), 1) // TILES).astype(F32)
+    turned = jnp.concatenate([chosen, chosen], axis=0).T[: 2 * PAIRS] - part
+    for j in range(BANK // 2):
+        pick = (turned == 2 * j).astype(F32).astype(BF16)
+        for half in range(2):
+            col = (half * BANK // 2 + j) * 128
+            picks_ref[:, col : col + 128] = pick
+    for p in range(BANK):
+        bank_ref[p * DEPTH : (p + 1) * DEPTH, :] = basis_ref[p].T
 
 
 def message_kernel(counts_ref, attenuation_ref, flux_ref, message0_ref, message1_ref, message2_ref, message3_ref, rows_ref):
@@ -101,7 +115,7 @@
 
 
 def forward_kernel(
-    code_ref, volume_ref, basis_ref, mine_ref, theirs_ref, chosen_ref, rounded_ref, square_ref, rows_ref, parts_ref
+    picks_ref, volume_ref, basis_ref, mine_ref, theirs_ref, rounded_ref, rows_ref, parts_ref
 ):
     rows_ref[...] = volume_ref[...].astype(F32)
     volume = [rows_ref[:, near * CHANNELS + c, :].astype(BF16) for c in range(CHANNELS) for near in range(4)]
@@ -115,12 +129,7 @@
                 for c in range(CHANNELS):
                     piece = value[c * TILES : (c + 1) * TILES, p * DEPTH : (p + 1) * DEPTH]
                     parts_ref[row : row + TILES, c * DEPTH : (c + 1) * DEPTH] = piece
-    chosen = select(code_ref, square_ref)
-    chosen_ref[...] = chosen
-    part = (lax.broadcasted_iota(jnp.int32, (2 * PAIRS, 128), 1) // TILES).astype(F32)
-    turned = jnp.concatenate([chosen, chosen], axis=0).T[: 2 * PAIRS] - part
-    picks = [(turned == 2 * j).astype(F32).astype(BF16) for j in range(BANK // 2)]
-    lines = jnp.dot(jnp.concatenate(picks * 2, axis=1), parts_ref[...], preferred_element_type=F32)
+    lines = jnp.dot(picks_ref[...], parts_ref[...], preferred_element_type=F32)
 
     line = [lines[:, m * SPAN : (m + 1) * SPAN] for m in range(3)]
     grads = [jnp.zeros((2 * PAIRS, SPAN), F32) for m in range(3)]
@@ -139,7 +148,7 @@
         rounded_ref[:, m * SPAN : (m + 1) * SPAN] = grads[m].astype(BF16)
 
 
-def back_project(rounded, chosen_ref, basis_ref, parts_ref):
+def back_project(rounded, chosen_ref, bank_ref, parts_ref):
     own = [chosen_ref[far * 2 * SPOTS : far * 2 * SPOTS + SPOTS, : 2 * PAIRS] for far in range(2)]
     own = jnp.concatenate(own, axis=0)
     for j in range(BANK // 4):
@@ -152,56 +161,56 @@
                     row = (part * CHANNELS + c) * HALF
                     piece = value[p * HALF : (p + 1) * HALF, c * DEPTH : (c + 1) * DEPTH]
                     parts_ref[row : row + HALF, col : col + DEPTH] = piece
-    bank = jnp.concatenate([basis_ref[p] for p in range(BANK)], axis=1)
-    turn = (((1,), (1,)), ((), ()))
-    total = lax.dot_general(parts_ref[...], bank, turn, preferred_element_type=F32)
+    total = jnp.dot(parts_ref[...], bank_ref[...], preferred_element_type=F32)
     return total[: CHANNELS * HALF] + total[CHANNELS * HALF :]
 
 
-def own_kernel(rounded_ref, chosen_ref, basis_ref, total_ref, parts_ref):
-    total_ref[...] = back_project(rounded_ref[...], chosen_ref, basis_ref, parts_ref)
-
-
-def other_kernel(rounded_ref, chosen_ref, basis_ref, total_ref, grad_ref, parts_ref, rows_ref):
+def own_kernel(rounded_ref, chosen_ref, bank_ref, total_ref, parts_ref):
+    total_ref[...] = back_project(rounded_ref[...], chosen_ref, bank_ref, parts_ref)
+
+
+def other_kernel(rounded_ref, chosen_ref, bank_ref, total_ref, grad_ref, parts_ref, rows_ref):
     rounded = jnp.concatenate([rounded_ref[PAIRS:], rounded_ref[:PAIRS]], axis=0)
-    other = back_project(rounded, chosen_ref, basis_ref, parts_ref)
+    other = back_project(rounded, chosen_ref, bank_ref, parts_ref)
     own = total_ref[...]
     view = lax.axis_index("view")
     halves = jnp.where(view & 1 == 0, own, other), jnp.where(view & 1 == 0, other, own)
-    lanes = lax.broadcasted_iota(jnp.int32, (SPOTS, WIDTH), 1)
-    powers = jnp.zeros((SPOTS, WIDTH), F32)
+    lanes = lax.broadcasted_iota(jnp.int32, (SPOTS, 128), 1)
+    powers = jnp.zeros((SPOTS, 128), F32)
     for core in range(2):
         for c in range(CHANNELS):
             pair = halves[core][c * HALF : (c + 1) * HALF]
             largest = jnp.max(jnp.abs(pair), axis=1, keepdims=True)
             power = jnp.ceil(jnp.log2(jnp.maximum(largest, 1e-30)) - 14.9)
             pair = jnp.floor(pair * jnp.exp2(-power) + 0.5)
-            power = jnp.broadcast_to(power, (HALF, WIDTH))
+            power = jnp.broadcast_to(power, (HALF, 128))
             for far in range(2):
                 row = far * BLOCK + core * CHANNELS + c
-                rows_ref[:, row, :] = jnp.where(view & 2 == 2 * far, pair[:SPOTS], pair[SPOTS:])
+                tile = jnp.where(view & 2 == 2 * far, pair[:SPOTS], pair[SPOTS:])
+                rows_ref[:, row, :] = tile[:, :128]
+                rows_ref[:, 2 * BLOCK + row, :] = tile[:, 128:]
                 powers = jnp.where(lanes == row, jnp.where(view & 2 == 2 * far, power[:SPOTS], power[SPOTS:]), powers)
-    for row in range(2 * BLOCK, ROWS):
+    for row in range(4 * BLOCK, ROWS):
         rows_ref[:, row, :] = powers
     grad_ref[...] = rows_ref[...].astype(jnp.int32).astype(jnp.int16)
 
 
 def sum_kernel(scale, parts_ref, blocks_ref):
     total = jnp.zeros((2 * BLOCK, WIDTH), F32)
-    shape = (2 * BLOCK, WIDTH)
+    shape = (2 * BLOCK, 128)
     own = lax.broadcasted_iota(jnp.int32, shape, 0) == lax.broadcasted_iota(jnp.int32, shape, 1)
     for spot in range(SPOTS):
         part = parts_ref[spot].astype(jnp.int32).astype(F32)
-        powers = jnp.broadcast_to(part[2 * BLOCK : 2 * BLOCK + 1], shape)
+        powers = jnp.broadcast_to(part[4 * BLOCK : 4 * BLOCK + 1], shape)
         power = jnp.sum(jnp.where(own, powers, 0.0), axis=1, keepdims=True)
-        total += part[: 2 * BLOCK] * jnp.exp2(power)
+        part = jnp.concatenate([part[: 2 * BLOCK], part[2 * BLOCK : 4 * BLOCK]], axis=1)
+        total += part * jnp.exp2(power)
     total = total * scale
     for place in range(2 * QUARTERS):
         blocks_ref[place] = total[:BLOCK] if place < QUARTERS else total[BLOCK:]
 
 
 FORWARD = [
-    pltpu.VMEM((128, 128), F32),
     pltpu.VMEM((SPOTS, 2 * BLOCK, WIDTH), F32),
     pltpu.VMEM((2 * BANK * TILES, CHANNELS * DEPTH), BF16),
 ]
@@ -271,11 +280,23 @@
     code = index | (code & -TILES)
 
     wide = CHANNELS * DEPTH
-    chosen, rounded = call(
+    chosen, picks, bank = pl.pallas_call(
+        prepare_kernel,
+        out_shape=[
+            jax.ShapeDtypeStruct((TILES, 128), F32),
+            jax.ShapeDtypeStruct((2 * PAIRS, 2 * BANK * TILES), BF16),
+            jax.ShapeDtypeStruct((BANK * DEPTH, WIDTH), BF16),
+        ],
+        in_specs=[vmem] * 2,
+        out_specs=[vmem] * 3,
+        scratch_shapes=[pltpu.VMEM((128, 128), F32)],
+        compiler_params=pltpu.CompilerParams(vmem_limit_bytes=8 * 2**20),
+    )(code, basis)
+    rounded = call(
         forward_kernel,
-        [jax.ShapeDtypeStruct((TILES, 128), F32), jax.ShapeDtypeStruct((2 * PAIRS, wide), BF16)],
+        jax.ShapeDtypeStruct((2 * PAIRS, wide), BF16),
         FORWARD,
-        code,
+        picks,
         tiles,
         basis,
         keep,
@@ -283,15 +304,15 @@
     )
     swapped = lax.ppermute(rounded, BOTH, partners(CORE))
     total = call(
-        own_kernel, jax.ShapeDtypeStruct((CHANNELS * HALF, WIDTH), F32), BACKWARD, rounded, chosen, basis
+        own_kernel, jax.ShapeDtypeStruct((CHANNELS * HALF, WIDTH), F32), BACKWARD, rounded, chosen, bank
     )
     grads = call(
         other_kernel,
-        jax.ShapeDtypeStruct((SPOTS, ROWS, WIDTH), jnp.int16),
-        BACKWARD + [pltpu.VMEM((SPOTS, ROWS, WIDTH), F32)],
+        jax.ShapeDtypeStruct((SPOTS, ROWS, 128), jnp.int16),
+        BACKWARD + [pltpu.VMEM((SPOTS, ROWS, 128), F32)],
         swapped,
         chosen,
-        basis,
+        bank,
         total,
     )
 

time: 60.3 us -> 59.8 us (level)
  transfers between devices with their start and end apart: 9 -> 9, of which waited for: 4 -> 4; matrix products, arithmetic and copies ran while one was open for 1% -> 1% of each run, Pallas kernels for 3% -> 4%
where the time goes in v6:
time: 59.8 us; the launch traced here: 59.5 us
  blocking collectives  23.7 us (40%)
  starting transfers between devices  19.1 us (32%)
  waiting for transfers between devices  7.12 us (12%)
  Pallas kernels  5.74 us (10%)
  local copies, waits for them, and re-layouts  3.43 us (6%)
    all_to_all x1, blocking collectives, on_device(): lax.all_to_all(blocks, BOTH, 0, 0, tiled=True, axis_index_groups=line_gro...  12.1 us
    all_to_all x1, blocking collectives, on_device(): lax.all_to_all(grads, BOTH, 0, 0, tiled=True, axis_index_groups=plane_gro...  11.6 us
    all_to_all x1, starting transfers between devices, on_device(): lax.all_to_all(stack, BOTH, 0, 0, tiled=True, axis_index_groups=plane_gro...  7.48 us
    ppermute x1, starting transfers between devices, on_device(): theirs = lax.ppermute(mine, BOTH, partners(FAR))  6.39 us
    all_to_all x1, waiting for transfers between devices, on_device(): lax.all_to_all(stack, BOTH, 0, 0, tiled=True, axis_index_groups=plane_gro...  4.9 us
    ppermute x3, starting transfers between devices, on_device(): lax.ppermute(messages[shift], BOTH, partners(shift))  4.47 us
    pallas_call x3, Pallas kernels, call(): pl.pallas_call(kernel, out_shape=out_shape, in_specs=[vmem] * len(operand...  4.28 us
    unnamed x15, local copies, waits for them, and re-layouts  1.9 us
  transfers between devices with their start and end apart: 9, of which 4 were waited for; matrix products, arithmetic and copies ran while one was open for 1% of the time, Pallas kernels for 4%

profile of v6, /device:TPU:2, one launch (start us, length us, event | category | flops | bytes accessed | tf_op | source)
XLA Modules:
  0.0 59.5 jit_solution(9367890639903754078)
XLA Ops:
  0.0 0.7 %copy-done = bf16[1,3,16,256]{3,2,1,0:T(8,128)(2,1)S(1)} copy-done((bf16[1,3,16,256]{3,2,1,0:T(8,128)(2,1)S(1)}, bf16[1,3,16,256]{3,2,1,0:T(8,128)(2,1)}, u32[]{:S(2)}) %copy-start) | copy-done | bytes 24600
  0.8 6.4 %collective-permute-start.4 = (bf16[12,256]{1,0:T(8,128)(2,1)S(1)}, bf16[12,256]{1,0:T(8,128)(2,1)S(1)}, u32[]{:S(2)}, u32[]{:S(2)}) collective-permute-start(bf16[12,256]{1,0:T(8,128)(2,1)S(1)} %reshape.18.mine_ref), channel_id=1, source_target_pairs={{0,10},{1,11},{2,8},{3,9},{4,14},{5,15},{6,12},{7,13},{8,2},{9,3},... | collective-permute-start | bytes 18440 | tf_op jit(solution)/shard_map/ppermute | solution.py:243
  7.2 1.1 %copy-done.2 = s32[4,2,16,1536]{3,2,1,0:T(8,128)S(1)} copy-done((s32[4,2,16,1536]{3,2,1,0:T(8,128)S(1)}, s32[4,2,16,1536]{3,2,1,0:T(8,128)}, u32[]{:S(2)}) %copy-start.2) | copy-done | bytes 786456
  8.3 0.8 %shard_map.73 = (bf16[112,512]{1,0:T(8,128)(2,1)S(1)}, bf16[112,512]{1,0:T(8,128)(2,1)S(1)}, bf16[112,512]{1,0:T(8,128)(2,1)S(1)}, bf16[112,512]{1,0:T(8,128)(2,1)S(1)}) custom-call(s32[4,2,16,1536]{3,2,1,0:T(8,128)S(1)} %copy-done.2, f32[2,3]{1,0:T(2,128)S(1)} %copy-done.3, f32[2]{0:T(128)S(1)} %copy-done.4), custom_call_target="tpu_custom_call" | custom-call | tf_op jit(solution)/shard_map/pallas_call | solution.py:247
  9.1 2.0 %collective-permute-start = (bf16[112,512]{1,0:T(8,128)(2,1)S(1)}, bf16[112,512]{1,0:T(8,128)(2,1)S(1)}, u32[]{:S(2)}, u32[]{:S(2)}) collective-permute-start(bf16[112,512]{1,0:T(8,128)(2,1)S(1)} %get-tuple-element.16), channel_id=1, source_target_pairs={{0,3},{1,2},{2,1},{3,0},{4,7},{5,6},{6,5},{7,4},{8,11},{9,10},{10,... | collective-permute-start | bytes 344072 | tf_op jit(solution)/shard_map/ppermute | solution.py:269
  11.1 0.6 collective-permute-start.1
  11.7 1.9 %collective-permute-start.2 = (bf16[112,512]{1,0:T(8,128)(2,1)S(1)}, bf16[112,512]{1,0:T(8,128)(2,1)S(1)}, u32[]{:S(2)}, u32[]{:S(2)}) collective-permute-start(bf16[112,512]{1,0:T(8,128)(2,1)S(1)} %get-tuple-element.18), channel_id=1, source_target_pairs={{0,1},{1,0},{2,3},{3,2},{4,5},{5,4},{6,7},{7,6},{8,9},{9,8},{10,11... | collective-permute-start | bytes 344072 | tf_op jit(solution)/shard_map/ppermute | solution.py:269
  13.6 0.1 collective-permute-start.5
  13.8 1.1 %collective-permute-done.5 = bf16[2,6,256]{2,1,0:T(8,128)(2,1)S(1)} collective-permute-done((bf16[2,6,256]{2,1,0:T(8,128)(2,1)S(1)}, bf16[2,6,256]{2,1,0:T(8,128)(2,1)S(1)}, u32[]{:S(2)}, u32[]{:S(2)}) %collective-permute-start.5) | collective-permute-done | bytes 6176 | tf_op jit(solution)/shard_map/ppermute | solution.py:264
  14.9 0.7 %broadcast_in_dim.8 = bf16[16,24,256]{2,1,0:T(8,128)(2,1)} broadcast(bf16[24,256]{1,0:T(8,128)(2,1)S(1)} %broadcast_in_dim.7), dimensions={1,2} | broadcast | bytes 208896 | tf_op jit(solution)/shard_map/broadcast_in_dim | solution.py:266
  15.6 7.5 %all-to-all-start = ((bf16[16,24,256]{2,1,0:T(8,128)(2,1)}), bf16[16,24,256]{2,1,0:T(8,128)(2,1)S(1)}, u32[]{:S(2)}, u32[]{:S(2)}) async-start(bf16[16,24,256]{2,1,0:T(8,128)(2,1)} %broadcast_in_dim.8), calls=%async_computation | async-start | bytes 393216 | tf_op jit(solution)/shard_map/all_to_all | solution.py:267
  23.3 0.1 collective-permute-start.3
  23.4 0.5 collective-permute-start.6
  23.9 0.7 %collective-permute-done.3 = s32[48,56]{1,0:T(8,128)S(1)} collective-permute-done((s32[48,56]{1,0:T(8,128)S(1)}, s32[48,56]{1,0:T(8,128)S(1)}, u32[]{:S(2)}, u32[]{:S(2)}) %collective-permute-start.3) | collective-permute-done | bytes 10784 | tf_op jit(solution)/shard_map/ppermute | solution.py:277
  24.6 0.5 shard_map.74
  25.1 4.9 %all-to-all-done.volume_ref = bf16[16,24,256]{2,1,0:T(8,128)(2,1)S(1)} async-done(((bf16[16,24,256]{2,1,0:T(8,128)(2,1)}), bf16[16,24,256]{2,1,0:T(8,128)(2,1)S(1)}, u32[]{:S(2)}, u32[]{:S(2)}) %all-to-all-start) | async-done | bytes 196640 | tf_op jit(solution)/shard_map/all_to_all | solution.py:267
  30.0 2.0 %shard_map.76.rounded_ref = bf16[96,768]{1,0:T(8,128)(2,1)S(1)} custom-call(bf16[96,2048]{1,0:T(8,128)(2,1)S(1)} %get-tuple-element.21.picks_ref, bf16[16,24,256]{2,1,0:T(8,128)(2,1)S(1)} %all-to-all-done.volume_ref, bf16[16,256,128]{2,1,0:T(8,128)(2,1)S(1)} %copy-done.1, bf16[4,112,256]{2,1,0:T(8,128)(2,1)S(1)} %constant_dynamic-slice_fusion.mine_ref, ...), custom_call_target="tpu_custom_call" | custom-call | tf_op jit(solution)/shard_map/pallas_call | solution.py:222
  32.1 0.9 %shard_map.77.total_ref = f32[192,256]{1,0:T(8,128)S(1)} custom-call(bf16[96,768]{1,0:T(8,128)(2,1)S(1)} %shard_map.76.rounded_ref, f32[64,128]{1,0:T(8,128)S(1)} %get-tuple-element.25.chosen_ref, bf16[2048,256]{1,0:T(8,128)(2,1)S(1)} %get-tuple-element.26.bank_ref), custom_call_target="tpu_custom_call" | custom-call | tf_op jit(solution)/shard_map/pallas_call | solution.py:222
  33.1 0.4 collective-permute-done.7.rounded_ref
  33.5 1.4 %shard_map.78 = s16[16,56,128]{2,1,0:T(8,128)(2,1)S(1)} custom-call(bf16[96,768]{1,0:T(8,128)(2,1)S(1)} %collective-permute-done.7.rounded_ref, f32[64,128]{1,0:T(8,128)S(1)} %get-tuple-element.25.chosen_ref, bf16[2048,256]{1,0:T(8,128)(2,1)S(1)} %get-tuple-element.26.bank_ref, f32[192,256]{1,0:T(8,128)S(1)} %shard_map.77.total_ref), custom_call_target="tpu_custom_call" | custom-call | tf_op jit(solution)/shard_map/pallas_call | solution.py:222
  34.9 11.6 %all_to_all.15.parts_ref = s16[16,56,128]{2,1,0:T(8,128)(2,1)S(1)} all-to-all(s16[16,56,128]{2,1,0:T(8,128)(2,1)S(1)} %shard_map.78), channel_id=1, replica_groups={{0,16,32,48,64,80,96,112,128,144,160,176,192,208,224,240},{1,17,33,49,6..., dimensions={0} | all-to-all | bytes 458752 | tf_op jit(solution)/shard_map/all_to_all | solution.py:319
  46.5 0.1 shard_map.79
  46.7 12.1 %all_to_all.16 = f32[8,12,256]{2,1,0:T(8,128)S(1)} all-to-all(f32[8,12,256]{2,1,0:T(8,128)S(1)} %shard_map.79), channel_id=1, replica_groups={{0,1,2,3,8,9,10,11},{4,5,6,7,12,13,14,15},{16,17,18,19,24,25,26,27},{20..., dimensions={0} | all-to-all | bytes 196608 | tf_op jit(solution)/shard_map/all_to_all | solution.py:328
  58.8 0.7 %reshape.20 = f32[1,3,16,256]{3,2,1,0:T(8,128)} reshape(f32[3,4,2,2,256]{4,3,2,1,0:T(2,128)S(1)} %copy.21) | data formatting | bytes 98304 | tf_op jit(solution)/shard_map/reshape | solution.py:331
  (38 shorter events, 0.5 us)
Async XLA Ops:
  0.0 0.7 %copy-start = (bf16[1,3,16,256]{3,2,1,0:T(8,128)(2,1)S(1)}, bf16[1,3,16,256]{3,2,1,0:T(8,128)(2,1)}, u32[]{:S(2)}) copy-start(bf16[1,3,16,256]{3,2,1,0:T(8,128)(2,1)} %param.7) | copy-start | bytes 73732
  0.8 6.4 %copy-start.3 = (f32[2,3]{1,0:T(2,128)S(1)}, f32[2,3]{1,0:T(2,128)}, u32[]{:S(2)}) copy-start(f32[2,3]{1,0:T(2,128)} %attenuation_ref.1) | copy-start | bytes 76
  0.8 6.4 %copy-start.4 = (f32[2]{0:T(128)S(1)}, f32[2]{0:T(128)}, u32[]{:S(2)}) copy-start(f32[2]{0:T(128)} %flux_ref.1) | copy-start | bytes 28
  0.8 12.8 %collective-permute-start.4 = (bf16[12,256]{1,0:T(8,128)(2,1)S(1)}, bf16[12,256]{1,0:T(8,128)(2,1)S(1)}, u32[]{:S(2)}, u32[]{:S(2)}) collective-permute-start(bf16[12,256]{1,0:T(8,128)(2,1)S(1)} %reshape.18.mine_ref), channel_id=1, source_target_pairs={{0,10},{1,11},{2,8},{3,9},{4,14},{5,15},{6,12},{7,13},{8,2},{9,3},... | collective-permute-start | bytes 18440 | tf_op jit(solution)/shard_map/ppermute | solution.py:243
  7.2 1.1 %copy-start.2 = (s32[4,2,16,1536]{3,2,1,0:T(8,128)S(1)}, s32[4,2,16,1536]{3,2,1,0:T(8,128)}, u32[]{:S(2)}) copy-start(s32[4,2,16,1536]{3,2,1,0:T(8,128)} %counts_ref.1) | copy-start | bytes 2359300
  8.3 5.4 %copy-start.5 = (s32[4,12,56]{2,0,1:T(4,128)S(1)}, s32[4,12,56]{2,0,1:T(4,128)}, u32[]{:S(2)}) copy-start(s32[4,12,56]{2,0,1:T(4,128)} %param.9) | copy-start | bytes 32260
  8.3 5.4 %copy-start.6 = (s32[4,12,56]{2,0,1:T(4,128)S(1)}, s32[4,12,56]{2,0,1:T(4,128)}, u32[]{:S(2)}) copy-start(s32[4,12,56]{2,0,1:T(4,128)} %param.10) | copy-start | bytes 32260
  9.1 14.0 %collective-permute-start = (bf16[112,512]{1,0:T(8,128)(2,1)S(1)}, bf16[112,512]{1,0:T(8,128)(2,1)S(1)}, u32[]{:S(2)}, u32[]{:S(2)}) collective-permute-start(bf16[112,512]{1,0:T(8,128)(2,1)S(1)} %get-tuple-element.16), channel_id=1, source_target_pairs={{0,3},{1,2},{2,1},{3,0},{4,7},{5,6},{6,5},{7,4},{8,11},{9,10},{10,... | collective-permute-start | bytes 344072 | tf_op jit(solution)/shard_map/ppermute | solution.py:269
  11.1 12.0 %collective-permute-start.1 = (bf16[112,512]{1,0:T(8,128)(2,1)S(1)}, bf16[112,512]{1,0:T(8,128)(2,1)S(1)}, u32[]{:S(2)}, u32[]{:S(2)}) collective-permute-start(bf16[112,512]{1,0:T(8,128)(2,1)S(1)} %get-tuple-element.17), channel_id=1, source_target_pairs={{0,2},{1,3},{2,0},{3,1},{4,6},{5,7},{6,4},{7,5},{8,10},{9,11},{10,... | collective-permute-start | bytes 344072 | tf_op jit(solution)/shard_map/ppermute | solution.py:269
  11.7 11.4 %collective-permute-start.2 = (bf16[112,512]{1,0:T(8,128)(2,1)S(1)}, bf16[112,512]{1,0:T(8,128)(2,1)S(1)}, u32[]{:S(2)}, u32[]{:S(2)}) collective-permute-start(bf16[112,512]{1,0:T(8,128)(2,1)S(1)} %get-tuple-element.18), channel_id=1, source_target_pairs={{0,1},{1,0},{2,3},{3,2},{4,5},{5,4},{6,7},{7,6},{8,9},{9,8},{10,11... | collective-permute-start | bytes 344072 | tf_op jit(solution)/shard_map/ppermute | solution.py:269
  13.6 1.3 %collective-permute-start.5 = (bf16[2,6,256]{2,1,0:T(8,128)(2,1)S(1)}, bf16[2,6,256]{2,1,0:T(8,128)(2,1)S(1)}, u32[]{:S(2)}, u32[]{:S(2)}) collective-permute-start(bf16[2,6,256]{2,1,0:T(8,128)(2,1)S(1)} %get-tuple-element.23), channel_id=1, source_target_pairs={{0,4},{1,5},{2,6},{3,7},{4,0},{5,1},{6,2},{7,3},{8,12},{9,13},{10,... | collective-permute-start | bytes 18440 | tf_op jit(solution)/shard_map/ppermute | solution.py:264
  15.6 14.5 %all-to-all-start = ((bf16[16,24,256]{2,1,0:T(8,128)(2,1)}), bf16[16,24,256]{2,1,0:T(8,128)(2,1)S(1)}, u32[]{:S(2)}, u32[]{:S(2)}) async-start(bf16[16,24,256]{2,1,0:T(8,128)(2,1)} %broadcast_in_dim.8), calls=%async_computation | async-start | bytes 393216 | tf_op jit(solution)/shard_map/all_to_all | solution.py:267
  23.1 1.4 %copy-start.1 = (bf16[16,256,128]{2,1,0:T(8,128)(2,1)S(1)}, bf16[16,256,128]{2,1,0:T(8,128)(2,1)}, u32[]{:S(2)}) copy-start(bf16[16,256,128]{2,1,0:T(8,128)(2,1)} %basis_ref.3) | copy-start | bytes 3145732
  23.3 1.3 %collective-permute-start.3 = (s32[48,56]{1,0:T(8,128)S(1)}, s32[48,56]{1,0:T(8,128)S(1)}, u32[]{:S(2)}, u32[]{:S(2)}) collective-permute-start(s32[48,56]{1,0:T(8,128)S(1)} %add.26), channel_id=1, source_target_pairs={{0,4},{1,5},{2,6},{3,7},{4,0},{5,1},{6,2},{7,3},{8,12},{9,13},{10,... | collective-permute-start | bytes 32264 | tf_op jit(solution)/shard_map/ppermute | solution.py:277
  23.4 6.7 %collective-permute-start.6 = (bf16[4,96,256]{2,1,0:T(8,128)(2,1)S(1)}, bf16[4,96,256]{2,1,0:T(8,128)(2,1)S(1)}, u32[]{:S(2)}, u32[]{:S(2)}) collective-permute-start(bf16[4,96,256]{2,1,0:T(8,128)(2,1)S(1)} %constant_dynamic-slice_fusion.2), channel_id=1, source_target_pairs={{0,4},{1,5},{2,6},{3,7},{4,0},{5,1},{6,2},{7,3},{8,12},{9,13},{10,... | collective-permute-start | bytes 589832 | tf_op jit(solution)/shard_map/ppermute | solution.py:276
  32.0 1.5 %collective-permute-start.7 = (bf16[96,768]{1,0:T(8,128)(2,1)S(1)}, bf16[96,768]{1,0:T(8,128)(2,1)S(1)}, u32[]{:S(2)}, u32[]{:S(2)}) collective-permute-start(bf16[96,768]{1,0:T(8,128)(2,1)S(1)} %shard_map.76.rounded_ref), channel_id=1, source_target_pairs={{0,4},{1,5},{2,6},{3,7},{4,0},{5,1},{6,2},{7,3},{8,12},{9,13},{10,... | collective-permute-start | bytes 442376 | tf_op jit(solution)/shard_map/ppermute | solution.py:305

commit v7 on v6

--- a/solution.py
+++ b/solution.py
@@ -165,31 +165,30 @@
     return total[: CHANNELS * HALF] + total[CHANNELS * HALF :]
 
 
-def own_kernel(rounded_ref, chosen_ref, bank_ref, total_ref, parts_ref):
-    total_ref[...] = back_project(rounded_ref[...], chosen_ref, bank_ref, parts_ref)
-
-
-def other_kernel(rounded_ref, chosen_ref, bank_ref, total_ref, grad_ref, parts_ref, rows_ref):
+def encode(pair):
+    largest = jnp.max(jnp.abs(pair), axis=1, keepdims=True)
+    power = jnp.ceil(jnp.log2(jnp.maximum(largest, 1e-30)) - 14.9)
+    return jnp.floor(pair * jnp.exp2(-power) + 0.5), jnp.broadcast_to(power, (pair.shape[0], 128))
+
+
+def own_kernel(rounded_ref, chosen_ref, bank_ref, total_ref, power_ref, parts_ref):
+    total = back_project(rounded_ref[...], chosen_ref, bank_ref, parts_ref)
+    total_ref[...], power_ref[...] = encode(total)
+
+
+def other_kernel(rounded_ref, chosen_ref, bank_ref, total_ref, power_ref, grad_ref, parts_ref, rows_ref):
     rounded = jnp.concatenate([rounded_ref[PAIRS:], rounded_ref[:PAIRS]], axis=0)
-    other = back_project(rounded, chosen_ref, bank_ref, parts_ref)
-    own = total_ref[...]
-    view = lax.axis_index("view")
-    halves = jnp.where(view & 1 == 0, own, other), jnp.where(view & 1 == 0, other, own)
+    other, other_power = encode(back_project(rounded, chosen_ref, bank_ref, parts_ref))
     lanes = lax.broadcasted_iota(jnp.int32, (SPOTS, 128), 1)
     powers = jnp.zeros((SPOTS, 128), F32)
-    for core in range(2):
+    for half, (total, power) in enumerate(((total_ref[...], power_ref[...]), (other, other_power))):
         for c in range(CHANNELS):
-            pair = halves[core][c * HALF : (c + 1) * HALF]
-            largest = jnp.max(jnp.abs(pair), axis=1, keepdims=True)
-            power = jnp.ceil(jnp.log2(jnp.maximum(largest, 1e-30)) - 14.9)
-            pair = jnp.floor(pair * jnp.exp2(-power) + 0.5)
-            power = jnp.broadcast_to(power, (HALF, 128))
             for far in range(2):
-                row = far * BLOCK + core * CHANNELS + c
-                tile = jnp.where(view & 2 == 2 * far, pair[:SPOTS], pair[SPOTS:])
-                rows_ref[:, row, :] = tile[:, :128]
-                rows_ref[:, 2 * BLOCK + row, :] = tile[:, 128:]
-                powers = jnp.where(lanes == row, jnp.where(view & 2 == 2 * far, power[:SPOTS], power[SPOTS:]), powers)
+                place = c * HALF + far * SPOTS
+                row = far * BLOCK + half * CHANNELS + c
+                rows_ref[:, row, :] = total[place : place + SPOTS, :128]
+                rows_ref[:, 2 * BLOCK + row, :] = total[place : place + SPOTS, 128:]
+                powers = jnp.where(lanes == row, power[place : place + SPOTS], powers)
     for row in range(4 * BLOCK, ROWS):
         rows_ref[:, row, :] = powers
     grad_ref[...] = rows_ref[...].astype(jnp.int32).astype(jnp.int16)
@@ -206,8 +205,16 @@
         part = jnp.concatenate([part[: 2 * BLOCK], part[2 * BLOCK : 4 * BLOCK]], axis=1)
         total += part * jnp.exp2(power)
     total = total * scale
+    view = lax.axis_index("view")
+    tiles = []
+    for far in range(2):
+        own, other = [total[far * BLOCK + h * CHANNELS : far * BLOCK + (h + 1) * CHANNELS] for h in range(2)]
+        first = view & 1 == 0
+        tiles.append(jnp.concatenate([jnp.where(first, own, other), jnp.where(first, other, own)], axis=0))
+    near = view & 2 == 0
+    tiles = jnp.where(near, *tiles), jnp.where(near, *tiles[::-1])
     for place in range(2 * QUARTERS):
-        blocks_ref[place] = total[:BLOCK] if place < QUARTERS else total[BLOCK:]
+        blocks_ref[place] = tiles[place // QUARTERS]
 
 
 FORWARD = [
@@ -303,8 +310,13 @@
         other,
     )
     swapped = lax.ppermute(rounded, BOTH, partners(CORE))
-    total = call(
-        own_kernel, jax.ShapeDtypeStruct((CHANNELS * HALF, WIDTH), F32), BACKWARD, rounded, chosen, bank
+    total, power = call(
+        own_kernel,
+        [jax.ShapeDtypeStruct((CHANNELS * HALF, width), F32) for width in (WIDTH, 128)],
+        BACKWARD,
+        rounded,
+        chosen,
+        bank,
     )
     grads = call(
         other_kernel,
@@ -314,6 +326,7 @@
         chosen,
         bank,
         total,
+        power,
     )
 
     parts = lax.all_to_all(grads, BOTH, 0, 0, tiled=True, axis_index_groups=plane_groups)

time: 59.8 us -> 59.7 us (level)
  no operation moved by 1% of the time
where the time goes in v7:
time: 59.7 us; the launch traced here: 59.4 us
  blocking collectives  23.7 us (40%)
  starting transfers between devices  19.1 us (32%)
  waiting for transfers between devices  7.02 us (12%)
  Pallas kernels  5.75 us (10%)
  local copies, waits for them, and re-layouts  3.42 us (6%)
    all_to_all x1, blocking collectives, on_device(): lax.all_to_all(blocks, BOTH, 0, 0, tiled=True, axis_index_groups=line_gro...  12.1 us
    all_to_all x1, blocking collectives, on_device(): lax.all_to_all(grads, BOTH, 0, 0, tiled=True, axis_index_groups=plane_gro...  11.6 us
    all_to_all x1, starting transfers between devices, on_device(): lax.all_to_all(stack, BOTH, 0, 0, tiled=True, axis_index_groups=plane_gro...  7.48 us
    ppermute x1, starting transfers between devices, on_device(): theirs = lax.ppermute(mine, BOTH, partners(FAR))  6.39 us
    all_to_all x1, waiting for transfers between devices, on_device(): lax.all_to_all(stack, BOTH, 0, 0, tiled=True, axis_index_groups=plane_gro...  4.9 us
    ppermute x3, starting transfers between devices, on_device(): lax.ppermute(messages[shift], BOTH, partners(shift))  4.47 us
    pallas_call x3, Pallas kernels, call(): pl.pallas_call(kernel, out_shape=out_shape, in_specs=[vmem] * len(operand...  4.29 us
    unnamed x15, local copies, waits for them, and re-layouts  1.9 us
  transfers between devices with their start and end apart: 9, of which 4 were waited for; matrix products, arithmetic and copies ran while one was open for 1% of the time, Pallas kernels for 4%

profile of v7, /device:TPU:2, one launch (start us, length us, event | category | flops | bytes accessed | tf_op | source)
XLA Modules:
  0.0 59.4 jit_solution(12584221797132850817)
XLA Ops:
  0.0 0.7 %copy-done = bf16[1,3,16,256]{3,2,1,0:T(8,128)(2,1)S(1)} copy-done((bf16[1,3,16,256]{3,2,1,0:T(8,128)(2,1)S(1)}, bf16[1,3,16,256]{3,2,1,0:T(8,128)(2,1)}, u32[]{:S(2)}) %copy-start) | copy-done | bytes 24600
  0.8 6.4 %collective-permute-start.4 = (bf16[12,256]{1,0:T(8,128)(2,1)S(1)}, bf16[12,256]{1,0:T(8,128)(2,1)S(1)}, u32[]{:S(2)}, u32[]{:S(2)}) collective-permute-start(bf16[12,256]{1,0:T(8,128)(2,1)S(1)} %reshape.18.mine_ref), channel_id=1, source_target_pairs={{0,10},{1,11},{2,8},{3,9},{4,14},{5,15},{6,12},{7,13},{8,2},{9,3},... | collective-permute-start | bytes 18440 | tf_op jit(solution)/shard_map/ppermute | solution.py:250
  7.2 1.1 %copy-done.2 = s32[4,2,16,1536]{3,2,1,0:T(8,128)S(1)} copy-done((s32[4,2,16,1536]{3,2,1,0:T(8,128)S(1)}, s32[4,2,16,1536]{3,2,1,0:T(8,128)}, u32[]{:S(2)}) %copy-start.2) | copy-done | bytes 786456
  8.3 0.8 %shard_map.73 = (bf16[112,512]{1,0:T(8,128)(2,1)S(1)}, bf16[112,512]{1,0:T(8,128)(2,1)S(1)}, bf16[112,512]{1,0:T(8,128)(2,1)S(1)}, bf16[112,512]{1,0:T(8,128)(2,1)S(1)}) custom-call(s32[4,2,16,1536]{3,2,1,0:T(8,128)S(1)} %copy-done.2, f32[2,3]{1,0:T(2,128)S(1)} %copy-done.3, f32[2]{0:T(128)S(1)} %copy-done.4), custom_call_target="tpu_custom_call" | custom-call | tf_op jit(solution)/shard_map/pallas_call | solution.py:254
  9.1 2.0 %collective-permute-start = (bf16[112,512]{1,0:T(8,128)(2,1)S(1)}, bf16[112,512]{1,0:T(8,128)(2,1)S(1)}, u32[]{:S(2)}, u32[]{:S(2)}) collective-permute-start(bf16[112,512]{1,0:T(8,128)(2,1)S(1)} %get-tuple-element.18), channel_id=1, source_target_pairs={{0,3},{1,2},{2,1},{3,0},{4,7},{5,6},{6,5},{7,4},{8,11},{9,10},{10,... | collective-permute-start | bytes 344072 | tf_op jit(solution)/shard_map/ppermute | solution.py:276
  11.1 0.6 collective-permute-start.1
  11.7 1.9 %collective-permute-start.2 = (bf16[112,512]{1,0:T(8,128)(2,1)S(1)}, bf16[112,512]{1,0:T(8,128)(2,1)S(1)}, u32[]{:S(2)}, u32[]{:S(2)}) collective-permute-start(bf16[112,512]{1,0:T(8,128)(2,1)S(1)} %get-tuple-element.20), channel_id=1, source_target_pairs={{0,1},{1,0},{2,3},{3,2},{4,5},{5,4},{6,7},{7,6},{8,9},{9,8},{10,11... | collective-permute-start | bytes 344072 | tf_op jit(solution)/shard_map/ppermute | solution.py:276
  13.6 0.1 collective-permute-start.5
  13.8 1.1 %collective-permute-done.5 = bf16[2,6,256]{2,1,0:T(8,128)(2,1)S(1)} collective-permute-done((bf16[2,6,256]{2,1,0:T(8,128)(2,1)S(1)}, bf16[2,6,256]{2,1,0:T(8,128)(2,1)S(1)}, u32[]{:S(2)}, u32[]{:S(2)}) %collective-permute-start.5) | collective-permute-done | bytes 6176 | tf_op jit(solution)/shard_map/ppermute | solution.py:271
  14.9 0.7 %broadcast_in_dim.8 = bf16[16,24,256]{2,1,0:T(8,128)(2,1)} broadcast(bf16[24,256]{1,0:T(8,128)(2,1)S(1)} %broadcast_in_dim.7), dimensions={1,2} | broadcast | bytes 208896 | tf_op jit(solution)/shard_map/broadcast_in_dim | solution.py:273
  15.6 7.5 %all-to-all-start = ((bf16[16,24,256]{2,1,0:T(8,128)(2,1)}), bf16[16,24,256]{2,1,0:T(8,128)(2,1)S(1)}, u32[]{:S(2)}, u32[]{:S(2)}) async-start(bf16[16,24,256]{2,1,0:T(8,128)(2,1)} %broadcast_in_dim.8), calls=%async_computation | async-start | bytes 393216 | tf_op jit(solution)/shard_map/all_to_all | solution.py:274
  23.3 0.1 collective-permute-start.3
  23.4 0.5 collective-permute-start.6
  23.9 0.7 %collective-permute-done.3 = s32[48,56]{1,0:T(8,128)S(1)} collective-permute-done((s32[48,56]{1,0:T(8,128)S(1)}, s32[48,56]{1,0:T(8,128)S(1)}, u32[]{:S(2)}, u32[]{:S(2)}) %collective-permute-start.3) | collective-permute-done | bytes 10784 | tf_op jit(solution)/shard_map/ppermute | solution.py:284
  24.6 0.5 shard_map.74
  25.1 4.9 %all-to-all-done.volume_ref = bf16[16,24,256]{2,1,0:T(8,128)(2,1)S(1)} async-done(((bf16[16,24,256]{2,1,0:T(8,128)(2,1)}), bf16[16,24,256]{2,1,0:T(8,128)(2,1)S(1)}, u32[]{:S(2)}, u32[]{:S(2)}) %all-to-all-start) | async-done | bytes 196640 | tf_op jit(solution)/shard_map/all_to_all | solution.py:274
  30.0 2.0 %shard_map.76.rounded_ref = bf16[96,768]{1,0:T(8,128)(2,1)S(1)} custom-call(bf16[96,2048]{1,0:T(8,128)(2,1)S(1)} %get-tuple-element.23.picks_ref, bf16[16,24,256]{2,1,0:T(8,128)(2,1)S(1)} %all-to-all-done.volume_ref, bf16[16,256,128]{2,1,0:T(8,128)(2,1)S(1)} %copy-done.1, bf16[4,112,256]{2,1,0:T(8,128)(2,1)S(1)} %constant_dynamic-slice_fusion.mine_ref, ...), custom_call_target="tpu_custom_call" | custom-call | tf_op jit(solution)/shard_map/pallas_call | solution.py:229
  32.1 1.0 %shard_map.77 = (f32[192,256]{1,0:T(8,128)S(1)}, f32[192,128]{1,0:T(8,128)S(1)}) custom-call(bf16[96,768]{1,0:T(8,128)(2,1)S(1)} %shard_map.76.rounded_ref, f32[64,128]{1,0:T(8,128)S(1)} %get-tuple-element.27.chosen_ref, bf16[2048,256]{1,0:T(8,128)(2,1)S(1)} %get-tuple-element.28.bank_ref), custom_call_target="tpu_custom_call" | custom-call | tf_op jit(solution)/shard_map/pallas_call | solution.py:229
  33.1 0.3 collective-permute-done.7.rounded_ref
  33.5 1.3 %shard_map.78 = s16[16,56,128]{2,1,0:T(8,128)(2,1)S(1)} custom-call(bf16[96,768]{1,0:T(8,128)(2,1)S(1)} %collective-permute-done.7.rounded_ref, f32[64,128]{1,0:T(8,128)S(1)} %get-tuple-element.27.chosen_ref, bf16[2048,256]{1,0:T(8,128)(2,1)S(1)} %get-tuple-element.28.bank_ref, f32[192,256]{1,0:T(8,128)S(1)} %get-tuple-element.29.total_ref, ...), custom_call_target="tpu_custom_call" | custom-call | tf_op jit(solution)/shard_map/pallas_call | solution.py:229
  34.8 11.6 %all_to_all.15.parts_ref = s16[16,56,128]{2,1,0:T(8,128)(2,1)S(1)} all-to-all(s16[16,56,128]{2,1,0:T(8,128)(2,1)S(1)} %shard_map.78), channel_id=1, replica_groups={{0,16,32,48,64,80,96,112,128,144,160,176,192,208,224,240},{1,17,33,49,6..., dimensions={0} | all-to-all | bytes 458752 | tf_op jit(solution)/shard_map/all_to_all | solution.py:332
  46.4 0.1 shard_map.79
  46.6 12.1 %all_to_all.16 = f32[8,12,256]{2,1,0:T(8,128)S(1)} all-to-all(f32[8,12,256]{2,1,0:T(8,128)S(1)} %shard_map.79), channel_id=1, replica_groups={{0,1,2,3,8,9,10,11},{4,5,6,7,12,13,14,15},{16,17,18,19,24,25,26,27},{20..., dimensions={0} | all-to-all | bytes 196608 | tf_op jit(solution)/shard_map/all_to_all | solution.py:341
  58.7 0.7 %reshape.20 = f32[1,3,16,256]{3,2,1,0:T(8,128)} reshape(f32[3,4,2,2,256]{4,3,2,1,0:T(2,128)S(1)} %copy.21) | data formatting | bytes 98304 | tf_op jit(solution)/shard_map/reshape | solution.py:344
  (38 shorter events, 0.5 us)
Async XLA Ops:
  0.0 0.7 %copy-start = (bf16[1,3,16,256]{3,2,1,0:T(8,128)(2,1)S(1)}, bf16[1,3,16,256]{3,2,1,0:T(8,128)(2,1)}, u32[]{:S(2)}) copy-start(bf16[1,3,16,256]{3,2,1,0:T(8,128)(2,1)} %param.7) | copy-start | bytes 73732
  0.8 6.4 %copy-start.3 = (f32[2,3]{1,0:T(2,128)S(1)}, f32[2,3]{1,0:T(2,128)}, u32[]{:S(2)}) copy-start(f32[2,3]{1,0:T(2,128)} %attenuation_ref.1) | copy-start | bytes 76
  0.8 6.4 %copy-start.4 = (f32[2]{0:T(128)S(1)}, f32[2]{0:T(128)}, u32[]{:S(2)}) copy-start(f32[2]{0:T(128)} %flux_ref.1) | copy-start | bytes 28
  0.8 12.8 %collective-permute-start.4 = (bf16[12,256]{1,0:T(8,128)(2,1)S(1)}, bf16[12,256]{1,0:T(8,128)(2,1)S(1)}, u32[]{:S(2)}, u32[]{:S(2)}) collective-permute-start(bf16[12,256]{1,0:T(8,128)(2,1)S(1)} %reshape.18.mine_ref), channel_id=1, source_target_pairs={{0,10},{1,11},{2,8},{3,9},{4,14},{5,15},{6,12},{7,13},{8,2},{9,3},... | collective-permute-start | bytes 18440 | tf_op jit(solution)/shard_map/ppermute | solution.py:250
  7.2 1.1 %copy-start.2 = (s32[4,2,16,1536]{3,2,1,0:T(8,128)S(1)}, s32[4,2,16,1536]{3,2,1,0:T(8,128)}, u32[]{:S(2)}) copy-start(s32[4,2,16,1536]{3,2,1,0:T(8,128)} %counts_ref.1) | copy-start | bytes 2359300
  8.3 5.4 %copy-start.5 = (s32[4,12,56]{2,0,1:T(4,128)S(1)}, s32[4,12,56]{2,0,1:T(4,128)}, u32[]{:S(2)}) copy-start(s32[4,12,56]{2,0,1:T(4,128)} %param.9) | copy-start | bytes 32260
  8.3 5.4 %copy-start.6 = (s32[4,12,56]{2,0,1:T(4,128)S(1)}, s32[4,12,56]{2,0,1:T(4,128)}, u32[]{:S(2)}) copy-start(s32[4,12,56]{2,0,1:T(4,128)} %param.10) | copy-start | bytes 32260
  9.1 14.0 %collective-permute-start = (bf16[112,512]{1,0:T(8,128)(2,1)S(1)}, bf16[112,512]{1,0:T(8,128)(2,1)S(1)}, u32[]{:S(2)}, u32[]{:S(2)}) collective-permute-start(bf16[112,512]{1,0:T(8,128)(2,1)S(1)} %get-tuple-element.18), channel_id=1, source_target_pairs={{0,3},{1,2},{2,1},{3,0},{4,7},{5,6},{6,5},{7,4},{8,11},{9,10},{10,... | collective-permute-start | bytes 344072 | tf_op jit(solution)/shard_map/ppermute | solution.py:276
  11.1 12.0 %collective-permute-start.1 = (bf16[112,512]{1,0:T(8,128)(2,1)S(1)}, bf16[112,512]{1,0:T(8,128)(2,1)S(1)}, u32[]{:S(2)}, u32[]{:S(2)}) collective-permute-start(bf16[112,512]{1,0:T(8,128)(2,1)S(1)} %get-tuple-element.19), channel_id=1, source_target_pairs={{0,2},{1,3},{2,0},{3,1},{4,6},{5,7},{6,4},{7,5},{8,10},{9,11},{10,... | collective-permute-start | bytes 344072 | tf_op jit(solution)/shard_map/ppermute | solution.py:276
  11.7 11.4 %collective-permute-start.2 = (bf16[112,512]{1,0:T(8,128)(2,1)S(1)}, bf16[112,512]{1,0:T(8,128)(2,1)S(1)}, u32[]{:S(2)}, u32[]{:S(2)}) collective-permute-start(bf16[112,512]{1,0:T(8,128)(2,1)S(1)} %get-tuple-element.20), channel_id=1, source_target_pairs={{0,1},{1,0},{2,3},{3,2},{4,5},{5,4},{6,7},{7,6},{8,9},{9,8},{10,11... | collective-permute-start | bytes 344072 | tf_op jit(solution)/shard_map/ppermute | solution.py:276
  13.6 1.3 %collective-permute-start.5 = (bf16[2,6,256]{2,1,0:T(8,128)(2,1)S(1)}, bf16[2,6,256]{2,1,0:T(8,128)(2,1)S(1)}, u32[]{:S(2)}, u32[]{:S(2)}) collective-permute-start(bf16[2,6,256]{2,1,0:T(8,128)(2,1)S(1)} %get-tuple-element.25), channel_id=1, source_target_pairs={{0,4},{1,5},{2,6},{3,7},{4,0},{5,1},{6,2},{7,3},{8,12},{9,13},{10,... | collective-permute-start | bytes 18440 | tf_op jit(solution)/shard_map/ppermute | solution.py:271
  15.6 14.5 %all-to-all-start = ((bf16[16,24,256]{2,1,0:T(8,128)(2,1)}), bf16[16,24,256]{2,1,0:T(8,128)(2,1)S(1)}, u32[]{:S(2)}, u32[]{:S(2)}) async-start(bf16[16,24,256]{2,1,0:T(8,128)(2,1)} %broadcast_in_dim.8), calls=%async_computation | async-start | bytes 393216 | tf_op jit(solution)/shard_map/all_to_all | solution.py:274
  23.1 1.4 %copy-start.1 = (bf16[16,256,128]{2,1,0:T(8,128)(2,1)S(1)}, bf16[16,256,128]{2,1,0:T(8,128)(2,1)}, u32[]{:S(2)}) copy-start(bf16[16,256,128]{2,1,0:T(8,128)(2,1)} %basis_ref.3) | copy-start | bytes 3145732
  23.3 1.3 %collective-permute-start.3 = (s32[48,56]{1,0:T(8,128)S(1)}, s32[48,56]{1,0:T(8,128)S(1)}, u32[]{:S(2)}, u32[]{:S(2)}) collective-permute-start(s32[48,56]{1,0:T(8,128)S(1)} %add.26), channel_id=1, source_target_pairs={{0,4},{1,5},{2,6},{3,7},{4,0},{5,1},{6,2},{7,3},{8,12},{9,13},{10,... | collective-permute-start | bytes 32264 | tf_op jit(solution)/shard_map/ppermute | solution.py:284
  23.4 6.7 %collective-permute-start.6 = (bf16[4,96,256]{2,1,0:T(8,128)(2,1)S(1)}, bf16[4,96,256]{2,1,0:T(8,128)(2,1)S(1)}, u32[]{:S(2)}, u32[]{:S(2)}) collective-permute-start(bf16[4,96,256]{2,1,0:T(8,128)(2,1)S(1)} %constant_dynamic-slice_fusion.2), channel_id=1, source_target_pairs={{0,4},{1,5},{2,6},{3,7},{4,0},{5,1},{6,2},{7,3},{8,12},{9,13},{10,... | collective-permute-start | bytes 589832 | tf_op jit(solution)/shard_map/ppermute | solution.py:283
  32.0 1.5 %collective-permute-start.7 = (bf16[96,768]{1,0:T(8,128)(2,1)S(1)}, bf16[96,768]{1,0:T(8,128)(2,1)S(1)}, u32[]{:S(2)}, u32[]{:S(2)}) collective-permute-start(bf16[96,768]{1,0:T(8,128)(2,1)S(1)} %shard_map.76.rounded_ref), channel_id=1, source_target_pairs={{0,4},{1,5},{2,6},{3,7},{4,0},{5,1},{6,2},{7,3},{8,12},{9,13},{10,... | collective-permute-start | bytes 442376 | tf_op jit(solution)/shard_map/ppermute | solution.py:312
